TPU v7x, 256 devices: a whole 4x4x8 slice. The times are simulated.
256 devices in a mesh: dap: 128 (over y_lo, z, x, core), dp: 2 (over y_hi).
Axes of the slice: x: 4, y: 4 (y_hi: 2, y_lo: 2; y = y_hi * 2 + y_lo), z: 8, core: 2. Of those that a mesh axis runs over, the one named last changes fastest.
Arguments:
- pair: bfloat16 [1024, 512, 128], P(('dp', 'dap')), parts along dimension 0, may hold values from -6 to 6
- valid: int32 [2], P('dp'), parts along dimension 0, may hold values from 256 to 512
- w_query: bfloat16 [2, 128, 128], replicated, as said below
- w_key: bfloat16 [2, 128, 128], replicated, as said below
- w_value: bfloat16 [2, 128, 128], replicated, may hold values from -0.5 to 0.5
- w_gate: bfloat16 [2, 128, 128], replicated, may hold values from -0.5 to 0.5
- w_bias: bfloat16 [2, 128, 4], replicated, may hold values from -0.5 to 0.5
- w_out: bfloat16 [2, 128, 128], replicated, may hold values from -0.5 to 0.5
Outputs:
- mixed: bfloat16 [1024, 512, 128], P(('dp', 'dap')), parts along dimension 0
There are 2 independent parts, one for each index of `dp`. A program takes and returns all parts, laid end to end along the dimension named above; an argument that names none is the same for every part. Nothing has to cross between parts.
Inputs may be any that keep to these rules, and one draw needn't show every extreme that they name: pair rows and columns of index 511 down to valid are padding; they are masked as keys. `w_query`: a weight matrix of 128 rows; in some draws its entries are up to some tens of times the fan-in scale and correlated with w_key, so that scores may reach a few hundred. `w_key`: a weight matrix of 128 rows scaled by its fan-in.
All inputs are finite; a program needn't handle non-finite values.
Results may differ from a plain program's by a relative error of at most 0.015.
Values may be sent and summed in bfloat16 or wider, within the bound.
No kernel may reach another device: no remote copies, remote signals or barrier semaphores. Data moves between devices by JAX's collectives and lax.ppermute only.
A program may use at most 64 MiB of HBM per device.

v0:
```python
import math

import jax
import jax.numpy as jnp
from jax import lax
from jax.sharding import PartitionSpec as P

HEAD_DIM = 32


epsilon = 1e-05
masked_value = -1000000000.0


def layer_normed(values):
    wide = values.astype(jnp.float32)
    center = jnp.mean(wide, axis=-1, keepdims=True)
    spread = jnp.mean(jnp.square(wide - center), axis=-1, keepdims=True)
    return ((wide - center) * lax.rsqrt(spread + epsilon)).astype(jnp.bfloat16)


def attend(queries, key_rows, value_rows, gate_logits, bias_term, key_mask, w_output):
    count = queries.shape[0]
    heads = bias_term.shape[0]
    query_heads = queries.reshape(count, heads, -1)
    key_heads = key_rows.reshape(key_rows.shape[0], heads, -1)
    value_heads = value_rows.reshape(value_rows.shape[0], heads, -1)
    scores = jnp.einsum("qhd,khd->hqk", query_heads, key_heads, preferred_element_type=jnp.float32)
    scores = scores + bias_term.astype(jnp.float32) + key_mask[None, None, :]
    highest = jnp.max(scores, axis=-1, keepdims=True)
    expsum = jnp.exp(scores - highest)
    probs = (expsum / jnp.sum(expsum, axis=-1, keepdims=True)).astype(jnp.bfloat16)
    mixed_heads = jnp.einsum("hqk,khd->qhd", probs, value_heads, preferred_element_type=jnp.float32)
    gated = (jax.nn.sigmoid(gate_logits) * mixed_heads.reshape(count, -1)).astype(jnp.bfloat16)
    return jnp.dot(gated, w_output, preferred_element_type=jnp.float32)


def project_all(normed, w_query, w_key, w_value, w_gate):
    scale = 1.0 / math.sqrt(HEAD_DIM)
    flat = normed.reshape(-1, normed.shape[-1])
    lead_shape = normed.shape[:-1] + (w_query.shape[1],)
    queries = (
        (jnp.dot(flat, w_query, preferred_element_type=jnp.float32) * scale)
        .astype(jnp.bfloat16)
        .reshape(lead_shape)
    )
    key_rows = (
        jnp.dot(flat, w_key, preferred_element_type=jnp.float32)
        .astype(jnp.bfloat16)
        .reshape(lead_shape)
    )
    value_rows = (
        jnp.dot(flat, w_value, preferred_element_type=jnp.float32)
        .astype(jnp.bfloat16)
        .reshape(lead_shape)
    )
    gate_logits = jnp.dot(flat, w_gate, preferred_element_type=jnp.float32).reshape(lead_shape)
    return (queries, key_rows, value_rows, gate_logits)


def shards(pair, valid, w_query, w_key, w_value, w_gate, w_bias, w_out):
    width = pair.shape[1]
    positions = lax.iota(jnp.int32, width)
    key_mask = jnp.where(positions < valid[0], 0.0, masked_value).astype(jnp.float32)
    normed = layer_normed(pair)
    queries, key_rows, value_rows, gate_logits = project_all(
        normed, w_query[0], w_key[0], w_value[0], w_gate[0]
    )
    bias_local = jnp.einsum(
        "rnc,ch->hrn", normed, w_bias[0], preferred_element_type=jnp.float32
    ).astype(jnp.bfloat16)
    bias_all = lax.all_gather(bias_local, "dap", axis=1, tiled=True)

    def whole_row(operands):
        return attend(
            operands[0], operands[1], operands[2], operands[3], bias_all, key_mask, w_out[0]
        )

    first = lax.map(whole_row, (queries, key_rows, value_rows, gate_logits))
    section_one = (pair.astype(jnp.float32) + first).astype(jnp.bfloat16)
    normed_one = layer_normed(section_one)
    columns = lax.all_to_all(normed_one, "dap", split_axis=1, concat_axis=0, tiled=True)
    col_queries, col_keys, col_values, col_gates = project_all(
        columns, w_query[1], w_key[1], w_value[1], w_gate[1]
    )
    bias_rows = jnp.einsum(
        "knc,ch->hkn", normed_one, w_bias[1], preferred_element_type=jnp.float32
    ).astype(jnp.bfloat16)
    bias_end = jnp.swapaxes(lax.all_gather(bias_rows, "dap", axis=1, tiled=True), 1, 2)
    local_cols = columns.shape[1]
    initial = jnp.zeros((columns.shape[0], local_cols, pair.shape[2]), jnp.float32)

    def column_step(column, buffer):
        query_col = lax.dynamic_index_in_dim(col_queries, column, 1, keepdims=False)
        key_col = lax.dynamic_index_in_dim(col_keys, column, 1, keepdims=False)
        value_col = lax.dynamic_index_in_dim(col_values, column, 1, keepdims=False)
        gate_col = lax.dynamic_index_in_dim(col_gates, column, 1, keepdims=False)
        result = attend(query_col, key_col, value_col, gate_col, bias_end, key_mask, w_out[1])
        return lax.dynamic_update_slice_in_dim(buffer, result[:, None, :], column, 1)

    second = lax.fori_loop(0, local_cols, column_step, initial).astype(jnp.bfloat16)
    returned = lax.all_to_all(second, "dap", split_axis=0, concat_axis=1, tiled=True)
    return (section_one.astype(jnp.float32) + returned.astype(jnp.float32)).astype(jnp.bfloat16)


def solution(mesh):
    placed = (P(("dp", "dap"), None, None), P("dp"), P(), P(), P(), P(), P(), P())
    return jax.shard_map(
        shards, mesh=mesh, in_specs=placed, out_specs=P(("dp", "dap"), None, None), check_vma=False
    )
```

profile of v0, /device:TPU:16, one launch (start us, length us, event | category | flops | bytes accessed | tf_op | source)
XLA Modules:
  0.0 593.1 jit_solution(11044560633648899242)
XLA Ops:
  7.9 1.7 fusion.42
  9.6 1.6 fusion.43
  14.2 213.6 %all-gather.3.cloned.1.call-done = bf16[4,512,512]{2,0,1:T(4,128)(2,1)} async-done(((bf16[4,4,512]{2,0,1:T(4,128)(2,1)}), bf16[4,512,512]{2,0,1:T(4,128)(2,1)}) %all-gather.3.cloned.1.call-update) | async-done | bytes 2097168 | tf_op jit(solution)/shard_map/all_gather | solution.py:72
  227.8 4.3 copy.66
  232.1 38.8 %while.25 = (s32[]{:T(128)}, f32[4,512,128]{2,1,0:T(8,128)}, f32[4,512,128]{1,2,0:T(8,128)S(1)}, bf16[4,512,128]{2,1,0:T(8,128)(2,1)}, bf16[4,512,128]{2,1,0:T(8...) while((s32[]{:T(128)}, f32[4,512,128]{2,1,0:T(8,128)}, ...), condition=%wide.region_5.6_spmd.clone, body=%wide.region_2.5_spmd.clone.sunk | while | flops 229969920 | bytes 7789173 | solution.py:79
  233.0 3.2 fusion.123
  237.3 3.5 fusion.124
  242.7 3.2 fusion.123
  247.0 3.5 fusion.124
  252.4 3.2 fusion.123
  256.7 3.5 fusion.124
  262.1 3.2 fusion.123
  266.4 3.5 fusion.124
  270.9 1.6 convert_reduce_fusion
  275.8 10.3 %all-to-all-start = ((bf16[4,512,128]{2,0,1:T(4,128)(2,1)}), bf16[4,512,128]{2,0,1:T(4,128)(2,1)S(1)}, u32[]{:S(2)}, u32[]{:S(2)}) async-start(bf16[4,512,128]{2,0,1:T(4,128)(2,1)} %copy.67), calls=%async_computation | async-start | bytes 1048576 | tf_op jit(solution)/shard_map/all_to_all | solution.py:82
  286.2 19.8 %all-to-all-done = bf16[4,512,128]{2,0,1:T(4,128)(2,1)S(1)} async-done(((bf16[4,512,128]{2,0,1:T(4,128)(2,1)}), bf16[4,512,128]{2,0,1:T(4,128)(2,1)S(1)}, u32[]{:S(2)}, u32[]{:S(2)}) %all-to-all-start) | async-done | bytes 524320 | tf_op jit(solution)/shard_map/all_to_all | solution.py:82
  309.4 179.0 %all-gather.5.cloned.1.call-done = bf16[4,512,512]{2,0,1:T(4,128)(2,1)} async-done(((bf16[4,4,512]{2,0,1:T(4,128)(2,1)}), bf16[4,512,512]{2,0,1:T(4,128)(2,1)}) %all-gather.5.cloned.1.call-update) | async-done | bytes 2097168 | tf_op jit(solution)/shard_map/all_gather | solution.py:89
  488.4 3.3 copy.74
  491.7 64.2 %while.26 = (s32[]{:T(128)}, bf16[512,4,128]{2,1,0:T(4,128)(2,1)}, f32[512,4,128]{0,2,1:T(8,128)S(1)}, bf16[512,4,128]{0,2,1:T(8,128)(2,1)}, bf16[512,4,128]{0,2...) while((s32[]{:T(128)}, bf16[512,4,128]{2,1,0:T(4,128)(2,1)}, ...), condition=%wide.region_11.12_spmd.clone, body=%wide.region_8.11_spmd.clone.sunk | while | flops 229969920 | bytes 7526529 | solution.py:101
  492.4 3.2 fusion.134
  496.6 3.5 fusion.135
  500.4 7.4 %dynamic_update_slice.17 = bf16[512,4,128]{2,1,0:T(4,128)(2,1)} dynamic-update-slice(bf16[512,4,128]{2,1,0:T(4,128)(2,1)} %get-tuple-element.524, f32[512,1,128]{2,1,0:T(1,128)S(1)} %bitcast.172, s32[]{:T(128)} %constant.83.clone.1..sunk, s32[]{:T(128)} %get-tuple-element.523, s32[]{:T(128)} %constant.83.clone.1..sunk) | dynamic-update-slice | bytes 524292 | tf_op jit(solution)/shard_map/while/body/eval_jaxpr/dynamic_update_slice | solution.py:99
  508.4 3.2 fusion.134
  512.6 3.5 fusion.135
  516.4 7.4 %dynamic_update_slice.17 = bf16[512,4,128]{2,1,0:T(4,128)(2,1)} dynamic-update-slice(bf16[512,4,128]{2,1,0:T(4,128)(2,1)} %get-tuple-element.524, f32[512,1,128]{2,1,0:T(1,128)S(1)} %bitcast.172, s32[]{:T(128)} %constant.83.clone.1..sunk, s32[]{:T(128)} %get-tuple-element.523, s32[]{:T(128)} %constant.83.clone.1..sunk) | dynamic-update-slice | bytes 524292 | tf_op jit(solution)/shard_map/while/body/eval_jaxpr/dynamic_update_slice | solution.py:99
  524.5 3.2 fusion.134
  528.7 3.5 fusion.135
  532.4 7.4 %dynamic_update_slice.17 = bf16[512,4,128]{2,1,0:T(4,128)(2,1)} dynamic-update-slice(bf16[512,4,128]{2,1,0:T(4,128)(2,1)} %get-tuple-element.524, f32[512,1,128]{2,1,0:T(1,128)S(1)} %bitcast.172, s32[]{:T(128)} %constant.83.clone.1..sunk, s32[]{:T(128)} %get-tuple-element.523, s32[]{:T(128)} %constant.83.clone.1..sunk) | dynamic-update-slice | bytes 524292 | tf_op jit(solution)/shard_map/while/body/eval_jaxpr/dynamic_update_slice | solution.py:99
  540.5 3.2 fusion.134
  544.7 3.5 fusion.135
  548.5 7.4 %dynamic_update_slice.17 = bf16[512,4,128]{2,1,0:T(4,128)(2,1)} dynamic-update-slice(bf16[512,4,128]{2,1,0:T(4,128)(2,1)} %get-tuple-element.524, f32[512,1,128]{2,1,0:T(1,128)S(1)} %bitcast.172, s32[]{:T(128)} %constant.83.clone.1..sunk, s32[]{:T(128)} %get-tuple-element.523, s32[]{:T(128)} %constant.83.clone.1..sunk) | dynamic-update-slice | bytes 524292 | tf_op jit(solution)/shard_map/while/body/eval_jaxpr/dynamic_update_slice | solution.py:99
  555.9 29.3 %all_to_all.24 = bf16[512,4,128]{2,1,0:T(4,128)(2,1)S(1)} all-to-all(bf16[512,4,128]{2,1,0:T(4,128)(2,1)} %get-tuple-element.207), channel_id=1, replica_groups=mesh['dap'=128,'dp'=2] {'dap'}, dimensions={0} | all-to-all | bytes 1048576 | tf_op jit(solution)/shard_map/all_to_all | solution.py:102
  (103 shorter events, 31.2 us)
Async XLA Ops:
  6.5 4.7 copy-start.9
  6.5 5.7 copy-start.2
  6.5 6.7 %copy-start.3 = (bf16[2,128,128]{2,1,0:T(8,128)(2,1)S(1)}, bf16[2,128,128]{2,1,0:T(8,128)(2,1)}, u32[]{:S(2)}) copy-start(bf16[2,128,128]{2,1,0:T(8,128)(2,1)} %param.14) | copy-start | bytes 196612
  6.5 221.3 %all-gather.3.cloned.1.call-start = ((), (), s32[]{:S(2)}) async-start(), calls=%async_computation.2 | async-start | bytes 2113536 | tf_op jit(solution)/shard_map/all_gather | solution.py:72
  7.8 5.7 copy-start.5
  11.3 2.6 copy-start.7
  12.1 476.2 %all-gather.5.cloned.1.call-start = ((), (), s32[]{:S(2)}) async-start(), calls=%async_computation.3 | async-start | bytes 2113536 | tf_op jit(solution)/shard_map/all_gather | solution.py:89
  14.2 217.9 %copy-start.1 = (bf16[2,128,128]{2,1,0:T(8,128)(2,1)S(1)}, bf16[2,128,128]{2,1,0:T(8,128)(2,1)}, u32[]{:S(2)}) copy-start(bf16[2,128,128]{2,1,0:T(8,128)(2,1)} %param.19) | copy-start | bytes 196612
  232.1 38.8 %copy-start = (bf16[4,512,128]{2,1,0:T(8,128)(2,1)S(1)}, bf16[4,512,128]{2,1,0:T(8,128)(2,1)}, u32[]{:S(2)}) copy-start(bf16[4,512,128]{2,1,0:T(8,128)(2,1)} %param.12) | copy-start | bytes 1572868
  275.8 31.7 %copy-start.4 = (bf16[2,128,128]{2,1,0:T(8,128)(2,1)S(1)}, bf16[2,128,128]{2,1,0:T(8,128)(2,1)}, u32[]{:S(2)}) copy-start(bf16[2,128,128]{2,1,0:T(8,128)(2,1)} %param.14) | copy-start | bytes 196612
  275.8 30.1 %all-to-all-start = ((bf16[4,512,128]{2,0,1:T(4,128)(2,1)}), bf16[4,512,128]{2,0,1:T(4,128)(2,1)S(1)}, u32[]{:S(2)}, u32[]{:S(2)}) async-start(bf16[4,512,128]{2,0,1:T(4,128)(2,1)} %copy.67), calls=%async_computation | async-start | bytes 1048576 | tf_op jit(solution)/shard_map/all_to_all | solution.py:82
  306.2 2.0 copy-start.6
  307.9 1.2 copy-start.8
Sparse Core Ops, SparseCore 0:
  12.3 215.5 all-gather.2
  274.8 213.5 all-gather.4
where the time goes:
time: 597 us; the launch traced here: 593 us
  waiting for transfers between devices  412 us (69%)
  matrix products  63.1 us (11%)
  local copies, waits for them, and re-layouts  49.7 us (8%)
  blocking collectives  29.3 us (5%)
  other arithmetic  14.3 us (2%)
  between operations  13.6 us (2%)
  starting transfers between devices  10.4 us (2%)
    all_gather x1, waiting for transfers between devices, shards(): bias_all = lax.all_gather(bias_local, 'dap', axis=1, tiled=True)  214 us
    all_gather x1, waiting for transfers between devices, shards(): lax.all_gather(bias_rows, 'dap', axis=1, tiled=True)  179 us
    dynamic_update_slice x4, local copies, waits for them, and re-layouts, column_step(): lax.dynamic_update_slice_in_dim(buffer, result[:, None, :], column, 1)  29.6 us
    all_to_all x1, blocking collectives, shards(): lax.all_to_all(second, 'dap', split_axis=0, concat_axis=1, tiled=True)  29.3 us
    dot_general x8, matrix products, attend(): jnp.einsum('hqk,khd->qhd', probs, value_heads, preferred_element_type=jnp...  28.3 us
    sub x8, matrix products, attend(): expsum = jnp.exp(scores - highest)  25.5 us
    all_to_all x1, waiting for transfers between devices, shards(): lax.all_to_all(normed_one, 'dap', split_axis=1, concat_axis=0, tiled=True)  19.8 us
  transfers between devices with their start and end apart: 3, of which 3 were waited for; matrix products, arithmetic and copies ran while one was open for 1% of the time, Pallas kernels for 0%

commit v1 on v0

v1 whole, which is shorter than its diff:
```python
import functools
import math

import jax
import jax.numpy as jnp
from jax import lax
from jax.experimental import pallas as pl
from jax.experimental.pallas import tpu as pltpu
from jax.sharding import Mesh, PartitionSpec as P

HEAD_DIM = 32
EPSILON = 1e-05
MASKED = -1000000000.0
CHIPS = ("y", "z", "x")
VMEM_LIMIT = 48 * 1024 * 1024

SMEM = pl.BlockSpec(memory_space=pltpu.SMEM)


def params():
    return pltpu.CompilerParams(vmem_limit_bytes=VMEM_LIMIT)


def layer_normed(wide):
    center = jnp.mean(wide, axis=-1, keepdims=True)
    moved = wide - center
    spread = jnp.mean(jnp.square(moved), axis=-1, keepdims=True)
    return moved * lax.rsqrt(spread + EPSILON)


def head_bias(normed, wb, place, tokens):
    both = lax.dot_general(
        wb, normed, (((1,), (1,)), ((), ())), preferred_element_type=jnp.float32
    )
    first = place[0] == 0
    return (
        jnp.where(first, both[0:1], both[2:3]),
        jnp.where(first, both[1:2], both[3:4]),
    )


def masked_bias(rows, place):
    positions = lax.broadcasted_iota(jnp.int32, rows.shape, 1)
    return jnp.where(positions < place[2], rows, MASKED).astype(jnp.bfloat16)


def prepare_rows(place, sib_ref, own_ref, wb_ref, normed_ref, bias_ref, rows_ref):
    core = place[0]
    count, tokens, _ = own_ref.shape
    for half, (ref, at) in enumerate(((sib_ref, 1 - core), (own_ref, core))):
        for r in range(count):
            normed = layer_normed(ref[r].astype(jnp.float32)).astype(jnp.bfloat16)
            normed_ref[half * count + r] = normed
            one, two = head_bias(normed, wb_ref[...], place, tokens)
            rows_ref[pl.ds(at * count + r, 1), :] = one
            rows_ref[pl.ds((2 + at) * count + r, 1), :] = two
    bias_ref[...] = masked_bias(rows_ref[...], place)


def prepare_columns(place, own_ref, sib_ref, wb_ref, normed_ref, bias_ref, rows_ref, wide_ref):
    core = place[0]
    chips, count, width, channels = own_ref.shape
    tokens = chips * 2 * count
    for ref, at in ((own_ref, core), (sib_ref, 1 - core)):
        wide_ref[:, pl.ds(at, 1)] = ref[...].astype(jnp.float32)[:, None]
    flat = wide_ref.reshape(tokens, width, channels)
    for j in range(width):
        normed = flat[:, j, :].astype(jnp.bfloat16)
        normed_ref[j] = normed
        one, two = head_bias(normed, wb_ref[...], place, tokens)
        rows_ref[pl.ds(j, 1), :] = one
        rows_ref[pl.ds(width + j, 1), :] = two
    bias_ref[...] = masked_bias(rows_ref[...], place)


def load_bias(place, pieces, wide_ref):
    for step, ref in enumerate(pieces):
        spot = place[3 + step]
        rows = ref.shape[1] // 2
        wide = ref[...].astype(jnp.float32)
        wide_ref[0, :, pl.ds(spot, 1)] = wide[:, None, :rows]
        wide_ref[1, :, pl.ds(spot, 1)] = wide[:, None, rows:]


def attend(place, normed, w_ref, bias_ref, chunk):
    core = place[0]
    tokens, channels = normed.shape
    projected = jnp.dot(normed, w_ref[...], preferred_element_type=jnp.float32)
    scale = 1.0 / math.sqrt(HEAD_DIM)
    query = (projected[:, :channels] * scale).astype(jnp.bfloat16)
    key_t = projected[:, channels : 2 * channels].T.astype(jnp.bfloat16)
    value = projected[:, 2 * channels : 3 * channels].astype(jnp.bfloat16)
    gate = projected[:, 3 * channels :]
    lane_head = lax.broadcasted_iota(jnp.int32, (tokens, channels), 1) // HEAD_DIM
    queries, values = [], []
    for h in range(2):
        head = 2 * core + h
        mine = lane_head == head
        queries.append(jnp.where(mine, query, jnp.zeros_like(query)))
        ones = jnp.where(lane_head == (head + 2) % 4, 1.0, 0.0).astype(jnp.bfloat16)
        values.append(jnp.where(mine, value, ones))
    parts = []
    for at in range(0, tokens, chunk):
        total = None
        for h in range(2):
            score = jnp.dot(
                queries[h][at : at + chunk], key_t, preferred_element_type=jnp.float32
            )
            score = score + bias_ref[h, at : at + chunk, :]
            highest = jnp.max(score, axis=-1, keepdims=True)
            weight = jnp.exp(score - highest).astype(jnp.bfloat16)
            out = jnp.dot(weight, values[h], preferred_element_type=jnp.float32)
            total = out if total is None else total + out
        sums = pltpu.roll(total, channels // 2, 1)
        part = jax.nn.sigmoid(gate[at : at + chunk]) * total / sums
        parts.append(jnp.where(lane_head[at : at + chunk] // 2 == core, part, 0.0))
    return jnp.concatenate(parts, axis=0)


def attend_rows(place, normed_ref, w_ref, b0, b1, b2, b3, sib_ref, own_ref, wide_ref):
    step = pl.program_id(0)

    @pl.when(step == 0)
    def _():
        load_bias(place, (b0, b1, b2, b3), wide_ref)

    tokens = normed_ref.shape[1]
    bias = wide_ref.reshape(2, tokens, tokens)
    gated = attend(place, normed_ref[0], w_ref, bias, 128).astype(jnp.bfloat16)

    @pl.when(step < 4)
    def _():
        sib_ref[0] = gated

    @pl.when(step >= 4)
    def _():
        own_ref[0] = gated


def attend_columns(place, normed_ref, w_ref, b0, b1, b2, b3, sib_ref, own_ref, wide_ref, out_ref):
    step = pl.program_id(0)

    @pl.when(step == 0)
    def _():
        load_bias(place, (b0, b1, b2, b3), wide_ref)

    tokens = normed_ref.shape[1]
    bias = wide_ref.reshape(2, tokens, tokens)
    gated = attend(place, normed_ref[0], w_ref, bias, 128)
    chips, two, rows, width, channels = out_ref.shape
    for j in range(width):

        @pl.when(step == j)
        def _():
            out_ref.reshape(tokens, width, channels)[:, j, :] = gated

    @pl.when(step == width - 1)
    def _():
        core = place[0]
        own_ref[...] = out_ref[:, pl.ds(core, 1)][:, 0].astype(jnp.bfloat16)
        sib_ref[...] = out_ref[:, pl.ds(1 - core, 1)][:, 0].astype(jnp.bfloat16)


def finish_rows(own_ref, got_ref, pair_ref, w_ref, one_ref, normed_ref):
    gated = own_ref[0] + got_ref[0]
    branch = jnp.dot(gated, w_ref[...], preferred_element_type=jnp.float32)
    one = (pair_ref[0].astype(jnp.float32) + branch).astype(jnp.bfloat16)
    one_ref[0] = one
    normed = layer_normed(one.astype(jnp.float32))
    chips, _, width, channels = normed_ref.shape
    normed_ref[:, 0] = normed.reshape(chips, width, channels).astype(jnp.bfloat16)


def finish_columns(own_ref, got_ref, w_ref, out_ref):
    chips, rows, width, channels = own_ref.shape
    gated = own_ref[...].astype(jnp.float32) + got_ref[...].astype(jnp.float32)
    gated = gated.reshape(chips * rows * width, channels).astype(jnp.bfloat16)
    branch = jnp.dot(gated, w_ref[...], preferred_element_type=jnp.float32)
    out_ref[...] = branch.reshape(chips, rows, width, channels).astype(jnp.bfloat16)


def add_back(one_ref, back_ref, out_ref):
    chips, _, width, channels = back_ref.shape
    back = back_ref[...].astype(jnp.float32).reshape(chips * width, channels)
    out_ref[0] = (one_ref[0].astype(jnp.float32) + back).astype(jnp.bfloat16)


def swap(array):
    return lax.ppermute(array, "c", [(0, 1), (1, 0)])


def gather_bias(bias, x_chips):
    group = lax.axis_size("y") * lax.axis_size("z")
    copies = jnp.broadcast_to(bias[None], (group,) + bias.shape)
    piece = lax.all_to_all(copies, ("y", "z"), 0, 0)
    return [piece] + [
        lax.ppermute(piece, "x", [(i, i ^ s) for i in range(x_chips)]) for s in range(1, x_chips)
    ]


def full(shape):
    return pl.BlockSpec(shape, lambda *_: (0,) * len(shape))


def run_attention(columns, place, normed, weights, pieces):
    rows, tokens, channels = normed.shape
    chips = tokens // 8
    bf16 = jnp.bfloat16
    specs = [
        SMEM,
        pl.BlockSpec((1, tokens, channels), lambda s: (s, 0, 0)),
        full(weights.shape),
    ] + [full(p.shape) for p in pieces]
    scratch = [pltpu.VMEM((2, chips // 4, 4, 8, tokens), jnp.float32)]
    if columns:
        shape = (chips, 4, 8, channels)
        out_specs = [full(shape), full(shape)]
        scratch.append(pltpu.VMEM((chips, 2, 4, 8, channels), jnp.float32))
        body = attend_columns
    else:
        shape = (rows // 2, tokens, channels)
        block = (1, tokens, channels)
        out_specs = [
            pl.BlockSpec(block, lambda s: (jnp.minimum(s, 3), 0, 0)),
            pl.BlockSpec(block, lambda s: (jnp.maximum(s - 4, 0), 0, 0)),
        ]
        body = attend_rows
    return pl.pallas_call(
        body,
        grid=(rows,),
        in_specs=specs,
        out_specs=out_specs,
        out_shape=[jax.ShapeDtypeStruct(shape, bf16)] * 2,
        scratch_shapes=scratch,
        compiler_params=params(),
    )(place, normed, weights, *pieces)


def shards(pair, valid, w_query, w_key, w_value, w_gate, w_bias, w_out):
    count, tokens, channels = pair.shape
    bf16 = jnp.bfloat16
    x_chips = lax.axis_size("x")
    chips = tokens // (2 * count)
    core, x = lax.axis_index("c"), lax.axis_index("x")
    place = jnp.stack([core, x, valid[0]] + [x ^ s for s in range(x_chips)]).astype(jnp.int32)
    wb = jnp.pad(jnp.swapaxes(w_bias, 1, 2), ((0, 0), (0, 4), (0, 0)))
    weights = jnp.concatenate([w_query, w_key, w_value, w_gate], axis=2)
    piece = (chips, count, 2 * count, channels)

    normed, bias = pl.pallas_call(
        prepare_rows,
        in_specs=[SMEM] + [pl.BlockSpec(memory_space=pltpu.VMEM)] * 3,
        out_specs=[pl.BlockSpec(memory_space=pltpu.VMEM)] * 2,
        out_shape=[
            jax.ShapeDtypeStruct((2 * count, tokens, channels), bf16),
            jax.ShapeDtypeStruct((4 * count, tokens), bf16),
        ],
        scratch_shapes=[pltpu.VMEM((4 * count, tokens), jnp.float32)],
        compiler_params=params(),
    )(place, swap(pair), pair, wb[0])
    pieces = gather_bias(bias, x_chips)
    for_sib, own = run_attention(False, place, normed, weights[0], pieces)
    row = pl.BlockSpec((1, tokens, channels), lambda s: (s, 0, 0))
    one, normed_one = pl.pallas_call(
        finish_rows,
        grid=(count,),
        in_specs=[row, row, row, full((channels, channels))],
        out_specs=[row, pl.BlockSpec((chips, 1, 2 * count, channels), lambda s: (0, s, 0, 0))],
        out_shape=[
            jax.ShapeDtypeStruct((count, tokens, channels), bf16),
            jax.ShapeDtypeStruct(piece, bf16),
        ],
        compiler_params=params(),
    )(own, swap(for_sib), pair, w_out[0])

    got = lax.all_to_all(normed_one, CHIPS, 0, 0)
    normed, bias = pl.pallas_call(
        prepare_columns,
        in_specs=[SMEM] + [pl.BlockSpec(memory_space=pltpu.VMEM)] * 3,
        out_specs=[pl.BlockSpec(memory_space=pltpu.VMEM)] * 2,
        out_shape=[
            jax.ShapeDtypeStruct((2 * count, tokens, channels), bf16),
            jax.ShapeDtypeStruct((4 * count, tokens), bf16),
        ],
        scratch_shapes=[
            pltpu.VMEM((4 * count, tokens), jnp.float32),
            pltpu.VMEM((chips, 2, count, 2 * count, channels), jnp.float32),
        ],
        compiler_params=params(),
    )(place, got, swap(got), wb[1])
    pieces = gather_bias(bias, x_chips)
    for_sib, own = run_attention(True, place, normed, weights[1], pieces)
    branch = pl.pallas_call(
        finish_columns,
        in_specs=[pl.BlockSpec(memory_space=pltpu.VMEM)] * 3,
        out_specs=pl.BlockSpec(memory_space=pltpu.VMEM),
        out_shape=jax.ShapeDtypeStruct(piece, bf16),
        compiler_params=params(),
    )(own, swap(for_sib), w_out[1])
    back = lax.all_to_all(branch, CHIPS, 0, 0)
    return pl.pallas_call(
        add_back,
        grid=(count,),
        in_specs=[row, pl.BlockSpec((chips, 1, 2 * count, channels), lambda s: (0, s, 0, 0))],
        out_specs=row,
        out_shape=jax.ShapeDtypeStruct((count, tokens, channels), bf16),
        compiler_params=params(),
    )(one, back)


def solution(mesh):
    fine = Mesh(mesh.devices.reshape(2, 8, 4, 2, 2), ("y", "z", "x", "c", "dp"))
    held = P(("dp", "y", "z", "x", "c"), None, None)
    return jax.shard_map(
        shards,
        mesh=fine,
        in_specs=(held, P("dp"), P(), P(), P(), P(), P(), P()),
        out_specs=held,
        check_vma=False,
    )
```

time: 597 us -> 169 us (0.28)
  waiting for transfers between devices: 412 us -> 35 us
  matrix products: 63.1 us -> 0 us
  local copies, waits for them, and re-layouts: 49.7 us -> 4.22 us
  Pallas kernels: 0 us -> 42.8 us
  blocking collectives: 29.3 us -> 67 us
  other arithmetic: 14.3 us -> 0 us
  between operations: 13.6 us -> 0.81 us
  starting transfers between devices: 10.4 us -> 17.8 us
    all_gather x2 -> x0, waiting for transfers between devices: 393 us -> none  [the longest x1 214 us: shards(): bias_all = lax.all_gather(bias_local, 'dap', axis=1, tiled=True)]
    pallas_call x0 -> x7, Pallas kernels: none -> 42.8 us  [the longest x2 33.9 us: run_attention(): pl.pallas_call(body, grid=(rows,), in_specs=specs, out_specs=out_specs, o...]
    all_to_all x1 -> x3, blocking collectives: 29.3 us -> 67 us  [the longest x1 26.9 us: shards(): got = lax.all_to_all(normed_one, CHIPS, 0, 0)]
    dot_general x26 -> x0, matrix products: 37.6 us -> none  [the longest x8 28.3 us: attend(): jnp.einsum('hqk,khd->qhd', probs, value_heads, preferred_element_type=jnp...]
    dynamic_update_slice x4 -> x0, local copies, waits for them, and re-layouts: 29.6 us -> none  [column_step(): lax.dynamic_update_slice_in_dim(buffer, result[:, None, :], column, 1)]
    ppermute x0 -> x10, waiting for transfers between devices: none -> 26.2 us  [the longest x6 19.8 us: gather_bias(): lax.ppermute(piece, 'x', [(i, i ^ s) for i in range(x_chips)])]
    sub x8 -> x0, matrix products: 25.5 us -> none  [attend(): expsum = jnp.exp(scores - highest)]
    all_to_all x1, waiting for transfers between devices: 19.8 us -> 8.73 us  [gather_bias(): piece = lax.all_to_all(copies, ('y', 'z'), 0, 0)]
  transfers between devices with their start and end apart: 3 -> 11, of which waited for: 3 -> 10; matrix products, arithmetic and copies ran while one was open for 1% -> 0% of each run, Pallas kernels for 0% -> 0%
where the time goes in v1:
time: 169 us; the launch traced here: 168 us
  blocking collectives  67 us (40%)
  Pallas kernels  42.8 us (25%)
  waiting for transfers between devices  35 us (21%)
  starting transfers between devices  17.8 us (11%)
  local copies, waits for them, and re-layouts  4.22 us (2%)
    pallas_call x2, Pallas kernels, run_attention(): pl.pallas_call(body, grid=(rows,), in_specs=specs, out_specs=out_specs, o...  33.9 us
    all_to_all x1, blocking collectives, shards(): got = lax.all_to_all(normed_one, CHIPS, 0, 0)  26.9 us
    all_to_all x1, blocking collectives, shards(): back = lax.all_to_all(branch, CHIPS, 0, 0)  25.5 us
    ppermute x6, waiting for transfers between devices, gather_bias(): lax.ppermute(piece, 'x', [(i, i ^ s) for i in range(x_chips)])  19.8 us
    all_to_all x1, blocking collectives, gather_bias(): piece = lax.all_to_all(copies, ('y', 'z'), 0, 0)  14.6 us
    all_to_all x1, starting transfers between devices, gather_bias(): piece = lax.all_to_all(copies, ('y', 'z'), 0, 0)  9.42 us
    all_to_all x1, waiting for transfers between devices, gather_bias(): piece = lax.all_to_all(copies, ('y', 'z'), 0, 0)  8.73 us
    ppermute x6, starting transfers between devices, gather_bias(): lax.ppermute(piece, 'x', [(i, i ^ s) for i in range(x_chips)])  8.19 us
  transfers between devices with their start and end apart: 11, of which 10 were waited for; matrix products, arithmetic and copies ran while one was open for 0% of the time, Pallas kernels for 0%

profile of v1, /device:TPU:16, one launch (start us, length us, event | category | flops | bytes accessed | tf_op | source)
XLA Modules:
  0.0 167.6 jit_solution(16780436785425588492)
XLA Ops:
  0.8 0.6 copy-done.7
  1.3 0.8 collective-permute-done.sib_ref
  2.1 1.0 copy-done
  3.2 1.9 %shard_map.82 = (bf16[8,512,128]{2,1,0:T(8,128)(2,1)S(1)}, bf16[16,512]{1,0:T(8,128)(2,1)S(1)}) custom-call(s32[7]{0:T(128)S(1)} %stack.24.place, bf16[4,512,128]{2,1,0:T(8,128)(2,1)S(1)} %collective-permute-done.sib_ref, bf16[4,512,128]{2,1,0:T(8,128)(2,1)S(1)} %copy-done, bf16[8,128]{1,0:T(8,128)(2,1)S(1)} %get-tuple-element.30.wb_ref), custom_call_target="tpu_custom_call" | custom-call | tf_op jit(solution)/shard_map/pallas_call | solution.py:250
  5.1 0.7 broadcast_in_dim.4
  5.8 9.4 %all-to-all-start = ((bf16[16,16,512]{2,1,0:T(8,128)(2,1)}), bf16[16,16,512]{2,1,0:T(8,128)(2,1)S(1)}, u32[]{:S(2)}, u32[]{:S(2)}) async-start(bf16[16,16,512]{2,1,0:T(8,128)(2,1)} %broadcast_in_dim.4), calls=%async_computation | async-start | bytes 524288 | tf_op jit(solution)/shard_map/all_to_all | solution.py:195
  15.3 0.8 copy-done.3
  16.1 0.8 copy-done.4
  16.9 8.7 %all-to-all-done.b0 = bf16[16,16,512]{2,1,0:T(8,128)(2,1)S(1)} async-done(((bf16[16,16,512]{2,1,0:T(8,128)(2,1)}), bf16[16,16,512]{2,1,0:T(8,128)(2,1)S(1)}, u32[]{:S(2)}, u32[]{:S(2)}) %all-to-all-start) | async-done | bytes 262176 | tf_op jit(solution)/shard_map/all_to_all | solution.py:195
  25.7 2.8 %collective-permute-start.3 = (bf16[16,16,512]{2,1,0:T(8,128)(2,1)S(1)}, bf16[16,16,512]{2,1,0:T(8,128)(2,1)S(1)}, u32[]{:S(2)}, u32[]{:S(2)}) collective-permute-start(bf16[16,16,512]{2,1,0:T(8,128)(2,1)S(1)} %all-to-all-done.b0), channel_id=1, source_target_pairs={{0,12},{4,8},{8,4},{12,0},{1,13},{5,9},{9,5},{13,1},{2,14},{6,10},... | collective-permute-start | bytes 786440 | tf_op jit(solution)/shard_map/ppermute | solution.py:197
  28.4 0.8 collective-permute-start.2
  29.2 0.5 collective-permute-start.1
  29.8 9.1 %collective-permute-done.3.b3 = bf16[16,16,512]{2,1,0:T(8,128)(2,1)S(1)} collective-permute-done((bf16[16,16,512]{2,1,0:T(8,128)(2,1)S(1)}, bf16[16,16,512]{2,1,0:T(8,128)(2,1)S(1)}, u32[]{:S(2)}, u32[]{:S(2)}) %collective-permute-start.3) | collective-permute-done | bytes 262176 | tf_op jit(solution)/shard_map/ppermute | solution.py:197
  38.9 0.1 collective-permute-done.2.b2
  39.1 0.6 collective-permute-done.1.b1
  39.7 16.3 %shard_map.83 = (bf16[4,512,128]{2,1,0:T(8,128)(2,1)S(1)}, bf16[4,512,128]{2,1,0:T(8,128)(2,1)S(1)}) custom-call(s32[7]{0:T(128)S(1)} %stack.24.place, bf16[8,512,128]{2,1,0:T(8,128)(2,1)S(1)} %get-tuple-element.15.normed_ref, bf16[128,512]{1,0:T(8,128)(2,1)S(1)} %get-tuple-element.26.w_ref, bf16[16,16,512]{2,1,0:T(8,128)(2,1)S(1)} %all-to-all-done.b0, ...), custom_call_target="tpu_custom_call" | custom-call | tf_op jit(solution)/shard_map/pallas_call | solution.py:228
  56.1 1.9 %collective-permute-done.4.got_ref = bf16[4,512,128]{2,1,0:T(8,128)(2,1)S(1)} collective-permute-done((bf16[4,512,128]{2,1,0:T(8,128)(2,1)S(1)}, bf16[4,512,128]{2,1,0:T(8,128)(2,1)S(1)}, u32[]{:S(2)}, u32[]{:S(2)}) %collective-permute-start.4) | collective-permute-done | bytes 524320 | tf_op jit(solution)/shard_map/ppermute | solution.py:189
  58.0 1.6 shard_map.84
  59.6 26.9 %all_to_all.20.own_ref = bf16[64,4,8,128]{3,2,1,0:T(8,128)(2,1)S(1)} all-to-all(bf16[64,4,8,128]{3,2,1,0:T(8,128)(2,1)S(1)} %get-tuple-element.20), channel_id=1, replica_groups=mesh['y'=2,'z'=8,'x'=4,'c'=2,'dp'=2] {'y','z','x'}, dimensions={0} | all-to-all | bytes 1048576 | tf_op jit(solution)/shard_map/all_to_all | solution.py:276
  86.4 1.9 %collective-permute-done.5.sib_ref = bf16[64,4,8,128]{3,2,1,0:T(8,128)(2,1)S(1)} collective-permute-done((bf16[64,4,8,128]{3,2,1,0:T(8,128)(2,1)S(1)}, bf16[64,4,8,128]{3,2,1,0:T(8,128)(2,1)S(1)}, u32[]{:S(2)}, u32[]{:S(2)}) %collective-permute-start.5) | collective-permute-done | bytes 524320 | tf_op jit(solution)/shard_map/ppermute | solution.py:189
  88.3 3.6 %shard_map.85 = (bf16[8,512,128]{2,1,0:T(8,128)(2,1)S(1)}, bf16[16,512]{1,0:T(8,128)(2,1)S(1)}) custom-call(s32[7]{0:T(128)S(1)} %stack.24.place, bf16[64,4,8,128]{3,2,1,0:T(8,128)(2,1)S(1)} %all_to_all.20.own_ref, bf16[64,4,8,128]{3,2,1,0:T(8,128)(2,1)S(1)} %collective-permute-done.5.sib_ref, bf16[8,128]{1,0:T(8,128)(2,1)S(1)} %get-tuple-element.29.wb_ref), custom_call_target="tpu_custom_call" | custom-call | tf_op jit(solution)/shard_map/pallas_call | solution.py:277
  92.0 14.6 %all_to_all.21.b0 = bf16[16,16,512]{2,1,0:T(8,128)(2,1)S(1)} all-to-all(bf16[16,16,512]{2,1,0:T(8,128)(2,1)S(1)} %broadcast_in_dim.5), channel_id=1, replica_groups=mesh['y'=2,'z'=8,'x'=4,'c'=2,'dp'=2] {'y','z'}, dimensions={0} | all-to-all | bytes 524288 | tf_op jit(solution)/shard_map/all_to_all | solution.py:195
  106.6 1.6 collective-permute-start.8
  108.2 1.1 collective-permute-start.7
  109.3 1.5 collective-permute-start.6
  110.7 9.3 %collective-permute-done.8.b3 = bf16[16,16,512]{2,1,0:T(8,128)(2,1)S(1)} collective-permute-done((bf16[16,16,512]{2,1,0:T(8,128)(2,1)S(1)}, bf16[16,16,512]{2,1,0:T(8,128)(2,1)S(1)}, u32[]{:S(2)}, u32[]{:S(2)}) %collective-permute-start.8) | collective-permute-done | bytes 262176 | tf_op jit(solution)/shard_map/ppermute | solution.py:197
  120.0 0.6 collective-permute-done.6.b1
  120.6 17.6 %shard_map.86 = (bf16[64,4,8,128]{3,2,1,0:T(8,128)(2,1)S(1)}, bf16[64,4,8,128]{3,2,1,0:T(8,128)(2,1)S(1)}) custom-call(s32[7]{0:T(128)S(1)} %stack.24.place, bf16[8,512,128]{2,1,0:T(8,128)(2,1)S(1)} %get-tuple-element.21.normed_ref, bf16[128,512]{1,0:T(8,128)(2,1)S(1)} %get-tuple-element.25.w_ref, bf16[16,16,512]{2,1,0:T(8,128)(2,1)S(1)} %all_to_all.21.b0, ...), custom_call_target="tpu_custom_call" | custom-call | tf_op jit(solution)/shard_map/pallas_call | solution.py:228
  138.3 1.9 %collective-permute-done.9.got_ref = bf16[64,4,8,128]{3,2,1,0:T(8,128)(2,1)S(1)} collective-permute-done((bf16[64,4,8,128]{3,2,1,0:T(8,128)(2,1)S(1)}, bf16[64,4,8,128]{3,2,1,0:T(8,128)(2,1)S(1)}, u32[]{:S(2)}, u32[]{:S(2)}) %collective-permute-start.9) | collective-permute-done | bytes 524320 | tf_op jit(solution)/shard_map/ppermute | solution.py:189
  140.2 0.3 shard_map.87
  140.5 25.5 %all_to_all.22.back_ref = bf16[64,4,8,128]{3,2,1,0:T(8,128)(2,1)S(1)} all-to-all(bf16[64,4,8,128]{3,2,1,0:T(8,128)(2,1)S(1)} %shard_map.87), channel_id=1, replica_groups=mesh['y'=2,'z'=8,'x'=4,'c'=2,'dp'=2] {'y','z','x'}, dimensions={0} | all-to-all | bytes 1048576 | tf_op jit(solution)/shard_map/all_to_all | solution.py:300
  166.1 1.5 shard_map.88
  (26 shorter events, 0.4 us)
Async XLA Ops:
  0.0 2.1 %collective-permute-start = (bf16[4,512,128]{2,1,0:T(8,128)(2,1)}, bf16[4,512,128]{2,1,0:T(8,128)(2,1)S(1)}, u32[]{:S(2)}, u32[]{:S(2)}) collective-permute-start(bf16[4,512,128]{2,1,0:T(8,128)(2,1)} %pair_ref.1), channel_id=1, source_target_pairs={{0,2},{2,0},{1,3},{3,1},{4,6},{6,4},{5,7},{7,5},{8,10},{10,8},{9,1... | collective-permute-start | bytes 1572872 | tf_op jit(solution)/shard_map/ppermute | solution.py:189
  0.7 0.7 copy-start.7
  2.1 1.0 copy-start
  5.8 9.4 %copy-start.2 = (bf16[2,128,128]{2,1,0:T(8,128)(2,1)S(1)}, bf16[2,128,128]{2,1,0:T(8,128)(2,1)}, u32[]{:S(2)}) copy-start(bf16[2,128,128]{2,1,0:T(8,128)(2,1)} %param.10) | copy-start | bytes 196612
  5.8 19.9 %all-to-all-start = ((bf16[16,16,512]{2,1,0:T(8,128)(2,1)}), bf16[16,16,512]{2,1,0:T(8,128)(2,1)S(1)}, u32[]{:S(2)}, u32[]{:S(2)}) async-start(bf16[16,16,512]{2,1,0:T(8,128)(2,1)} %broadcast_in_dim.4), calls=%async_computation | async-start | bytes 524288 | tf_op jit(solution)/shard_map/all_to_all | solution.py:195
  15.2 0.8 copy-start.3
  16.1 0.8 copy-start.4
  16.9 12.9 %copy-start.5 = (bf16[2,128,128]{2,1,0:T(8,128)(2,1)S(1)}, bf16[2,128,128]{2,1,0:T(8,128)(2,1)}, u32[]{:S(2)}) copy-start(bf16[2,128,128]{2,1,0:T(8,128)(2,1)} %param.13) | copy-start | bytes 196612
  25.7 13.3 %collective-permute-start.3 = (bf16[16,16,512]{2,1,0:T(8,128)(2,1)S(1)}, bf16[16,16,512]{2,1,0:T(8,128)(2,1)S(1)}, u32[]{:S(2)}, u32[]{:S(2)}) collective-permute-start(bf16[16,16,512]{2,1,0:T(8,128)(2,1)S(1)} %all-to-all-done.b0), channel_id=1, source_target_pairs={{0,12},{4,8},{8,4},{12,0},{1,13},{5,9},{9,5},{13,1},{2,14},{6,10},... | collective-permute-start | bytes 786440 | tf_op jit(solution)/shard_map/ppermute | solution.py:197
  28.4 10.6 %collective-permute-start.2 = (bf16[16,16,512]{2,1,0:T(8,128)(2,1)S(1)}, bf16[16,16,512]{2,1,0:T(8,128)(2,1)S(1)}, u32[]{:S(2)}, u32[]{:S(2)}) collective-permute-start(bf16[16,16,512]{2,1,0:T(8,128)(2,1)S(1)} %all-to-all-done.b0), channel_id=1, source_target_pairs={{0,8},{4,12},{8,0},{12,4},{1,9},{5,13},{9,1},{13,5},{2,10},{6,14},... | collective-permute-start | bytes 786440 | tf_op jit(solution)/shard_map/ppermute | solution.py:197
  29.2 10.4 %collective-permute-start.1 = (bf16[16,16,512]{2,1,0:T(8,128)(2,1)S(1)}, bf16[16,16,512]{2,1,0:T(8,128)(2,1)S(1)}, u32[]{:S(2)}, u32[]{:S(2)}) collective-permute-start(bf16[16,16,512]{2,1,0:T(8,128)(2,1)S(1)} %all-to-all-done.b0), channel_id=1, source_target_pairs={{0,4},{4,0},{8,12},{12,8},{1,5},{5,1},{9,13},{13,9},{2,6},{6,2},{1... | collective-permute-start | bytes 786440 | tf_op jit(solution)/shard_map/ppermute | solution.py:197
  39.7 16.4 %copy-start.6 = (bf16[2,128,128]{2,1,0:T(8,128)(2,1)S(1)}, bf16[2,128,128]{2,1,0:T(8,128)(2,1)}, u32[]{:S(2)}) copy-start(bf16[2,128,128]{2,1,0:T(8,128)(2,1)} %param.15) | copy-start | bytes 196612
  39.7 18.3 %copy-start.1 = (bf16[4,512,128]{2,1,0:T(8,128)(2,1)S(1)}, bf16[4,512,128]{2,1,0:T(8,128)(2,1)}, u32[]{:S(2)}) copy-start(bf16[4,512,128]{2,1,0:T(8,128)(2,1)} %pair_ref.1) | copy-start | bytes 1572868
  56.0 2.0 %collective-permute-start.4 = (bf16[4,512,128]{2,1,0:T(8,128)(2,1)S(1)}, bf16[4,512,128]{2,1,0:T(8,128)(2,1)S(1)}, u32[]{:S(2)}, u32[]{:S(2)}) collective-permute-start(bf16[4,512,128]{2,1,0:T(8,128)(2,1)S(1)} %get-tuple-element.18), channel_id=1, source_target_pairs={{0,2},{2,0},{1,3},{3,1},{4,6},{6,4},{5,7},{7,5},{8,10},{10,8},{9,1... | collective-permute-start | bytes 1572872 | tf_op jit(solution)/shard_map/ppermute | solution.py:189
  86.4 1.9 %collective-permute-start.5 = (bf16[64,4,8,128]{3,2,1,0:T(8,128)(2,1)S(1)}, bf16[64,4,8,128]{3,2,1,0:T(8,128)(2,1)S(1)}, u32[]{:S(2)}, u32[]{:S(2)}) collective-permute-start(bf16[64,4,8,128]{3,2,1,0:T(8,128)(2,1)S(1)} %all_to_all.20.own_ref), channel_id=1, source_target_pairs={{0,2},{2,0},{1,3},{3,1},{4,6},{6,4},{5,7},{7,5},{8,10},{10,8},{9,1... | collective-permute-start | bytes 1572872 | tf_op jit(solution)/shard_map/ppermute | solution.py:189
  106.6 13.4 %collective-permute-start.8 = (bf16[16,16,512]{2,1,0:T(8,128)(2,1)S(1)}, bf16[16,16,512]{2,1,0:T(8,128)(2,1)S(1)}, u32[]{:S(2)}, u32[]{:S(2)}) collective-permute-start(bf16[16,16,512]{2,1,0:T(8,128)(2,1)S(1)} %all_to_all.21.b0), channel_id=1, source_target_pairs={{0,12},{4,8},{8,4},{12,0},{1,13},{5,9},{9,5},{13,1},{2,14},{6,10},... | collective-permute-start | bytes 786440 | tf_op jit(solution)/shard_map/ppermute | solution.py:197
  108.2 11.8 %collective-permute-start.7 = (bf16[16,16,512]{2,1,0:T(8,128)(2,1)S(1)}, bf16[16,16,512]{2,1,0:T(8,128)(2,1)S(1)}, u32[]{:S(2)}, u32[]{:S(2)}) collective-permute-start(bf16[16,16,512]{2,1,0:T(8,128)(2,1)S(1)} %all_to_all.21.b0), channel_id=1, source_target_pairs={{0,8},{4,12},{8,0},{12,4},{1,9},{5,13},{9,1},{13,5},{2,10},{6,14},... | collective-permute-start | bytes 786440 | tf_op jit(solution)/shard_map/ppermute | solution.py:197
  109.3 11.4 %collective-permute-start.6 = (bf16[16,16,512]{2,1,0:T(8,128)(2,1)S(1)}, bf16[16,16,512]{2,1,0:T(8,128)(2,1)S(1)}, u32[]{:S(2)}, u32[]{:S(2)}) collective-permute-start(bf16[16,16,512]{2,1,0:T(8,128)(2,1)S(1)} %all_to_all.21.b0), channel_id=1, source_target_pairs={{0,4},{4,0},{8,12},{12,8},{1,5},{5,1},{9,13},{13,9},{2,6},{6,2},{1... | collective-permute-start | bytes 786440 | tf_op jit(solution)/shard_map/ppermute | solution.py:197
  138.2 2.0 %collective-permute-start.9 = (bf16[64,4,8,128]{3,2,1,0:T(8,128)(2,1)S(1)}, bf16[64,4,8,128]{3,2,1,0:T(8,128)(2,1)S(1)}, u32[]{:S(2)}, u32[]{:S(2)}) collective-permute-start(bf16[64,4,8,128]{3,2,1,0:T(8,128)(2,1)S(1)} %get-tuple-element.24), channel_id=1, source_target_pairs={{0,2},{2,0},{1,3},{3,1},{4,6},{6,4},{5,7},{7,5},{8,10},{10,8},{9,1... | collective-permute-start | bytes 1572872 | tf_op jit(solution)/shard_map/ppermute | solution.py:189

commit v2 on v0

v2 whole, which is shorter than its diff:
```python
import functools
import math

import jax
import jax.numpy as jnp
from jax import lax
from jax.experimental import pallas as pl
from jax.experimental.pallas import tpu as pltpu
from jax.sharding import Mesh, PartitionSpec as P

HEAD_DIM = 32
EPSILON = 1e-05
MASKED = -1000000000.0
VMEM_LIMIT = 48 * 1024 * 1024

X, YZ, ROWS = 4, 16, 8
QUARTER = YZ * ROWS

SMEM = pl.BlockSpec(memory_space=pltpu.SMEM)
VMEM = pl.BlockSpec(memory_space=pltpu.VMEM)
ANY = pl.BlockSpec(memory_space=pl.ANY)

CORE, VALID, SPOT, FIRST_ROW = 0, 2, 3, 7


def params():
    return pltpu.CompilerParams(vmem_limit_bytes=VMEM_LIMIT)


def cost(flops, nbytes, exps=0):
    return pl.CostEstimate(flops=flops, bytes_accessed=nbytes, transcendentals=exps)


def inner_order(rows):
    parts = rows.reshape(YZ, X, ROWS, rows.shape[-1])
    return jnp.concatenate([parts[:, x].reshape(QUARTER, -1) for x in range(X)], axis=0)


def outer_order(rows):
    parts = rows.reshape(X, YZ, ROWS, rows.shape[-1])
    return jnp.stack([parts[x] for x in range(X)], axis=1).reshape(rows.shape)


def layer_normed(wide):
    center = jnp.mean(wide, axis=-1, keepdims=True)
    moved = wide - center
    spread = jnp.mean(jnp.square(moved), axis=-1, keepdims=True)
    return moved * lax.rsqrt(spread + EPSILON)


def bias_rows(wb, normed):
    return lax.dot_general(
        wb, normed, (((1,), (1,)), ((), ())), preferred_element_type=jnp.float32
    )


def prepare_rows(place, sib_ref, own_ref, wb_ref, normed_ref, bias_ref, rows_ref):
    core = place[CORE]
    first = core == 0
    count = own_ref.shape[0]
    for half, (ref, at) in enumerate(((sib_ref, 1 - core), (own_ref, core))):
        for r in range(count):
            wide = inner_order(ref[r].astype(jnp.float32))
            normed = layer_normed(wide).astype(jnp.bfloat16)
            normed_ref[half * count + r] = normed
            four = bias_rows(wb_ref[...], normed)
            spot = at * count + r
            rows_ref[pl.ds(spot, 1), :] = jnp.where(first, four[0:1], four[2:3])
            rows_ref[pl.ds(ROWS + spot, 1), :] = jnp.where(first, four[1:2], four[3:4])
    lane = lax.broadcasted_iota(jnp.int32, bias_ref.shape, 1)
    x, rest = lane // QUARTER, lane % QUARTER
    token = ((rest // ROWS) * X + x) * ROWS + rest % ROWS
    bias_ref[...] = jnp.where(token < place[VALID], rows_ref[...], MASKED).astype(jnp.bfloat16)


def project(core, normed, w_ref):
    tokens, channels = normed.shape
    projected = jnp.dot(normed, w_ref[...], preferred_element_type=jnp.float32)
    query = (projected[:, :channels] * (1.0 / math.sqrt(HEAD_DIM))).astype(jnp.bfloat16)
    key_t = projected[:, channels : 2 * channels].astype(jnp.bfloat16).T
    half = lax.broadcasted_iota(jnp.int32, (tokens, channels), 1) // (2 * HEAD_DIM)
    value = jnp.where(half == core, projected[:, 2 * channels : 3 * channels], 1.0)
    gate = jax.nn.sigmoid(projected[:, 3 * channels :])
    return query, key_t, value.astype(jnp.bfloat16), gate


def project_rows(place, normed_ref, w_ref, query_ref, key_ref, value_ref, gate_ref):
    for r in range(normed_ref.shape[0]):
        query, key_t, value, gate = project(place[CORE], normed_ref[r], w_ref)
        query_ref[r], key_ref[r], value_ref[r], gate_ref[r] = query, key_t, value, gate


def attend(core, units):
    count, channels = units[0][0].shape
    head = lax.broadcasted_iota(jnp.int32, (count, channels), 1) // HEAD_DIM
    mine = head // 2 == core

    def scores(unit):
        query, key_t = unit[0], unit[1]
        zero = jnp.zeros_like(query)
        both = [jnp.where(head == 2 * core + h, query, zero) for h in range(2)]
        return jnp.dot(
            jnp.concatenate(both, axis=0), key_t, preferred_element_type=jnp.float32
        )

    def finish(unit, weight):
        _, _, _, value, gate, put = unit
        out = jnp.dot(weight, value, preferred_element_type=jnp.float32)
        total = jnp.where(head % 2 == 0, out[:count], out[count:])
        sums = pltpu.roll(total, channels // 2, 1)
        put(jnp.where(mine, gate * total / sums, 0.0))

    pending = None
    following = scores(units[0])
    for i, unit in enumerate(units):
        score = following
        if i + 1 < len(units):
            following = scores(units[i + 1])
        score = score + unit[2]().reshape(score.shape)
        highest = jnp.max(score, axis=-1, keepdims=True)
        weight = jnp.exp(score - highest).astype(jnp.bfloat16)
        if pending is not None:
            finish(*pending)
        pending = (unit, weight)
    finish(*pending)


def attend_quarter(count, place, *refs):
    query_ref, key_ref, value_ref, gate_ref = refs[:4]
    pieces = refs[4 : 4 + count]
    sib_ref, own_ref, wide_ref = refs[-3:]
    for step, ref in enumerate(pieces):

        @pl.when(pl.program_id(0) == step)
        def _():
            wide = ref[...].astype(jnp.float32)
            for h in range(2):
                wide_ref[h] = wide[:, h * ROWS : (h + 1) * ROWS].reshape(wide_ref.shape[1:])

    units = []
    for r in range(ROWS):
        out_ref, at = (sib_ref, r) if r < ROWS // 2 else (own_ref, r - ROWS // 2)

        def put(value, out_ref=out_ref, at=at):
            out_ref[at] = value.astype(jnp.bfloat16)

        units.append(
            (query_ref[r], key_ref[r], lambda: wide_ref[...], value_ref[r], gate_ref[r], put)
        )
    attend(place[CORE], units)


def attend_rows(place, projected, steps, pieces, outs):
    query, key_t, value, gate = projected
    rows, tokens, channels = query.shape
    first, stride = SPOT + steps[0], (steps[-1] - steps[0]) // max(len(steps) - 1, 1)
    quarter = lambda s, place: (0, place[first + stride * s], 0)
    whole = lambda s, place: (0, 0, 0)
    half = pl.BlockSpec((rows // 2, QUARTER, channels), quarter)
    shape = jax.ShapeDtypeStruct((rows // 2, tokens, channels), jnp.bfloat16)
    operands = [place, query, key_t, value, gate] + list(pieces)
    specs = [
        pl.BlockSpec((rows, QUARTER, channels), quarter),
        pl.BlockSpec(key_t.shape, whole),
        pl.BlockSpec(value.shape, whole),
        pl.BlockSpec((rows, QUARTER, channels), quarter),
    ] + [pl.BlockSpec(p.shape, whole) for p in pieces]
    aliases = {}
    if outs is not None:
        aliases = {len(operands) + i: i for i in range(2)}
        operands += list(outs)
        specs += [ANY, ANY]
    units = len(steps) * rows * 2
    return pl.pallas_call(
        functools.partial(attend_quarter, len(steps)),
        grid_spec=pltpu.PrefetchScalarGridSpec(
            num_scalar_prefetch=1,
            grid=(len(steps),),
            in_specs=specs,
            out_specs=[half, half],
            scratch_shapes=[pltpu.VMEM((2, QUARTER, tokens), jnp.float32)],
        ),
        out_shape=[shape, shape],
        input_output_aliases=aliases,
        compiler_params=params(),
        cost_estimate=cost(
            units * 4 * QUARTER * tokens * channels, 4 << 20, units * QUARTER * tokens
        ),
    )(*operands)


def finish_rows(place, own_ref, got_ref, pair_ref, w_ref, wb_ref, one_ref, normed_ref, mine_ref, other_ref, rows_ref):
    core = place[CORE]
    first = core == 0
    chips, count, width, channels = normed_ref.shape
    for r in range(count):
        gated = own_ref[r] + got_ref[r]
        branch = jnp.dot(gated, w_ref[...], preferred_element_type=jnp.float32)
        one = (inner_order(pair_ref[r].astype(jnp.float32)) + branch).astype(jnp.bfloat16)
        one_ref[r] = one
        normed = layer_normed(one.astype(jnp.float32))
        normed_ref[:, r] = normed.reshape(chips, width, channels).astype(jnp.bfloat16)
        four = bias_rows(wb_ref[...], normed.astype(jnp.bfloat16))
        four = jnp.where(place[FIRST_ROW] + r < place[VALID], four, MASKED)
        for h in range(2):
            rows_ref[0, pl.ds(h * count + r, 1), :] = jnp.where(
                first, four[h : h + 1], four[2 + h : 3 + h]
            )
            rows_ref[1, pl.ds(h * count + r, 1), :] = jnp.where(
                first, four[2 + h : 3 + h], four[h : h + 1]
            )
    mine_ref[...] = rows_ref[0].astype(jnp.bfloat16)
    other_ref[...] = rows_ref[1].astype(jnp.bfloat16)


def attend_columns(place, own_in, sib_in, w_ref, b0, b1, b2, b3, sib_ref, own_ref, wide_ref, cols_ref, normed_ref, gated_ref):
    step = pl.program_id(0)
    core = place[CORE]
    chips, count, width, channels = own_in.shape
    tokens = chips * 2 * count

    @pl.when(step == 0)
    def _():
        for ref, at in ((own_in, core), (sib_in, 1 - core)):
            cols_ref[:, pl.ds(at, 1)] = ref[...].astype(jnp.float32)[:, None]
        flat = cols_ref.reshape(tokens, width, channels)
        for j in range(width):
            normed_ref[j] = flat[:, j, :].astype(jnp.bfloat16)
        for s, ref in enumerate((b0, b1, b2, b3)):
            at = pl.multiple_of(place[SPOT + s] * QUARTER, QUARTER)
            wide = ref[...].astype(jnp.float32)
            for h in range(2):
                keyed = wide[:, h * ROWS : (h + 1) * ROWS].reshape(QUARTER, tokens)
                wide_ref[h, :, pl.ds(at, QUARTER)] = keyed.T

    chunk = tokens // 2
    units = []
    for j in range(width // 2):
        column = step * (width // 2) + j
        query, key_t, value, gate = project(core, normed_ref[column], w_ref)
        for at in range(0, tokens, chunk):

            def put(value, column=column, at=at):
                gated_ref[pl.ds(column, 1), at : at + chunk, :] = value[None]

            def bias(at=at):
                return wide_ref[:, at : at + chunk, :]

            units.append(
                (query[at : at + chunk], key_t, bias, value, gate[at : at + chunk], put)
            )
    attend(core, units)

    @pl.when(step == 1)
    def _():
        flat = cols_ref.reshape(tokens, width, channels)
        for j in range(width):
            flat[:, j, :] = gated_ref[j]
        own_ref[...] = cols_ref[:, pl.ds(core, 1)][:, 0].astype(jnp.bfloat16)
        sib_ref[...] = cols_ref[:, pl.ds(1 - core, 1)][:, 0].astype(jnp.bfloat16)


def finish_columns(own_ref, got_ref, w_ref, out_ref):
    chips, rows, width, channels = own_ref.shape
    gated = own_ref[...].astype(jnp.float32) + got_ref[...].astype(jnp.float32)
    gated = gated.reshape(chips * rows * width, channels).astype(jnp.bfloat16)
    branch = jnp.dot(gated, w_ref[...], preferred_element_type=jnp.float32)
    out_ref[...] = branch.reshape(chips, rows, width, channels).astype(jnp.bfloat16)


def add_back(one_ref, back_ref, out_ref):
    chips, count, width, channels = back_ref.shape
    for r in range(count):
        back = back_ref[:, r].astype(jnp.float32).reshape(chips * width, channels)
        total = one_ref[r].astype(jnp.float32) + back
        out_ref[r] = outer_order(total).astype(jnp.bfloat16)


def swap(array):
    return lax.ppermute(array, "c", [(0, 1), (1, 0)])


def gather_bias(bias):
    copies = jnp.broadcast_to(bias[None], (YZ,) + bias.shape)
    piece = lax.all_to_all(copies, ("y", "z"), 0, 0)
    moved = {s: lax.ppermute(piece, "x", [(i, i ^ s) for i in range(X)]) for s in (1, 3, 2)}
    return [piece, moved[1], moved[2], moved[3]]


def struct(shape, kind=jnp.bfloat16):
    return jax.ShapeDtypeStruct(shape, kind)


def shards(pair, valid, w_query, w_key, w_value, w_gate, w_bias, w_out):
    count, tokens, channels = pair.shape
    core, x = lax.axis_index("c"), lax.axis_index("x")
    chip = lax.axis_index("y") * lax.axis_size("z") + lax.axis_index("z")
    first_row = (chip * X + x) * ROWS + core * count
    place = jnp.stack([core, x, valid[0]] + [x ^ s for s in range(X)] + [first_row])
    place = place.astype(jnp.int32)
    wb = jnp.pad(jnp.swapaxes(w_bias, 1, 2), ((0, 0), (0, 4), (0, 0)))
    weights = jnp.concatenate([w_query, w_key, w_value, w_gate], axis=2)
    chips = X * YZ
    piece = (chips, count, ROWS, channels)
    rows = (ROWS, tokens, channels)

    normed, bias = pl.pallas_call(
        prepare_rows,
        in_specs=[SMEM, VMEM, VMEM, VMEM],
        out_specs=[VMEM, VMEM],
        out_shape=[struct(rows), struct((2 * ROWS, tokens))],
        scratch_shapes=[pltpu.VMEM((2 * ROWS, tokens), jnp.float32)],
        compiler_params=params(),
        cost_estimate=cost(1 << 25, 2 << 20),
    )(place, swap(pair), pair, wb[0])
    pieces = gather_bias(bias)
    block = pl.BlockSpec((ROWS // 2, tokens, channels), lambda s: (s, 0, 0))
    block_t = pl.BlockSpec((ROWS // 2, channels, tokens), lambda s: (s, 0, 0))
    projected = pl.pallas_call(
        project_rows,
        grid=(2,),
        in_specs=[SMEM, block, pl.BlockSpec((channels, 4 * channels), lambda s: (0, 0))],
        out_specs=[block, block_t, block, block],
        out_shape=[
            struct(rows),
            struct((ROWS, channels, tokens)),
            struct(rows),
            struct(rows, jnp.float32),
        ],
        compiler_params=params(),
        cost_estimate=cost(8 * ROWS * tokens * channels * channels, 6 << 20),
    )(place, normed, weights[0])
    outs = attend_rows(place, projected, (0,), pieces[:1], None)
    outs = attend_rows(place, projected, (1, 3), [pieces[1], pieces[3]], outs)
    for_sib, own = attend_rows(place, projected, (2,), pieces[2:3], outs)
    one, normed_one, mine, other = pl.pallas_call(
        finish_rows,
        in_specs=[SMEM] + [VMEM] * 5,
        out_specs=[VMEM] * 4,
        out_shape=[
            struct((count, tokens, channels)),
            struct(piece),
            struct((2 * count, tokens)),
            struct((2 * count, tokens)),
        ],
        scratch_shapes=[pltpu.VMEM((2, 2 * count, tokens), jnp.float32)],
        compiler_params=params(),
        cost_estimate=cost(1 << 27, 3 << 20),
    )(place, own, swap(for_sib), pair, w_out[0], wb[1])

    got_bias = swap(other)
    mine, got_bias = mine.reshape(2, count, tokens), got_bias.reshape(2, count, tokens)
    low, high = jnp.where(core == 0, mine, got_bias), jnp.where(core == 0, got_bias, mine)
    bias = jnp.stack([low, high], axis=1).reshape(2 * ROWS, tokens)
    pieces = gather_bias(bias)
    got = lax.all_to_all(normed_one, ("x", "y", "z"), 0, 0)
    for_sib, own = pl.pallas_call(
        attend_columns,
        grid=(2,),
        in_specs=[SMEM]
        + [pl.BlockSpec(piece, lambda s: (0, 0, 0, 0))] * 2
        + [pl.BlockSpec((channels, 4 * channels), lambda s: (0, 0))]
        + [pl.BlockSpec((YZ, 2 * ROWS, tokens), lambda s: (0, 0, 0))] * X,
        out_specs=[pl.BlockSpec(piece, lambda s: (0, 0, 0, 0))] * 2,
        out_shape=[struct(piece)] * 2,
        scratch_shapes=[
            pltpu.VMEM((2, tokens, tokens), jnp.float32),
            pltpu.VMEM((chips, 2, count, ROWS, channels), jnp.float32),
            pltpu.VMEM(rows, jnp.bfloat16),
            pltpu.VMEM(rows, jnp.float32),
        ],
        compiler_params=params(),
        cost_estimate=cost(1 << 33, 4 << 20, 1 << 22),
    )(place, got, swap(got), weights[1], *pieces)
    branch = pl.pallas_call(
        finish_columns,
        in_specs=[VMEM] * 3,
        out_specs=VMEM,
        out_shape=struct(piece),
        compiler_params=params(),
    )(own, swap(for_sib), w_out[1])
    back = lax.all_to_all(branch, ("x", "y", "z"), 0, 0)
    return pl.pallas_call(
        add_back,
        in_specs=[VMEM, VMEM],
        out_specs=VMEM,
        out_shape=struct((count, tokens, channels)),
        compiler_params=params(),
    )(one, back)


def solution(mesh):
    fine = Mesh(mesh.devices.reshape(2, 8, 4, 2, 2), ("y", "z", "x", "c", "dp"))
    held = P(("dp", "y", "z", "x", "c"), None, None)
    return jax.shard_map(
        shards,
        mesh=fine,
        in_specs=(held, P("dp"), P(), P(), P(), P(), P(), P()),
        out_specs=held,
        check_vma=False,
    )
```

time: 597 us -> 151 us (0.25)
  waiting for transfers between devices: 412 us -> 55.2 us
  matrix products: 63.1 us -> 0 us
  local copies, waits for them, and re-layouts: 49.7 us -> 4.3 us
  Pallas kernels: 0 us -> 31.6 us
  starting transfers between devices: 10.4 us -> 30.5 us
  other arithmetic: 14.3 us -> 0.02 us
  between operations: 13.6 us -> 0.91 us
    all_gather x2 -> x0, waiting for transfers between devices: 393 us -> none  [the longest x1 214 us: shards(): bias_all = lax.all_gather(bias_local, 'dap', axis=1, tiled=True)]
    dot_general x26 -> x0, matrix products: 37.6 us -> none  [the longest x8 28.3 us: attend(): jnp.einsum('hqk,khd->qhd', probs, value_heads, preferred_element_type=jnp...]
    pallas_call x0 -> x9, Pallas kernels: none -> 31.6 us  [the longest x3 11.7 us: attend_rows(): pl.pallas_call(functools.partial(attend_quarter, len(steps)), grid_spec=p...]
    dynamic_update_slice x4 -> x0, local copies, waits for them, and re-layouts: 29.6 us -> none  [column_step(): lax.dynamic_update_slice_in_dim(buffer, result[:, None, :], column, 1)]
    sub x8 -> x0, matrix products: 25.5 us -> none  [attend(): expsum = jnp.exp(scores - highest)]
    ppermute x0 -> x11, waiting for transfers between devices: none -> 18.7 us  [the longest x6 13.2 us: gather_bias(): lax.ppermute(piece, 'x', [(i, i ^ s) for i in range(X)])]
    all_to_all x1 -> x3, waiting for transfers between devices: 19.8 us -> 36.5 us  [the longest x2 19.1 us: gather_bias(): piece = lax.all_to_all(copies, ('y', 'z'), 0, 0)]
    all_to_all x1 -> x3, starting transfers between devices: 10.3 us -> 21 us  [the longest x2 12.8 us: gather_bias(): piece = lax.all_to_all(copies, ('y', 'z'), 0, 0)]
  transfers between devices with their start and end apart: 3 -> 14, of which waited for: 3 -> 11; matrix products, arithmetic and copies ran while one was open for 1% -> 1% of each run, Pallas kernels for 0% -> 8%
where the time goes in v2:
time: 151 us; the launch traced here: 150 us
  waiting for transfers between devices  55.2 us (37%)
  Pallas kernels  31.6 us (21%)
  starting transfers between devices  30.5 us (20%)
  blocking collectives  27.9 us (18%)
  local copies, waits for them, and re-layouts  4.3 us (3%)
    all_to_all x1, blocking collectives, shards(): back = lax.all_to_all(branch, ('x', 'y', 'z'), 0, 0)  27.9 us
    all_to_all x2, waiting for transfers between devices, gather_bias(): piece = lax.all_to_all(copies, ('y', 'z'), 0, 0)  19.1 us
    all_to_all x1, waiting for transfers between devices, shards(): got = lax.all_to_all(normed_one, ('x', 'y', 'z'), 0, 0)  17.4 us
    ppermute x6, waiting for transfers between devices, gather_bias(): lax.ppermute(piece, 'x', [(i, i ^ s) for i in range(X)])  13.2 us
    all_to_all x2, starting transfers between devices, gather_bias(): piece = lax.all_to_all(copies, ('y', 'z'), 0, 0)  12.8 us
    pallas_call x3, Pallas kernels, attend_rows(): pl.pallas_call(functools.partial(attend_quarter, len(steps)), grid_spec=p...  11.7 us
    pallas_call x1, Pallas kernels, shards(): pl.pallas_call(attend_columns, grid=(2,), in_specs=[SMEM] + [pl.BlockSpec...  11.7 us
    ppermute x6, starting transfers between devices, gather_bias(): lax.ppermute(piece, 'x', [(i, i ^ s) for i in range(X)])  8.92 us
  transfers between devices with their start and end apart: 14, of which 11 were waited for; matrix products, arithmetic and copies ran while one was open for 1% of the time, Pallas kernels for 8%

profile of v2, /device:TPU:16, one launch (start us, length us, event | category | flops | bytes accessed | tf_op | source)
XLA Modules:
  0.0 150.4 jit_solution(1122083456843867267)
XLA Ops:
  0.8 0.7 fusion.1
  1.5 0.6 collective-permute-done.sib_ref
  2.1 1.0 copy-done
  3.2 1.9 %shard_map.82 = (bf16[8,512,128]{2,1,0:T(8,128)(2,1)S(1)}, bf16[16,512]{1,0:T(8,128)(2,1)S(1)}) custom-call(s32[8]{0:T(128)S(1)} %stack.33.place, bf16[4,512,128]{2,1,0:T(8,128)(2,1)S(1)} %collective-permute-done.sib_ref, bf16[4,512,128]{2,1,0:T(8,128)(2,1)S(1)} %copy-done, bf16[8,128]{1,0:T(8,128)(2,1)S(1)} %get-tuple-element.48.wb_ref), custom_call_target="tpu_custom_call" | custom-call | flops 33554432 | bytes 2097152 | tf_op jit(solution)/shard_map/pallas_call | solution.py:307
  5.1 0.7 broadcast_in_dim.6
  5.8 9.3 %all-to-all-start = ((bf16[16,16,512]{2,1,0:T(8,128)(2,1)}), bf16[16,16,512]{2,1,0:T(8,128)(2,1)S(1)}, u32[]{:S(2)}, u32[]{:S(2)}) async-start(bf16[16,16,512]{2,1,0:T(8,128)(2,1)} %broadcast_in_dim.6), calls=%async_computation | async-start | bytes 524288 | tf_op jit(solution)/shard_map/all_to_all | solution.py:285
  15.1 0.9 constant_dynamic-update-slice_fusion.3
  16.1 9.5 %all-to-all-done.refs_4_ = bf16[16,16,512]{2,1,0:T(8,128)(2,1)S(1)} async-done(((bf16[16,16,512]{2,1,0:T(8,128)(2,1)}), bf16[16,16,512]{2,1,0:T(8,128)(2,1)S(1)}, u32[]{:S(2)}, u32[]{:S(2)}) %all-to-all-start) | async-done | bytes 262176 | tf_op jit(solution)/shard_map/all_to_all | solution.py:285
  25.6 1.5 collective-permute-start.2
  27.0 2.1 %collective-permute-start.3 = (bf16[16,16,512]{2,1,0:T(8,128)(2,1)S(1)}, bf16[16,16,512]{2,1,0:T(8,128)(2,1)S(1)}, u32[]{:S(2)}, u32[]{:S(2)}) collective-permute-start(bf16[16,16,512]{2,1,0:T(8,128)(2,1)S(1)} %all-to-all-done.refs_4_), channel_id=1, source_target_pairs={{0,12},{4,8},{8,4},{12,0},{1,13},{5,9},{9,5},{13,1},{2,14},{6,10},... | collective-permute-start | bytes 786440 | tf_op jit(solution)/shard_map/ppermute | solution.py:286
  29.8 3.0 %shard_map.83 = (bf16[8,512,128]{2,1,0:T(8,128)(2,1)S(1)}, bf16[8,128,512]{2,1,0:T(8,128)(2,1)S(1)}, bf16[8,512,128]{2,1,0:T(8,128)(2,1)S(1)}, f32[8,512,128]{2,1,0:T(8,128)}) custom-call(s32[8]{0:T(128)S(1)} %stack.33.place, bf16[8,512,128]{2,1,0:T(8,128)(2,1)S(1)} %get-tuple-element.23.normed_ref, bf16[128,512]{1,0:T(8,128)(2,1)S(1)} %get-tuple-element.42.w_ref), custom_call_target="tpu_custom_call" | custom-call | flops 536870912 | bytes 6291456 | tf_op jit(solution)/shard_map/pallas_call | solution.py:319
  32.8 3.3 %shard_map.84 = (bf16[4,512,128]{2,1,0:T(8,128)(2,1)S(1)}, bf16[4,512,128]{2,1,0:T(8,128)(2,1)S(1)}) custom-call(s32[8]{0:T(128)S(1)} %stack.33.place, bf16[8,512,128]{2,1,0:T(8,128)(2,1)S(1)} %get-tuple-element.24.refs_0_, bf16[8,128,512]{2,1,0:T(8,128)(2,1)S(1)} %get-tuple-element.25.refs_1_, bf16[8,512,128]{2,1,0:T(8,128)(2,1)S(1)} %get-tuple-element.26.refs_2_, ...), custom_call_target="tpu_custom_call" | custom-call | flops 536870912 | bytes 4194304 | tf_op jit(solution)/shard_map/pallas_call | solution.py:174
  36.1 4.1 %collective-permute-done.3.refs_5_ = bf16[16,16,512]{2,1,0:T(8,128)(2,1)S(1)} collective-permute-done((bf16[16,16,512]{2,1,0:T(8,128)(2,1)S(1)}, bf16[16,16,512]{2,1,0:T(8,128)(2,1)S(1)}, u32[]{:S(2)}, u32[]{:S(2)}) %collective-permute-start.3) | collective-permute-done | bytes 262176 | tf_op jit(solution)/shard_map/ppermute | solution.py:286
  40.1 5.1 %shard_map.85 = (bf16[4,512,128]{2,1,0:T(8,128)(2,1)S(1)}, bf16[4,512,128]{2,1,0:T(8,128)(2,1)S(1)}) custom-call(s32[8]{0:T(128)S(1)} %stack.33.place, bf16[8,512,128]{2,1,0:T(8,128)(2,1)S(1)} %get-tuple-element.24.refs_0_, bf16[8,128,512]{2,1,0:T(8,128)(2,1)S(1)} %get-tuple-element.25.refs_1_, ...), custom_call_target="tpu_custom_call", output_to_operand_aliasing={{0}: (7, {}), {1}: (8, {})} | custom-call | flops 1073741824 | bytes 4194304 | tf_op jit(solution)/shard_map/pallas_call | solution.py:174
  45.3 3.3 %shard_map.86 = (bf16[4,512,128]{2,1,0:T(8,128)(2,1)S(1)}, bf16[4,512,128]{2,1,0:T(8,128)(2,1)S(1)}) custom-call(s32[8]{0:T(128)S(1)} %stack.33.place, bf16[8,512,128]{2,1,0:T(8,128)(2,1)S(1)} %get-tuple-element.24.refs_0_, bf16[8,128,512]{2,1,0:T(8,128)(2,1)S(1)} %get-tuple-element.25.refs_1_, ...), custom_call_target="tpu_custom_call", output_to_operand_aliasing={{0}: (6, {}), {1}: (7, {})} | custom-call | flops 536870912 | bytes 4194304 | tf_op jit(solution)/shard_map/pallas_call | solution.py:174
  48.7 1.9 %collective-permute-done.4.got_ref = bf16[4,512,128]{2,1,0:T(8,128)(2,1)S(1)} collective-permute-done((bf16[4,512,128]{2,1,0:T(8,128)(2,1)S(1)}, bf16[4,512,128]{2,1,0:T(8,128)(2,1)S(1)}, u32[]{:S(2)}, u32[]{:S(2)}) %collective-permute-start.4) | collective-permute-done | bytes 524320 | tf_op jit(solution)/shard_map/ppermute | solution.py:280
  50.6 2.2 %shard_map.87 = (bf16[4,512,128]{2,1,0:T(8,128)(2,1)S(1)}, bf16[64,4,8,128]{3,2,1,0:T(8,128)(2,1)}, bf16[8,512]{1,0:T(8,128)(2,1)S(1)}, bf16[8,512]{1,0:T(8,128)(2,1)S(1)}) custom-call(s32[8]{0:T(128)S(1)} %stack.33.place, bf16[4,512,128]{2,1,0:T(8,128)(2,1)S(1)} %get-tuple-element.33.own_ref, bf16[4,512,128]{2,1,0:T(8,128)(2,1)S(1)} %collective-permute-done.4.got_ref, ...), custom_call_target="tpu_custom_call" | custom-call | flops 134217728 | bytes 3145728 | tf_op jit(solution)/shard_map/pallas_call | solution.py:336
  52.8 8.2 %all-to-all-start.1 = ((bf16[64,4,8,128]{3,2,1,0:T(8,128)(2,1)}), bf16[64,4,8,128]{3,2,1,0:T(8,128)(2,1)S(1)}, u32[]{:S(2)}, u32[]{:S(2)}) async-start(bf16[64,4,8,128]{3,2,1,0:T(8,128)(2,1)} %get-tuple-element.36), calls=%async_computation.1 | async-start | bytes 1048576 | tf_op jit(solution)/shard_map/all_to_all | solution.py:356
  61.2 1.2 collective-permute-done.6
  62.5 17.4 %all-to-all-done.1.own_in = bf16[64,4,8,128]{3,2,1,0:T(8,128)(2,1)S(1)} async-done(((bf16[64,4,8,128]{3,2,1,0:T(8,128)(2,1)}), bf16[64,4,8,128]{3,2,1,0:T(8,128)(2,1)S(1)}, u32[]{:S(2)}, u32[]{:S(2)}) %all-to-all-start.1) | async-done | bytes 524320 | tf_op jit(solution)/shard_map/all_to_all | solution.py:356
  79.8 0.7 broadcast_in_dim.15
  80.6 3.5 %all-to-all-start.2 = ((bf16[16,16,512]{2,1,0:T(8,128)(2,1)}), bf16[16,16,512]{2,1,0:T(8,128)(2,1)S(1)}, u32[]{:S(2)}, u32[]{:S(2)}) async-start(bf16[16,16,512]{2,1,0:T(8,128)(2,1)} %broadcast_in_dim.15), calls=%async_computation.2 | async-start | bytes 524288 | tf_op jit(solution)/shard_map/all_to_all | solution.py:285
  84.2 9.6 %all-to-all-done.2.b0 = bf16[16,16,512]{2,1,0:T(8,128)(2,1)S(1)} async-done(((bf16[16,16,512]{2,1,0:T(8,128)(2,1)}), bf16[16,16,512]{2,1,0:T(8,128)(2,1)S(1)}, u32[]{:S(2)}, u32[]{:S(2)}) %all-to-all-start.2) | async-done | bytes 262176 | tf_op jit(solution)/shard_map/all_to_all | solution.py:285
  94.1 2.1 %collective-permute-start.8 = (bf16[16,16,512]{2,1,0:T(8,128)(2,1)S(1)}, bf16[16,16,512]{2,1,0:T(8,128)(2,1)S(1)}, u32[]{:S(2)}, u32[]{:S(2)}) collective-permute-start(bf16[16,16,512]{2,1,0:T(8,128)(2,1)S(1)} %all-to-all-done.2.b0), channel_id=1, source_target_pairs={{0,8},{4,12},{8,0},{12,4},{1,9},{5,13},{9,1},{13,5},{2,10},{6,14},... | collective-permute-start | bytes 786440 | tf_op jit(solution)/shard_map/ppermute | solution.py:286
  96.2 2.3 %collective-permute-start.9 = (bf16[16,16,512]{2,1,0:T(8,128)(2,1)S(1)}, bf16[16,16,512]{2,1,0:T(8,128)(2,1)S(1)}, u32[]{:S(2)}, u32[]{:S(2)}) collective-permute-start(bf16[16,16,512]{2,1,0:T(8,128)(2,1)S(1)} %all-to-all-done.2.b0), channel_id=1, source_target_pairs={{0,12},{4,8},{8,4},{12,0},{1,13},{5,9},{9,5},{13,1},{2,14},{6,10},... | collective-permute-start | bytes 786440 | tf_op jit(solution)/shard_map/ppermute | solution.py:286
  98.5 3.6 %collective-permute-done.7.b1 = bf16[16,16,512]{2,1,0:T(8,128)(2,1)S(1)} collective-permute-done((bf16[16,16,512]{2,1,0:T(8,128)(2,1)S(1)}, bf16[16,16,512]{2,1,0:T(8,128)(2,1)S(1)}, u32[]{:S(2)}, u32[]{:S(2)}) %collective-permute-start.7) | collective-permute-done | bytes 262176 | tf_op jit(solution)/shard_map/ppermute | solution.py:286
  102.1 3.0 %collective-permute-done.8.b2 = bf16[16,16,512]{2,1,0:T(8,128)(2,1)S(1)} collective-permute-done((bf16[16,16,512]{2,1,0:T(8,128)(2,1)S(1)}, bf16[16,16,512]{2,1,0:T(8,128)(2,1)S(1)}, u32[]{:S(2)}, u32[]{:S(2)}) %collective-permute-start.8) | collective-permute-done | bytes 262176 | tf_op jit(solution)/shard_map/ppermute | solution.py:286
  105.1 2.5 %collective-permute-done.9.b3 = bf16[16,16,512]{2,1,0:T(8,128)(2,1)S(1)} collective-permute-done((bf16[16,16,512]{2,1,0:T(8,128)(2,1)S(1)}, bf16[16,16,512]{2,1,0:T(8,128)(2,1)S(1)}, u32[]{:S(2)}, u32[]{:S(2)}) %collective-permute-start.9) | collective-permute-done | bytes 262176 | tf_op jit(solution)/shard_map/ppermute | solution.py:286
  107.6 11.7 %shard_map.88 = (bf16[64,4,8,128]{3,2,1,0:T(8,128)(2,1)S(1)}, bf16[64,4,8,128]{3,2,1,0:T(8,128)(2,1)S(1)}) custom-call(s32[8]{0:T(128)S(1)} %stack.33.place, bf16[64,4,8,128]{3,2,1,0:T(8,128)(2,1)S(1)} %all-to-all-done.1.own_in, bf16[64,4,8,128]{3,2,1,0:T(8,128)(2,1)S(1)} %collective-permute-done.5.sib_in, bf16[128,512]{1,0:T(8,128)(2,1)S(1)} %get-tuple-element.41.w_ref, ...), custom_call_target="tpu_custom_call" | custom-call | flops 8589934592 | bytes 4194304 | tf_op jit(solution)/shard_map/pallas_call | solution.py:357
  119.4 1.9 %collective-permute-done.10.got_ref = bf16[64,4,8,128]{3,2,1,0:T(8,128)(2,1)S(1)} collective-permute-done((bf16[64,4,8,128]{3,2,1,0:T(8,128)(2,1)S(1)}, bf16[64,4,8,128]{3,2,1,0:T(8,128)(2,1)S(1)}, u32[]{:S(2)}, u32[]{:S(2)}) %collective-permute-start.10) | collective-permute-done | bytes 524320 | tf_op jit(solution)/shard_map/ppermute | solution.py:280
  121.6 27.9 %all_to_all.20.back_ref = bf16[64,4,8,128]{3,2,1,0:T(8,128)(2,1)S(1)} all-to-all(bf16[64,4,8,128]{3,2,1,0:T(8,128)(2,1)S(1)} %shard_map.89), channel_id=1, replica_groups=mesh['y'=2,'z'=8,'x'=4,'c'=2,'dp'=2] {'x','y','z'}, dimensions={0} | all-to-all | bytes 1048576 | tf_op jit(solution)/shard_map/all_to_all | solution.py:382
  149.5 0.9 shard_map.90
  (34 shorter events, 2.1 us)
Async XLA Ops:
  0.0 16.0 %copy-start.2 = (bf16[2,128,128]{2,1,0:T(8,128)(2,1)S(1)}, bf16[2,128,128]{2,1,0:T(8,128)(2,1)}, u32[]{:S(2)}) copy-start(bf16[2,128,128]{2,1,0:T(8,128)(2,1)} %param.11) | copy-start | bytes 196612
  0.0 2.1 %collective-permute-start = (bf16[4,512,128]{2,1,0:T(8,128)(2,1)}, bf16[4,512,128]{2,1,0:T(8,128)(2,1)S(1)}, u32[]{:S(2)}, u32[]{:S(2)}) collective-permute-start(bf16[4,512,128]{2,1,0:T(8,128)(2,1)} %pair_ref.1), channel_id=1, source_target_pairs={{0,2},{2,0},{1,3},{3,1},{4,6},{6,4},{5,7},{7,5},{8,10},{10,8},{9,1... | collective-permute-start | bytes 1572872 | tf_op jit(solution)/shard_map/ppermute | solution.py:280
  2.1 1.0 copy-start
  3.2 12.8 %copy-start.3 = (bf16[2,128,128]{2,1,0:T(8,128)(2,1)S(1)}, bf16[2,128,128]{2,1,0:T(8,128)(2,1)}, u32[]{:S(2)}) copy-start(bf16[2,128,128]{2,1,0:T(8,128)(2,1)} %param.12) | copy-start | bytes 196612
  3.2 12.9 %copy-start.4 = (bf16[2,128,128]{2,1,0:T(8,128)(2,1)S(1)}, bf16[2,128,128]{2,1,0:T(8,128)(2,1)}, u32[]{:S(2)}) copy-start(bf16[2,128,128]{2,1,0:T(8,128)(2,1)} %param.13) | copy-start | bytes 196612
  5.8 19.7 %all-to-all-start = ((bf16[16,16,512]{2,1,0:T(8,128)(2,1)}), bf16[16,16,512]{2,1,0:T(8,128)(2,1)S(1)}, u32[]{:S(2)}, u32[]{:S(2)}) async-start(bf16[16,16,512]{2,1,0:T(8,128)(2,1)} %broadcast_in_dim.6), calls=%async_computation | async-start | bytes 524288 | tf_op jit(solution)/shard_map/all_to_all | solution.py:285
  25.6 10.5 %collective-permute-start.2 = (bf16[16,16,512]{2,1,0:T(8,128)(2,1)S(1)}, bf16[16,16,512]{2,1,0:T(8,128)(2,1)S(1)}, u32[]{:S(2)}, u32[]{:S(2)}) collective-permute-start(bf16[16,16,512]{2,1,0:T(8,128)(2,1)S(1)} %all-to-all-done.refs_4_), channel_id=1, source_target_pairs={{0,4},{4,0},{8,12},{12,8},{1,5},{5,1},{9,13},{13,9},{2,6},{6,2},{1... | collective-permute-start | bytes 786440 | tf_op jit(solution)/shard_map/ppermute | solution.py:286
  27.0 13.1 %collective-permute-start.3 = (bf16[16,16,512]{2,1,0:T(8,128)(2,1)S(1)}, bf16[16,16,512]{2,1,0:T(8,128)(2,1)S(1)}, u32[]{:S(2)}, u32[]{:S(2)}) collective-permute-start(bf16[16,16,512]{2,1,0:T(8,128)(2,1)S(1)} %all-to-all-done.refs_4_), channel_id=1, source_target_pairs={{0,12},{4,8},{8,4},{12,0},{1,13},{5,9},{9,5},{13,1},{2,14},{6,10},... | collective-permute-start | bytes 786440 | tf_op jit(solution)/shard_map/ppermute | solution.py:286
  29.1 16.1 %collective-permute-start.1 = (bf16[16,16,512]{2,1,0:T(8,128)(2,1)S(1)}, bf16[16,16,512]{2,1,0:T(8,128)(2,1)S(1)}, u32[]{:S(2)}, u32[]{:S(2)}) collective-permute-start(bf16[16,16,512]{2,1,0:T(8,128)(2,1)S(1)} %all-to-all-done.refs_4_), channel_id=1, source_target_pairs={{0,8},{4,12},{8,0},{12,4},{1,9},{5,13},{9,1},{13,5},{2,10},{6,14},... | collective-permute-start | bytes 786440 | tf_op jit(solution)/shard_map/ppermute | solution.py:286
  45.3 3.4 %copy-start.5 = (bf16[2,128,128]{2,1,0:T(8,128)(2,1)S(1)}, bf16[2,128,128]{2,1,0:T(8,128)(2,1)}, u32[]{:S(2)}) copy-start(bf16[2,128,128]{2,1,0:T(8,128)(2,1)} %param.15) | copy-start | bytes 196612
  45.3 5.3 %copy-start.1 = (bf16[4,512,128]{2,1,0:T(8,128)(2,1)S(1)}, bf16[4,512,128]{2,1,0:T(8,128)(2,1)}, u32[]{:S(2)}) copy-start(bf16[4,512,128]{2,1,0:T(8,128)(2,1)} %pair_ref.1) | copy-start | bytes 1572868
  48.6 2.0 %collective-permute-start.4 = (bf16[4,512,128]{2,1,0:T(8,128)(2,1)S(1)}, bf16[4,512,128]{2,1,0:T(8,128)(2,1)S(1)}, u32[]{:S(2)}, u32[]{:S(2)}) collective-permute-start(bf16[4,512,128]{2,1,0:T(8,128)(2,1)S(1)} %get-tuple-element.34), channel_id=1, source_target_pairs={{0,2},{2,0},{1,3},{3,1},{4,6},{6,4},{5,7},{7,5},{8,10},{10,8},{9,1... | collective-permute-start | bytes 1572872 | tf_op jit(solution)/shard_map/ppermute | solution.py:280
  52.8 27.1 %all-to-all-start.1 = ((bf16[64,4,8,128]{3,2,1,0:T(8,128)(2,1)}), bf16[64,4,8,128]{3,2,1,0:T(8,128)(2,1)S(1)}, u32[]{:S(2)}, u32[]{:S(2)}) async-start(bf16[64,4,8,128]{3,2,1,0:T(8,128)(2,1)} %get-tuple-element.36), calls=%async_computation.1 | async-start | bytes 1048576 | tf_op jit(solution)/shard_map/all_to_all | solution.py:356
  60.9 1.4 collective-permute-start.6
  80.6 13.2 %all-to-all-start.2 = ((bf16[16,16,512]{2,1,0:T(8,128)(2,1)}), bf16[16,16,512]{2,1,0:T(8,128)(2,1)S(1)}, u32[]{:S(2)}, u32[]{:S(2)}) async-start(bf16[16,16,512]{2,1,0:T(8,128)(2,1)} %broadcast_in_dim.15), calls=%async_computation.2 | async-start | bytes 524288 | tf_op jit(solution)/shard_map/all_to_all | solution.py:285
  84.1 23.5 %collective-permute-start.5 = (bf16[64,4,8,128]{3,2,1,0:T(8,128)(2,1)S(1)}, bf16[64,4,8,128]{3,2,1,0:T(8,128)(2,1)S(1)}, u32[]{:S(2)}, u32[]{:S(2)}) collective-permute-start(bf16[64,4,8,128]{3,2,1,0:T(8,128)(2,1)S(1)} %all-to-all-done.1.own_in), channel_id=1, source_target_pairs={{0,2},{2,0},{1,3},{3,1},{4,6},{6,4},{5,7},{7,5},{8,10},{10,8},{9,1... | collective-permute-start | bytes 1572872 | tf_op jit(solution)/shard_map/ppermute | solution.py:280
  93.8 8.3 %collective-permute-start.7 = (bf16[16,16,512]{2,1,0:T(8,128)(2,1)S(1)}, bf16[16,16,512]{2,1,0:T(8,128)(2,1)S(1)}, u32[]{:S(2)}, u32[]{:S(2)}) collective-permute-start(bf16[16,16,512]{2,1,0:T(8,128)(2,1)S(1)} %all-to-all-done.2.b0), channel_id=1, source_target_pairs={{0,4},{4,0},{8,12},{12,8},{1,5},{5,1},{9,13},{13,9},{2,6},{6,2},{1... | collective-permute-start | bytes 786440 | tf_op jit(solution)/shard_map/ppermute | solution.py:286
  94.1 11.0 %collective-permute-start.8 = (bf16[16,16,512]{2,1,0:T(8,128)(2,1)S(1)}, bf16[16,16,512]{2,1,0:T(8,128)(2,1)S(1)}, u32[]{:S(2)}, u32[]{:S(2)}) collective-permute-start(bf16[16,16,512]{2,1,0:T(8,128)(2,1)S(1)} %all-to-all-done.2.b0), channel_id=1, source_target_pairs={{0,8},{4,12},{8,0},{12,4},{1,9},{5,13},{9,1},{13,5},{2,10},{6,14},... | collective-permute-start | bytes 786440 | tf_op jit(solution)/shard_map/ppermute | solution.py:286
  96.2 11.4 %collective-permute-start.9 = (bf16[16,16,512]{2,1,0:T(8,128)(2,1)S(1)}, bf16[16,16,512]{2,1,0:T(8,128)(2,1)S(1)}, u32[]{:S(2)}, u32[]{:S(2)}) collective-permute-start(bf16[16,16,512]{2,1,0:T(8,128)(2,1)S(1)} %all-to-all-done.2.b0), channel_id=1, source_target_pairs={{0,12},{4,8},{8,4},{12,0},{1,13},{5,9},{9,5},{13,1},{2,14},{6,10},... | collective-permute-start | bytes 786440 | tf_op jit(solution)/shard_map/ppermute | solution.py:286
  119.3 2.0 %collective-permute-start.10 = (bf16[64,4,8,128]{3,2,1,0:T(8,128)(2,1)S(1)}, bf16[64,4,8,128]{3,2,1,0:T(8,128)(2,1)S(1)}, u32[]{:S(2)}, u32[]{:S(2)}) collective-permute-start(bf16[64,4,8,128]{3,2,1,0:T(8,128)(2,1)S(1)} %get-tuple-element.40), channel_id=1, source_target_pairs={{0,2},{2,0},{1,3},{3,1},{4,6},{6,4},{5,7},{7,5},{8,10},{10,8},{9,1... | collective-permute-start | bytes 1572872 | tf_op jit(solution)/shard_map/ppermute | solution.py:280

commit v3 on v2

v3 whole, which is shorter than its diff:
```python
import functools
import math

import jax
import jax.numpy as jnp
from jax import lax
from jax.experimental import pallas as pl
from jax.experimental.pallas import tpu as pltpu
from jax.sharding import Mesh, PartitionSpec as P

HEAD_DIM = 32
EPSILON = 1e-05
MASKED = -1000000000.0

X, YZ, ROWS = 4, 16, 8
QUARTER = YZ * ROWS

SMEM = pl.BlockSpec(memory_space=pltpu.SMEM)
VMEM = pl.BlockSpec(memory_space=pltpu.VMEM)

CORE, VALID, SPOT, FIRST_ROW = 0, 2, 3, 7


def params(mebibytes=12):
    return pltpu.CompilerParams(vmem_limit_bytes=mebibytes * 1024 * 1024)


def cost(flops, nbytes, exps=0):
    return pl.CostEstimate(flops=flops, bytes_accessed=nbytes, transcendentals=exps)


def inner_order(rows):
    parts = rows.reshape(YZ, X, ROWS, rows.shape[-1])
    return jnp.concatenate([parts[:, x].reshape(QUARTER, -1) for x in range(X)], axis=0)


def outer_order(rows):
    parts = rows.reshape(X, YZ, ROWS, rows.shape[-1])
    return jnp.stack([parts[x] for x in range(X)], axis=1).reshape(rows.shape)


def layer_normed(wide):
    center = jnp.mean(wide, axis=-1, keepdims=True)
    moved = wide - center
    spread = jnp.mean(jnp.square(moved), axis=-1, keepdims=True)
    return moved * lax.rsqrt(spread + EPSILON)


def bias_rows(wb_ref, step, normed, r, count, masked, rows_ref):
    four = lax.dot_general(
        wb_ref[step], normed, (((1,), (1,)), ((), ())), preferred_element_type=jnp.float32
    )
    four = jnp.where(masked, MASKED, four)
    for h in range(four.shape[0]):
        rows_ref[h * count + r : h * count + r + 1, :] = four[h : h + 1]


def prepare_rows(place, pair_ref, wb_ref, normed_ref, mine_ref, other_ref, rows_ref):
    count, tokens, _ = pair_ref.shape
    lane = lax.broadcasted_iota(jnp.int32, (1, tokens), 1)
    x, rest = lane // QUARTER, lane % QUARTER
    token = ((rest // ROWS) * X + x) * ROWS + rest % ROWS
    masked = token >= place[VALID]
    for r in range(count):
        wide = inner_order(pair_ref[r].astype(jnp.float32))
        normed = layer_normed(wide).astype(jnp.bfloat16)
        normed_ref[r] = normed
        bias_rows(wb_ref, 0, normed, r, count, masked, rows_ref)
    low, high = rows_ref[: 2 * count], rows_ref[2 * count :]
    first = place[CORE] == 0
    mine_ref[...] = jnp.where(first, low, high).astype(jnp.bfloat16)
    other_ref[...] = jnp.where(first, high, low).astype(jnp.bfloat16)


def project(core, normed, weights):
    tokens, channels = normed.shape
    projected = jnp.dot(normed, weights, preferred_element_type=jnp.float32)
    query = (projected[:, :channels] * (1.0 / math.sqrt(HEAD_DIM))).astype(jnp.bfloat16)
    key_t = projected[:, channels : 2 * channels].astype(jnp.bfloat16).T
    half = lax.broadcasted_iota(jnp.int32, (tokens, channels), 1) // (2 * HEAD_DIM)
    value = jnp.where(half == core, projected[:, 2 * channels : 3 * channels], 1.0)
    gate = jax.nn.sigmoid(projected[:, 3 * channels :])
    return query, key_t, value.astype(jnp.bfloat16), gate


def project_rows(place, sib_ref, own_ref, *refs):
    w_refs, (query_ref, key_ref, value_ref, gate_ref, next_ref) = refs[:4], refs[4:]
    weights = jnp.concatenate([ref[0] for ref in w_refs], axis=1)
    next_ref[...] = jnp.concatenate([ref[1] for ref in w_refs], axis=1)
    for r in range(ROWS):
        normed = sib_ref[r] if r < ROWS // 2 else own_ref[r - ROWS // 2]
        query, key_t, value, gate = project(place[CORE], normed, weights)
        query_ref[r], key_ref[r], value_ref[r], gate_ref[r] = query, key_t, value, gate


def project_columns(place, own_in, sib_in, w_ref, query_ref, key_ref, value_ref, gate_ref, cols_ref):
    core = place[CORE]
    chips, _, count, width, channels = cols_ref.shape
    for ref, at in ((own_in, core), (sib_in, 1 - core)):
        part = ref[:, : count * width, :].astype(jnp.float32)
        cols_ref[:, pl.ds(at, 1)] = part.reshape(chips, 1, count, width, channels)
    flat = cols_ref.reshape(chips * 2 * count, width, channels)
    for j in range(width):
        normed = flat[:, j, :].astype(jnp.bfloat16)
        query, key_t, value, gate = project(core, normed, w_ref[...])
        query_ref[j], key_ref[j], value_ref[j], gate_ref[j] = query, key_t, value, gate


def turn_bias(place, own_in, sib_in, out_ref, keyed_ref):
    first = place[CORE] == 0
    chips, width, _ = keyed_ref.shape[1:]
    count = width // 2
    parts = []
    for ref in (own_in, sib_in):
        rows = ref[:, count * width :, :].astype(jnp.float32)
        parts.append(jnp.where(first, rows[:, : 2 * count], rows[:, 2 * count :]))
    own, sib = parts
    low, high = jnp.where(first, own, sib), jnp.where(first, sib, own)
    for h in range(2):
        keyed_ref[h, :, :count, :] = low[:, h * count : (h + 1) * count]
        keyed_ref[h, :, count:, :] = high[:, h * count : (h + 1) * count]
        keyed = keyed_ref[h].reshape(chips * width, -1)
        out_ref[h] = keyed.T.astype(jnp.bfloat16)


def attend(core, units, count, channels):
    head = lax.broadcasted_iota(jnp.int32, (count, channels), 1) // HEAD_DIM
    mine = head // 2 == core

    def scores(unit):
        query, key_t = unit[0](), unit[1]()
        zero = jnp.zeros_like(query)
        both = [jnp.where(head == 2 * core + h, query, zero) for h in range(2)]
        return jnp.dot(
            jnp.concatenate(both, axis=0), key_t, preferred_element_type=jnp.float32
        )

    def finish(unit, weight):
        _, _, _, value, gate, put = unit
        out = jnp.dot(weight, value(), preferred_element_type=jnp.float32)
        total = jnp.where(head % 2 == 0, out[:count], out[count:])
        sums = pltpu.roll(total, channels // 2, 1)
        put(jnp.where(mine, gate() * total / sums, 0.0))

    pending = None
    following = scores(units[0])
    for i, unit in enumerate(units):
        score = following
        if i + 1 < len(units):
            following = scores(units[i + 1])
        score = score + unit[2]().reshape(score.shape)
        highest = jnp.max(score, axis=-1, keepdims=True)
        weight = jnp.exp(score - highest).astype(jnp.bfloat16)
        if pending is not None:
            finish(*pending)
        pending = (unit, weight)
    finish(*pending)


def attend_quarters(steps, columns, place, *refs):
    core = place[CORE]
    query_ref, key_ref, value_ref, gate_ref = refs[:4]
    pieces = refs[4 : 4 + len(steps)]
    sib_ref, own_ref, wide_ref = refs[-4:-1] if columns else refs[-3:]
    out_ref = refs[-1]
    units = []
    for i, (s, piece_ref) in enumerate(zip(steps, pieces)):
        wide = piece_ref[...].astype(jnp.float32)
        for h in range(2):
            rows = wide[h] if columns else wide[:, h * ROWS : (h + 1) * ROWS]
            wide_ref[i, h] = rows.reshape(wide_ref.shape[2:])
        span = pl.ds(pl.multiple_of(place[SPOT + s] * QUARTER, QUARTER), QUARTER)
        for r in range(ROWS):

            def put(value, i=i, r=r, span=span):
                if columns:
                    out_ref.reshape(len(steps), QUARTER, ROWS, -1)[i, :, r, :] = value
                elif r < ROWS // 2:
                    sib_ref[r, span, :] = value.astype(jnp.bfloat16)
                else:
                    own_ref[r - ROWS // 2, span, :] = value.astype(jnp.bfloat16)

            units.append(
                (
                    lambda r=r, span=span: query_ref[r, span, :],
                    lambda r=r: key_ref[r],
                    lambda i=i: wide_ref[i],
                    lambda r=r: value_ref[r],
                    lambda r=r, span=span: gate_ref[r, span, :],
                    put,
                )
            )
    attend(core, units, QUARTER, query_ref.shape[-1])
    if columns:
        for i, s in enumerate(steps):
            chips = pl.ds(place[SPOT + s] * YZ, YZ)
            for ref, at in ((own_ref, core), (sib_ref, 1 - core)):
                ref[chips] = out_ref[i, :, pl.ds(at, 1)][:, 0].astype(jnp.bfloat16)


def attend_some(steps, columns, place, projected, pieces, outs):
    rows, tokens, channels = projected[0].shape
    count = rows // 2
    scratch = [pltpu.VMEM((len(steps), 2, QUARTER, tokens), jnp.float32)]
    if columns:
        shape = struct((X * YZ, count, rows, channels))
        scratch.append(pltpu.VMEM((len(steps), YZ, 2, count, rows, channels), jnp.float32))
    else:
        shape = struct((count, tokens, channels))
    operands = [place, *projected, *pieces]
    aliases = {}
    if outs is not None:
        aliases = {len(operands) + i: i for i in range(2)}
        operands += list(outs)
    units = len(steps) * rows * 2
    return pl.pallas_call(
        functools.partial(attend_quarters, steps, columns),
        in_specs=[SMEM] + [VMEM] * (len(operands) - 1),
        out_specs=[VMEM, VMEM],
        scratch_shapes=scratch,
        out_shape=[shape, shape],
        input_output_aliases=aliases,
        compiler_params=params(16),
        cost_estimate=cost(
            units * 4 * QUARTER * tokens * channels, 4 << 20, units * QUARTER * tokens
        ),
    )(*operands)


def attend_all(columns, place, projected, piece):
    moved = {s: lax.ppermute(piece, "x", [(i, i ^ s) for i in range(X)]) for s in (1, 3, 2)}
    outs = attend_some((0,), columns, place, projected, [piece], None)
    outs = attend_some((1, 3), columns, place, projected, [moved[1], moved[3]], outs)
    return attend_some((2,), columns, place, projected, [moved[2]], outs)


def finish_rows(place, own_ref, got_ref, pair_ref, w_ref, wb_ref, one_ref, sent_ref, rows_ref, wide_ref):
    count, tokens, channels = own_ref.shape
    chips = sent_ref.shape[0]
    for r in range(count):
        gated = own_ref[r] + got_ref[r]
        branch = jnp.dot(gated, w_ref[0], preferred_element_type=jnp.float32)
        one = (inner_order(pair_ref[r].astype(jnp.float32)) + branch).astype(jnp.bfloat16)
        one_ref[r] = one
        normed = layer_normed(one.astype(jnp.float32))
        wide_ref[:, r * ROWS : (r + 1) * ROWS] = normed.reshape(chips, ROWS, channels)
        masked = place[FIRST_ROW] + r >= place[VALID]
        bias_rows(wb_ref, 1, normed.astype(jnp.bfloat16), r, count, masked, rows_ref)
    sent_ref[:, : count * ROWS] = wide_ref[...].astype(jnp.bfloat16)
    for x in range(X):
        quarter = rows_ref[:, x * QUARTER : (x + 1) * QUARTER].astype(jnp.bfloat16)
        sent_ref[x * YZ : (x + 1) * YZ, count * ROWS :] = jnp.broadcast_to(
            quarter[None], (YZ,) + quarter.shape
        )


def finish_columns(own_ref, got_ref, w_ref, out_ref):
    chips, rows, width, channels = own_ref.shape
    gated = own_ref[...].astype(jnp.float32) + got_ref[...].astype(jnp.float32)
    gated = gated.reshape(chips * rows * width, channels).astype(jnp.bfloat16)
    branch = jnp.dot(gated, w_ref[1], preferred_element_type=jnp.float32)
    out_ref[...] = branch.reshape(chips, rows, width, channels).astype(jnp.bfloat16)


def add_back(one_ref, back_ref, out_ref):
    chips, count, width, channels = back_ref.shape
    for r in range(count):
        back = back_ref[:, r].astype(jnp.float32).reshape(chips * width, channels)
        total = one_ref[r].astype(jnp.float32) + back
        out_ref[r] = outer_order(total).astype(jnp.bfloat16)


def swap(array):
    return lax.ppermute(array, "c", [(0, 1), (1, 0)])


def spread_bias(core, mine, other):
    got = swap(other)
    rows, tokens = mine.shape
    mine, got = (a.reshape(2, rows // 2, tokens) for a in (mine, got))
    low, high = jnp.where(core == 0, mine, got), jnp.where(core == 0, got, mine)
    bias = jnp.stack([low, high], axis=1).reshape(2 * rows, tokens)
    return lax.all_to_all(jnp.broadcast_to(bias[None], (YZ,) + bias.shape), ("y", "z"), 0, 0)


def whole(shape):
    return pl.BlockSpec(shape, lambda s: (0,) * len(shape))


def struct(shape, kind=jnp.bfloat16):
    return jax.ShapeDtypeStruct(shape, kind)


def shards(pair, valid, w_query, w_key, w_value, w_gate, w_bias, w_out):
    count, tokens, channels = pair.shape
    core, x = lax.axis_index("c"), lax.axis_index("x")
    chip = lax.axis_index("y") * lax.axis_size("z") + lax.axis_index("z")
    first_row = (chip * X + x) * ROWS + core * count
    place = jnp.stack([core, x, valid[0]] + [x ^ s for s in range(X)] + [first_row])
    place = place.astype(jnp.int32)
    wb = jnp.swapaxes(w_bias, 1, 2)
    weights = [w_query, w_key, w_value, w_gate]
    piece = (X * YZ, count, ROWS, channels)
    rows = (ROWS, tokens, channels)
    held = (count, tokens, channels)
    half = struct((ROWS, tokens))
    bias_scratch = pltpu.VMEM((4 * count, tokens), jnp.float32)
    projections = [
        struct(rows),
        struct((ROWS, channels, tokens)),
        struct(rows),
        struct(rows, jnp.float32),
    ]

    normed, mine, other = pl.pallas_call(
        prepare_rows,
        grid=(1,),
        in_specs=[SMEM, whole(pair.shape), whole(wb.shape)],
        out_specs=[VMEM] * 3,
        out_shape=[struct(held), half, half],
        scratch_shapes=[bias_scratch],
        compiler_params=params(),
        cost_estimate=cost(1 << 25, 2 << 20),
    )(place, pair, wb)
    gathered = spread_bias(core, mine, other)
    *projected, next_weights = pl.pallas_call(
        project_rows,
        in_specs=[SMEM] + [VMEM] * 6,
        out_specs=[VMEM] * 5,
        out_shape=projections + [struct((channels, 4 * channels))],
        compiler_params=params(),
        cost_estimate=cost(8 * ROWS * tokens * channels * channels, 6 << 20),
    )(place, swap(normed), normed, *weights)
    gathered, *projected = lax.optimization_barrier((gathered, *projected))
    for_sib, own = attend_all(False, place, projected, gathered)
    message = (X * YZ, count * ROWS + 4 * count, channels)
    one, sent = pl.pallas_call(
        finish_rows,
        in_specs=[SMEM] + [VMEM] * 5,
        out_specs=[VMEM] * 2,
        out_shape=[struct(held), struct(message)],
        scratch_shapes=[
            bias_scratch,
            pltpu.VMEM((X * YZ, count * ROWS, channels), jnp.float32),
        ],
        compiler_params=params(),
        cost_estimate=cost(1 << 27, 3 << 20),
    )(place, own, swap(for_sib), pair, w_out, wb)

    got = lax.all_to_all(sent, ("x", "y", "z"), 0, 0)
    got_sib = swap(got)
    quarter = pl.pallas_call(
        turn_bias,
        in_specs=[SMEM, VMEM, VMEM],
        out_specs=VMEM,
        out_shape=struct((2, QUARTER, tokens)),
        scratch_shapes=[pltpu.VMEM((2, X * YZ, ROWS, QUARTER), jnp.float32)],
        compiler_params=params(),
        cost_estimate=cost(1 << 20, 3 << 20),
    )(place, got, got_sib)
    projected = pl.pallas_call(
        project_columns,
        in_specs=[SMEM] + [VMEM] * 3,
        out_specs=[VMEM] * 4,
        out_shape=projections,
        scratch_shapes=[pltpu.VMEM((X * YZ, 2, count, ROWS, channels), jnp.float32)],
        compiler_params=params(),
        cost_estimate=cost(8 * ROWS * tokens * channels * channels, 6 << 20),
    )(place, got, got_sib, next_weights)
    for_sib, own = attend_all(True, place, projected, quarter)
    branch = pl.pallas_call(
        finish_columns,
        in_specs=[VMEM] * 3,
        out_specs=VMEM,
        out_shape=struct(piece),
        compiler_params=params(),
    )(own, swap(for_sib), w_out)
    back = lax.all_to_all(branch, ("x", "y", "z"), 0, 0)
    return pl.pallas_call(
        add_back,
        in_specs=[VMEM, VMEM],
        out_specs=VMEM,
        out_shape=struct(held),
        compiler_params=params(),
    )(one, back)


def solution(mesh):
    fine = Mesh(mesh.devices.reshape(2, 8, 4, 2, 2), ("y", "z", "x", "c", "dp"))
    held = P(("dp", "y", "z", "x", "c"), None, None)
    return jax.shard_map(
        shards,
        mesh=fine,
        in_specs=(held, P("dp"), P(), P(), P(), P(), P(), P()),
        out_specs=held,
        check_vma=False,
    )
```

time: 151 us -> 132 us (0.87)
  waiting for transfers between devices: 55.2 us -> 11.6 us
  blocking collectives: 27.9 us -> 58.7 us
  starting transfers between devices: 30.5 us -> 19.7 us
  local copies, waits for them, and re-layouts: 4.3 us -> 13.2 us
  Pallas kernels: 31.6 us -> 26.9 us
    all_to_all x3 -> x1, waiting for transfers between devices: 36.5 us -> 0.44 us  [spread_bias(): lax.all_to_all(jnp.broadcast_to(bias[None], (YZ,) + bias.shape), ('y', 'z...]
    all_to_all x0 -> x1, blocking collectives: none -> 34.2 us  [shards(): got = lax.all_to_all(sent, ('x', 'y', 'z'), 0, 0)]
    all_to_all x3 -> x1, starting transfers between devices: 21 us -> 9.29 us  [spread_bias(): lax.all_to_all(jnp.broadcast_to(bias[None], (YZ,) + bias.shape), ('y', 'z...]
    unnamed x15 -> x34, local copies, waits for them, and re-layouts: 1.96 us -> 12.4 us
    ppermute x6, waiting for transfers between devices: 13.2 us -> 4.45 us  [attend_all(): lax.ppermute(piece, 'x', [(i, i ^ s) for i in range(X)])]
    pallas_call x6 -> x10, Pallas kernels: 28.2 us -> 24.2 us  [the longest x6 17 us: attend_some(): pl.pallas_call(functools.partial(attend_quarters, steps, columns), in_spe...]
    all_to_all x1, blocking collectives: 27.9 us -> 24.5 us  [shards(): back = lax.all_to_all(branch, ('x', 'y', 'z'), 0, 0)]
  transfers between devices with their start and end apart: 14 -> 12, of which waited for: 11 -> 9; matrix products, arithmetic and copies ran while one was open for 1% -> 1% of each run, Pallas kernels for 8% -> 13%
where the time goes in v3:
time: 132 us; the launch traced here: 131 us
  blocking collectives  58.7 us (44%)
  Pallas kernels  26.9 us (20%)
  starting transfers between devices  19.7 us (15%)
  local copies, waits for them, and re-layouts  13.2 us (10%)
  waiting for transfers between devices  11.6 us (9%)
    all_to_all x1, blocking collectives, shards(): got = lax.all_to_all(sent, ('x', 'y', 'z'), 0, 0)  34.2 us
    all_to_all x1, blocking collectives, shards(): back = lax.all_to_all(branch, ('x', 'y', 'z'), 0, 0)  24.5 us
    pallas_call x6, Pallas kernels, attend_some(): pl.pallas_call(functools.partial(attend_quarters, steps, columns), in_spe...  17 us
    unnamed x34, local copies, waits for them, and re-layouts  12.4 us
    ppermute x6, starting transfers between devices, attend_all(): lax.ppermute(piece, 'x', [(i, i ^ s) for i in range(X)])  9.48 us
    all_to_all x1, starting transfers between devices, spread_bias(): lax.all_to_all(jnp.broadcast_to(bias[None], (YZ,) + bias.shape), ('y', 'z...  9.29 us
    ppermute x5, waiting for transfers between devices, swap(): return lax.ppermute(array, 'c', [(0, 1), (1, 0)])  6.74 us
    ppermute x6, waiting for transfers between devices, attend_all(): lax.ppermute(piece, 'x', [(i, i ^ s) for i in range(X)])  4.45 us
  transfers between devices with their start and end apart: 12, of which 9 were waited for; matrix products, arithmetic and copies ran while one was open for 1% of the time, Pallas kernels for 13%

profile of v3, /device:TPU:16, one launch (start us, length us, event | category | flops | bytes accessed | tf_op | source)
XLA Modules:
  0.0 131.1 jit_solution(3033609390797558508)
XLA Ops:
  0.7 1.0 copy-done.4
  2.5 1.3 %shard_map.82 = (bf16[4,512,128]{2,1,0:T(8,128)(2,1)S(1)}, bf16[8,512]{1,0:T(8,128)(2,1)S(1)}, bf16[8,512]{1,0:T(8,128)(2,1)S(1)}) custom-call(s32[8]{0:T(128)S(1)} %stack.33.place, bf16[4,512,128]{2,1,0:T(8,128)(2,1)S(1)} %copy-done.4, bf16[2,4,128]{2,1,0:T(4,128)(2,1)S(1)} %bitcast.7), custom_call_target="tpu_custom_call" | custom-call | flops 33554432 | bytes 2097152 | tf_op jit(solution)/shard_map/pallas_call | solution.py:315
  5.9 9.3 %all-to-all-start = ((bf16[16,16,512]{2,1,0:T(8,128)(2,1)}), bf16[16,16,512]{2,1,0:T(8,128)(2,1)S(1)}, u32[]{:S(2)}, u32[]{:S(2)}) async-start(bf16[16,16,512]{2,1,0:T(8,128)(2,1)} %broadcast_in_dim.8), calls=%async_computation | async-start | bytes 524288 | tf_op jit(solution)/shard_map/all_to_all | solution.py:283
  16.0 1.0 copy-done.10
  17.0 1.0 copy-done.12
  18.1 0.8 copy-done.13
  21.4 1.8 %shard_map.83 = (bf16[8,512,128]{2,1,0:T(8,128)(2,1)S(1)}, bf16[8,128,512]{2,1,0:T(8,128)(2,1)S(1)}, bf16[8,512,128]{2,1,0:T(8,128)(2,1)S(1)}, f32[8,512,128]{2,1,0:T(8,128)S(1)}, bf16[128,512]{1,0:T(8,128)(2,1)S(1)}) custom-call(s32[8]{0:T(128)S(1)} %stack.33.place, bf16[4,512,128]{2,1,0:T(8,128)(2,1)S(1)} %copy-done.12, ...), custom_call_target="tpu_custom_call" | custom-call | flops 536870912 | bytes 6291456 | tf_op jit(solution)/shard_map/pallas_call | solution.py:326
  23.3 1.0 copy-done
  24.3 1.0 copy-done.2
  25.7 2.8 %collective-permute-start.4 = (bf16[16,16,512]{2,1,0:T(8,128)(2,1)S(1)}, bf16[16,16,512]{2,1,0:T(8,128)(2,1)S(1)}, u32[]{:S(2)}, u32[]{:S(2)}) collective-permute-start(bf16[16,16,512]{2,1,0:T(8,128)(2,1)S(1)} %all-to-all-done.refs_4_), channel_id=1, source_target_pairs={{0,12},{4,8},{8,4},{12,0},{1,13},{5,9},{9,5},{13,1},{2,14},{6,10},... | collective-permute-start | bytes 786440 | tf_op jit(solution)/shard_map/ppermute | solution.py:231
  28.6 1.7 %collective-permute-start.2 = (bf16[16,16,512]{2,1,0:T(8,128)(2,1)S(1)}, bf16[16,16,512]{2,1,0:T(8,128)(2,1)S(1)}, u32[]{:S(2)}, u32[]{:S(2)}) collective-permute-start(bf16[16,16,512]{2,1,0:T(8,128)(2,1)S(1)} %all-to-all-done.refs_4_), channel_id=1, source_target_pairs={{0,8},{4,12},{8,0},{12,4},{1,9},{5,13},{9,1},{13,5},{2,10},{6,14},... | collective-permute-start | bytes 786440 | tf_op jit(solution)/shard_map/ppermute | solution.py:231
  30.4 1.2 copy-done.1
  31.6 1.2 copy-done.3
  32.8 2.2 %shard_map.84 = (bf16[4,512,128]{2,1,0:T(8,128)(2,1)S(1)}, bf16[4,512,128]{2,1,0:T(8,128)(2,1)S(1)}) custom-call(s32[8]{0:T(128)S(1)} %stack.33.place, bf16[8,512,128]{2,1,0:T(8,128)(2,1)S(1)} %get-tuple-element.43.refs_0_, bf16[8,128,512]{2,1,0:T(8,128)(2,1)S(1)} %copy-done.1, bf16[8,512,128]{2,1,0:T(8,128)(2,1)S(1)} %copy-done.3, ...), custom_call_target="tpu_custom_call" | custom-call | flops 536870912 | bytes 4194304 | tf_op jit(solution)/shard_map/pallas_call | solution.py:216
  35.2 2.5 %collective-permute-done.3.refs_4_ = bf16[16,16,512]{2,1,0:T(8,128)(2,1)S(1)} collective-permute-done((bf16[16,16,512]{2,1,0:T(8,128)(2,1)S(1)}, bf16[16,16,512]{2,1,0:T(8,128)(2,1)S(1)}, u32[]{:S(2)}, u32[]{:S(2)}) %collective-permute-start.3) | collective-permute-done | bytes 262176 | tf_op jit(solution)/shard_map/ppermute | solution.py:231
  37.7 3.6 %shard_map.85 = (bf16[4,512,128]{2,1,0:T(8,128)(2,1)S(1)}, bf16[4,512,128]{2,1,0:T(8,128)(2,1)S(1)}) custom-call(s32[8]{0:T(128)S(1)} %stack.33.place, bf16[8,512,128]{2,1,0:T(8,128)(2,1)S(1)} %get-tuple-element.43.refs_0_, bf16[8,128,512]{2,1,0:T(8,128)(2,1)S(1)} %copy-done.1, ...), custom_call_target="tpu_custom_call", output_to_operand_aliasing={{0}: (7, {}), {1}: (8, {})} | custom-call | flops 1073741824 | bytes 4194304 | tf_op jit(solution)/shard_map/pallas_call | solution.py:216
  41.3 2.2 %shard_map.86 = (bf16[4,512,128]{2,1,0:T(8,128)(2,1)S(1)}, bf16[4,512,128]{2,1,0:T(8,128)(2,1)S(1)}) custom-call(s32[8]{0:T(128)S(1)} %stack.33.place, bf16[8,512,128]{2,1,0:T(8,128)(2,1)S(1)} %get-tuple-element.43.refs_0_, bf16[8,128,512]{2,1,0:T(8,128)(2,1)S(1)} %copy-done.1, ...), custom_call_target="tpu_custom_call", output_to_operand_aliasing={{0}: (6, {}), {1}: (7, {})} | custom-call | flops 536870912 | bytes 4194304 | tf_op jit(solution)/shard_map/pallas_call | solution.py:216
  43.8 1.9 %collective-permute-done.5.got_ref = bf16[4,512,128]{2,1,0:T(8,128)(2,1)S(1)} collective-permute-done((bf16[4,512,128]{2,1,0:T(8,128)(2,1)S(1)}, bf16[4,512,128]{2,1,0:T(8,128)(2,1)S(1)}, u32[]{:S(2)}, u32[]{:S(2)}) %collective-permute-start.5) | collective-permute-done | bytes 524320 | tf_op jit(solution)/shard_map/ppermute | solution.py:274
  45.7 1.5 %shard_map.87 = (bf16[4,512,128]{2,1,0:T(8,128)(2,1)S(1)}, bf16[64,48,128]{2,1,0:T(8,128)(2,1)S(1)}) custom-call(s32[8]{0:T(128)S(1)} %stack.33.place, bf16[4,512,128]{2,1,0:T(8,128)(2,1)S(1)} %get-tuple-element.52.own_ref, bf16[4,512,128]{2,1,0:T(8,128)(2,1)S(1)} %collective-permute-done.5.got_ref, bf16[4,512,128]{2,1,0:T(8,128)(2,1)S(1)} %copy-done.5, ...), custom_call_target="tpu_custom_call" | custom-call | flops 134217728 | bytes 3145728 | tf_op jit(solution)/shard_map/pallas_call | solution.py:337
  47.2 34.2 %all_to_all.15.own_in = bf16[64,48,128]{2,1,0:T(8,128)(2,1)S(1)} all-to-all(bf16[64,48,128]{2,1,0:T(8,128)(2,1)S(1)} %get-tuple-element.55), channel_id=1, replica_groups=mesh['y'=2,'z'=8,'x'=4,'c'=2,'dp'=2] {'x','y','z'}, dimensions={0} | all-to-all | bytes 1572864 | tf_op jit(solution)/shard_map/all_to_all | solution.py:350
  81.4 2.3 %collective-permute-done.6.sib_in = bf16[64,48,128]{2,1,0:T(8,128)(2,1)S(1)} collective-permute-done((bf16[64,48,128]{2,1,0:T(8,128)(2,1)S(1)}, bf16[64,48,128]{2,1,0:T(8,128)(2,1)S(1)}, u32[]{:S(2)}, u32[]{:S(2)}) %collective-permute-start.6) | collective-permute-done | bytes 786464 | tf_op jit(solution)/shard_map/ppermute | solution.py:274
  84.5 1.2 collective-permute-start.9
  85.6 1.3 collective-permute-start.8
  86.9 2.3 %collective-permute-start.7 = (bf16[2,128,512]{2,1,0:T(8,128)(2,1)S(1)}, bf16[2,128,512]{2,1,0:T(8,128)(2,1)S(1)}, u32[]{:S(2)}, u32[]{:S(2)}) collective-permute-start(bf16[2,128,512]{2,1,0:T(8,128)(2,1)S(1)} %shard_map.89.refs_4_), channel_id=1, source_target_pairs={{0,8},{4,12},{8,0},{12,4},{1,9},{5,13},{9,1},{13,5},{2,10},{6,14},... | collective-permute-start | bytes 786440 | tf_op jit(solution)/shard_map/ppermute | solution.py:231
  89.2 3.3 %shard_map.88 = (bf16[8,512,128]{2,1,0:T(8,128)(2,1)S(1)}, bf16[8,128,512]{2,1,0:T(8,128)(2,1)S(1)}, bf16[8,512,128]{2,1,0:T(8,128)(2,1)S(1)}, f32[8,512,128]{2,1,0:T(8,128)S(1)}) custom-call(s32[8]{0:T(128)S(1)} %stack.33.place, bf16[64,48,128]{2,1,0:T(8,128)(2,1)S(1)} %all_to_all.15.own_in, bf16[64,48,128]{2,1,0:T(8,128)(2,1)S(1)} %collective-permute-done.6.sib_in, ...), custom_call_target="tpu_custom_call" | custom-call | flops 536870912 | bytes 6291456 | tf_op jit(solution)/shard_map/pallas_call | solution.py:361
  92.5 2.4 %shard_map.90 = (bf16[64,4,8,128]{3,2,1,0:T(8,128)(2,1)S(1)}, bf16[64,4,8,128]{3,2,1,0:T(8,128)(2,1)S(1)}) custom-call(s32[8]{0:T(128)S(1)} %stack.33.place, bf16[8,512,128]{2,1,0:T(8,128)(2,1)S(1)} %get-tuple-element.57.refs_0_, bf16[8,128,512]{2,1,0:T(8,128)(2,1)S(1)} %get-tuple-element.58.refs_1_, bf16[8,512,128]{2,1,0:T(8,128)(2,1)S(1)} %get-tuple-element.59.refs_2_, ...), custom_call_target="tpu_custom_call" | custom-call | flops 536870912 | bytes 4194304 | tf_op jit(solution)/shard_map/pallas_call | solution.py:216
  95.0 4.2 %shard_map.91 = (bf16[64,4,8,128]{3,2,1,0:T(8,128)(2,1)S(1)}, bf16[64,4,8,128]{3,2,1,0:T(8,128)(2,1)S(1)}) custom-call(s32[8]{0:T(128)S(1)} %stack.33.place, bf16[8,512,128]{2,1,0:T(8,128)(2,1)S(1)} %get-tuple-element.57.refs_0_, bf16[8,128,512]{2,1,0:T(8,128)(2,1)S(1)} %get-tuple-element.58.refs_1_, ...), custom_call_target="tpu_custom_call", output_to_operand_aliasing={{0}: (7, {}), {1}: (8, {})} | custom-call | flops 1073741824 | bytes 4194304 | tf_op jit(solution)/shard_map/pallas_call | solution.py:216
  99.2 1.7 %collective-permute-done.7.refs_4_ = bf16[2,128,512]{2,1,0:T(8,128)(2,1)S(1)} collective-permute-done((bf16[2,128,512]{2,1,0:T(8,128)(2,1)S(1)}, bf16[2,128,512]{2,1,0:T(8,128)(2,1)S(1)}, u32[]{:S(2)}, u32[]{:S(2)}) %collective-permute-start.7) | collective-permute-done | bytes 262176 | tf_op jit(solution)/shard_map/ppermute | solution.py:231
  100.9 2.4 %shard_map.92 = (bf16[64,4,8,128]{3,2,1,0:T(8,128)(2,1)S(1)}, bf16[64,4,8,128]{3,2,1,0:T(8,128)(2,1)S(1)}) custom-call(s32[8]{0:T(128)S(1)} %stack.33.place, bf16[8,512,128]{2,1,0:T(8,128)(2,1)S(1)} %get-tuple-element.57.refs_0_, bf16[8,128,512]{2,1,0:T(8,128)(2,1)S(1)} %get-tuple-element.58.refs_1_, ...), custom_call_target="tpu_custom_call", output_to_operand_aliasing={{0}: (6, {}), {1}: (7, {})} | custom-call | flops 536870912 | bytes 4194304 | tf_op jit(solution)/shard_map/pallas_call | solution.py:216
  103.4 1.9 %collective-permute-done.10.got_ref = bf16[64,4,8,128]{3,2,1,0:T(8,128)(2,1)S(1)} collective-permute-done((bf16[64,4,8,128]{3,2,1,0:T(8,128)(2,1)S(1)}, bf16[64,4,8,128]{3,2,1,0:T(8,128)(2,1)S(1)}, u32[]{:S(2)}, u32[]{:S(2)}) %collective-permute-start.10) | collective-permute-done | bytes 524320 | tf_op jit(solution)/shard_map/ppermute | solution.py:274
  105.6 24.5 %all_to_all.16.back_ref = bf16[64,4,8,128]{3,2,1,0:T(8,128)(2,1)S(1)} all-to-all(bf16[64,4,8,128]{3,2,1,0:T(8,128)(2,1)S(1)} %shard_map.93), channel_id=1, replica_groups=mesh['y'=2,'z'=8,'x'=4,'c'=2,'dp'=2] {'x','y','z'}, dimensions={0} | all-to-all | bytes 1048576 | tf_op jit(solution)/shard_map/all_to_all | solution.py:378
  130.1 0.9 shard_map.94
  (49 shorter events, 8.5 us)
Async XLA Ops:
  0.7 1.0 copy-start.4
  1.8 0.7 copy-start.7
  3.8 11.4 %copy-start.9 = (bf16[4,512,128]{2,1,0:T(8,128)(2,1)}, bf16[4,512,128]{2,1,0:T(8,128)(2,1)S(1)}, u32[]{:S(2)}) copy-start(bf16[4,512,128]{2,1,0:T(8,128)(2,1)S(1)} %get-tuple-element.38.own_ref) | copy-start | bytes 1572868
  3.8 1.3 collective-permute-start
  3.9 11.3 %collective-permute-start.1 = (bf16[4,512,128]{2,1,0:T(8,128)(2,1)S(1)}, bf16[4,512,128]{2,1,0:T(8,128)(2,1)S(1)}, u32[]{:S(2)}, u32[]{:S(2)}) collective-permute-start(bf16[4,512,128]{2,1,0:T(8,128)(2,1)S(1)} %get-tuple-element.38.own_ref), channel_id=1, source_target_pairs={{0,2},{2,0},{1,3},{3,1},{4,6},{6,4},{5,7},{7,5},{8,10},{10,8},{9,1... | collective-permute-start | bytes 1572872 | tf_op jit(solution)/shard_map/ppermute | solution.py:274
  5.9 19.8 %all-to-all-start = ((bf16[16,16,512]{2,1,0:T(8,128)(2,1)}), bf16[16,16,512]{2,1,0:T(8,128)(2,1)S(1)}, u32[]{:S(2)}, u32[]{:S(2)}) async-start(bf16[16,16,512]{2,1,0:T(8,128)(2,1)} %broadcast_in_dim.8), calls=%async_computation | async-start | bytes 524288 | tf_op jit(solution)/shard_map/all_to_all | solution.py:283
  15.2 0.8 copy-start.11
  16.0 1.0 copy-start.10
  17.0 1.0 copy-start.12
  18.1 0.8 copy-start.13
  18.9 0.8 copy-start.14
  19.7 0.8 copy-start.15
  20.6 0.8 copy-start.16
  23.3 1.0 copy-start
  24.2 1.0 copy-start.2
  25.7 9.6 %collective-permute-start.4 = (bf16[16,16,512]{2,1,0:T(8,128)(2,1)S(1)}, bf16[16,16,512]{2,1,0:T(8,128)(2,1)S(1)}, u32[]{:S(2)}, u32[]{:S(2)}) collective-permute-start(bf16[16,16,512]{2,1,0:T(8,128)(2,1)S(1)} %all-to-all-done.refs_4_), channel_id=1, source_target_pairs={{0,12},{4,8},{8,4},{12,0},{1,13},{5,9},{9,5},{13,1},{2,14},{6,10},... | collective-permute-start | bytes 786440 | tf_op jit(solution)/shard_map/ppermute | solution.py:231
  28.4 9.2 %collective-permute-start.3 = (bf16[16,16,512]{2,1,0:T(8,128)(2,1)S(1)}, bf16[16,16,512]{2,1,0:T(8,128)(2,1)S(1)}, u32[]{:S(2)}, u32[]{:S(2)}) collective-permute-start(bf16[16,16,512]{2,1,0:T(8,128)(2,1)S(1)} %all-to-all-done.refs_4_), channel_id=1, source_target_pairs={{0,4},{4,0},{8,12},{12,8},{1,5},{5,1},{9,13},{13,9},{2,6},{6,2},{1... | collective-permute-start | bytes 786440 | tf_op jit(solution)/shard_map/ppermute | solution.py:231
  28.6 12.7 %collective-permute-start.2 = (bf16[16,16,512]{2,1,0:T(8,128)(2,1)S(1)}, bf16[16,16,512]{2,1,0:T(8,128)(2,1)S(1)}, u32[]{:S(2)}, u32[]{:S(2)}) collective-permute-start(bf16[16,16,512]{2,1,0:T(8,128)(2,1)S(1)} %all-to-all-done.refs_4_), channel_id=1, source_target_pairs={{0,8},{4,12},{8,0},{12,4},{1,9},{5,13},{9,1},{13,5},{2,10},{6,14},... | collective-permute-start | bytes 786440 | tf_op jit(solution)/shard_map/ppermute | solution.py:231
  30.4 1.2 copy-start.1
  31.6 1.2 copy-start.3
  41.3 4.4 %copy-start.5 = (bf16[4,512,128]{2,1,0:T(8,128)(2,1)S(1)}, bf16[4,512,128]{2,1,0:T(8,128)(2,1)}, u32[]{:S(2)}) copy-start(bf16[4,512,128]{2,1,0:T(8,128)(2,1)} %pair_ref.3) | copy-start | bytes 1572868
  41.3 4.4 %copy-start.6 = (bf16[2,128,128]{2,1,0:T(8,128)(2,1)S(1)}, bf16[2,128,128]{2,1,0:T(8,128)(2,1)}, u32[]{:S(2)}) copy-start(bf16[2,128,128]{2,1,0:T(8,128)(2,1)} %w_ref.3) | copy-start | bytes 196612
  41.3 4.4 %copy-start.8 = (bf16[2,128,4]{1,2,0:T(4,128)(2,1)S(1)}, bf16[2,128,4]{1,2,0:T(4,128)(2,1)}, u32[]{:S(2)}) copy-start(bf16[2,128,4]{1,2,0:T(4,128)(2,1)} %param.14) | copy-start | bytes 6148
  43.5 2.2 %collective-permute-start.5 = (bf16[4,512,128]{2,1,0:T(8,128)(2,1)S(1)}, bf16[4,512,128]{2,1,0:T(8,128)(2,1)S(1)}, u32[]{:S(2)}, u32[]{:S(2)}) collective-permute-start(bf16[4,512,128]{2,1,0:T(8,128)(2,1)S(1)} %get-tuple-element.53), channel_id=1, source_target_pairs={{0,2},{2,0},{1,3},{3,1},{4,6},{6,4},{5,7},{7,5},{8,10},{10,8},{9,1... | collective-permute-start | bytes 1572872 | tf_op jit(solution)/shard_map/ppermute | solution.py:274
  81.4 2.3 %collective-permute-start.6 = (bf16[64,48,128]{2,1,0:T(8,128)(2,1)S(1)}, bf16[64,48,128]{2,1,0:T(8,128)(2,1)S(1)}, u32[]{:S(2)}, u32[]{:S(2)}) collective-permute-start(bf16[64,48,128]{2,1,0:T(8,128)(2,1)S(1)} %all_to_all.15.own_in), channel_id=1, source_target_pairs={{0,2},{2,0},{1,3},{3,1},{4,6},{6,4},{5,7},{7,5},{8,10},{10,8},{9,1... | collective-permute-start | bytes 2359304 | tf_op jit(solution)/shard_map/ppermute | solution.py:274
  84.5 10.5 %collective-permute-start.9 = (bf16[2,128,512]{2,1,0:T(8,128)(2,1)S(1)}, bf16[2,128,512]{2,1,0:T(8,128)(2,1)S(1)}, u32[]{:S(2)}, u32[]{:S(2)}) collective-permute-start(bf16[2,128,512]{2,1,0:T(8,128)(2,1)S(1)} %shard_map.89.refs_4_), channel_id=1, source_target_pairs={{0,12},{4,8},{8,4},{12,0},{1,13},{5,9},{9,5},{13,1},{2,14},{6,10},... | collective-permute-start | bytes 786440 | tf_op jit(solution)/shard_map/ppermute | solution.py:231
  85.6 9.3 %collective-permute-start.8 = (bf16[2,128,512]{2,1,0:T(8,128)(2,1)S(1)}, bf16[2,128,512]{2,1,0:T(8,128)(2,1)S(1)}, u32[]{:S(2)}, u32[]{:S(2)}) collective-permute-start(bf16[2,128,512]{2,1,0:T(8,128)(2,1)S(1)} %shard_map.89.refs_4_), channel_id=1, source_target_pairs={{0,4},{4,0},{8,12},{12,8},{1,5},{5,1},{9,13},{13,9},{2,6},{6,2},{1... | collective-permute-start | bytes 786440 | tf_op jit(solution)/shard_map/ppermute | solution.py:231
  86.9 14.0 %collective-permute-start.7 = (bf16[2,128,512]{2,1,0:T(8,128)(2,1)S(1)}, bf16[2,128,512]{2,1,0:T(8,128)(2,1)S(1)}, u32[]{:S(2)}, u32[]{:S(2)}) collective-permute-start(bf16[2,128,512]{2,1,0:T(8,128)(2,1)S(1)} %shard_map.89.refs_4_), channel_id=1, source_target_pairs={{0,8},{4,12},{8,0},{12,4},{1,9},{5,13},{9,1},{13,5},{2,10},{6,14},... | collective-permute-start | bytes 786440 | tf_op jit(solution)/shard_map/ppermute | solution.py:231
  103.3 2.0 %collective-permute-start.10 = (bf16[64,4,8,128]{3,2,1,0:T(8,128)(2,1)S(1)}, bf16[64,4,8,128]{3,2,1,0:T(8,128)(2,1)S(1)}, u32[]{:S(2)}, u32[]{:S(2)}) collective-permute-start(bf16[64,4,8,128]{3,2,1,0:T(8,128)(2,1)S(1)} %get-tuple-element.66), channel_id=1, source_target_pairs={{0,2},{2,0},{1,3},{3,1},{4,6},{6,4},{5,7},{7,5},{8,10},{10,8},{9,1... | collective-permute-start | bytes 1572872 | tf_op jit(solution)/shard_map/ppermute | solution.py:274

commit v4 on v3

--- a/solution.py
+++ b/solution.py
@@ -18,7 +18,10 @@
 SMEM = pl.BlockSpec(memory_space=pltpu.SMEM)
 VMEM = pl.BlockSpec(memory_space=pltpu.VMEM)
 
-CORE, VALID, SPOT, FIRST_ROW = 0, 2, 3, 7
+HALF = 2 * QUARTER
+
+CORE, UPPER, VALID, SPOT, FIRST_ROW, LOCAL = 0, 1, 2, 3, 7, 9
+X_AXES = ("xh", "xl")
 
 
 def params(mebibytes=12):
@@ -30,8 +33,12 @@
 
 
 def inner_order(rows):
+    return jnp.concatenate(inner_quarters(rows), axis=0)
+
+
+def inner_quarters(rows):
     parts = rows.reshape(YZ, X, ROWS, rows.shape[-1])
-    return jnp.concatenate([parts[:, x].reshape(QUARTER, -1) for x in range(X)], axis=0)
+    return [parts[:, x].reshape(QUARTER, -1) for x in range(X)]
 
 
 def outer_order(rows):
@@ -72,6 +79,12 @@
     other_ref[...] = jnp.where(first, high, low).astype(jnp.bfloat16)
 
 
+def prepare_far(far_ref, normed_ref):
+    for r in range(far_ref.shape[0]):
+        wide = inner_order(far_ref[r].astype(jnp.float32))
+        normed_ref[r] = layer_normed(wide).astype(jnp.bfloat16)
+
+
 def project(core, normed, weights):
     tokens, channels = normed.shape
     projected = jnp.dot(normed, weights, preferred_element_type=jnp.float32)
@@ -83,23 +96,35 @@
     return query, key_t, value.astype(jnp.bfloat16), gate
 
 
-def project_rows(place, sib_ref, own_ref, *refs):
-    w_refs, (query_ref, key_ref, value_ref, gate_ref, next_ref) = refs[:4], refs[4:]
-    weights = jnp.concatenate([ref[0] for ref in w_refs], axis=1)
-    next_ref[...] = jnp.concatenate([ref[1] for ref in w_refs], axis=1)
+def pack_weights(wq, wk, wv, wg, first_ref, next_ref):
+    for step, ref in enumerate((first_ref, next_ref)):
+        ref[...] = jnp.concatenate([w[step] for w in (wq, wk, wv, wg)], axis=1)
+
+
+def project_rows(place, sib_ref, own_ref, w_ref, query_ref, key_ref, value_ref, gate_ref, done_ref):
+    done_ref[...] = jnp.zeros_like(done_ref)
     for r in range(ROWS):
         normed = sib_ref[r] if r < ROWS // 2 else own_ref[r - ROWS // 2]
-        query, key_t, value, gate = project(place[CORE], normed, weights)
+        query, key_t, value, gate = project(place[CORE], normed, w_ref[...])
         query_ref[r], key_ref[r], value_ref[r], gate_ref[r] = query, key_t, value, gate
+
+
+def received_quarters(place):
+    upper = place[UPPER]
+    return [
+        (x, far, 2 * (1 - upper if far else upper) + x) for x in range(X // 2) for far in range(2)
+    ]
 
 
 def project_columns(place, own_in, sib_in, w_ref, query_ref, key_ref, value_ref, gate_ref, cols_ref):
     core = place[CORE]
-    chips, _, count, width, channels = cols_ref.shape
+    _, _, _, count, width, channels = cols_ref.shape
     for ref, at in ((own_in, core), (sib_in, 1 - core)):
-        part = ref[:, : count * width, :].astype(jnp.float32)
-        cols_ref[:, pl.ds(at, 1)] = part.reshape(chips, 1, count, width, channels)
-    flat = cols_ref.reshape(chips * 2 * count, width, channels)
+        part = ref[:, : 2 * count * width, :].astype(jnp.float32)
+        part = part.reshape(X // 2, YZ, 2, count, width, channels)
+        for x, far, quarter in received_quarters(place):
+            cols_ref[pl.ds(quarter, 1), :, pl.ds(at, 1)] = part[x, :, far][None, :, None]
+    flat = cols_ref.reshape(X * YZ * 2 * count, width, channels)
     for j in range(width):
         normed = flat[:, j, :].astype(jnp.bfloat16)
         query, key_t, value, gate = project(core, normed, w_ref[...])
@@ -108,18 +133,22 @@
 
 def turn_bias(place, own_in, sib_in, out_ref, keyed_ref):
     first = place[CORE] == 0
-    chips, width, _ = keyed_ref.shape[1:]
+    _, _, _, width, _ = keyed_ref.shape
     count = width // 2
     parts = []
     for ref in (own_in, sib_in):
-        rows = ref[:, count * width :, :].astype(jnp.float32)
-        parts.append(jnp.where(first, rows[:, : 2 * count], rows[:, 2 * count :]))
+        rows = ref[:, 2 * count * width :, :].astype(jnp.float32)
+        middle = rows.shape[1] // 2
+        parts.append(jnp.where(first, rows[:, :middle], rows[:, middle:]))
     own, sib = parts
     low, high = jnp.where(first, own, sib), jnp.where(first, sib, own)
     for h in range(2):
-        keyed_ref[h, :, :count, :] = low[:, h * count : (h + 1) * count]
-        keyed_ref[h, :, count:, :] = high[:, h * count : (h + 1) * count]
-        keyed = keyed_ref[h].reshape(chips * width, -1)
+        for x, far, quarter in received_quarters(place):
+            at = (2 * h + far) * count
+            for core, part in enumerate((low, high)):
+                piece = part[x * YZ : (x + 1) * YZ, at : at + count]
+                keyed_ref[h, pl.ds(quarter, 1), :, core * count : (core + 1) * count] = piece[None]
+        keyed = keyed_ref[h].reshape(X * YZ * width, -1)
         out_ref[h] = keyed.T.astype(jnp.bfloat16)
 
 
@@ -159,8 +188,8 @@
 
 def attend_quarters(steps, columns, place, *refs):
     core = place[CORE]
-    query_ref, key_ref, value_ref, gate_ref = refs[:4]
-    pieces = refs[4 : 4 + len(steps)]
+    groups = 1 if columns else 2
+    pieces = refs[4 * groups : 4 * groups + len(steps)]
     sib_ref, own_ref, wide_ref = refs[-4:-1] if columns else refs[-3:]
     out_ref = refs[-1]
     units = []
@@ -170,27 +199,30 @@
             rows = wide[h] if columns else wide[:, h * ROWS : (h + 1) * ROWS]
             wide_ref[i, h] = rows.reshape(wide_ref.shape[2:])
         span = pl.ds(pl.multiple_of(place[SPOT + s] * QUARTER, QUARTER), QUARTER)
-        for r in range(ROWS):
-
-            def put(value, i=i, r=r, span=span):
-                if columns:
-                    out_ref.reshape(len(steps), QUARTER, ROWS, -1)[i, :, r, :] = value
-                elif r < ROWS // 2:
-                    sib_ref[r, span, :] = value.astype(jnp.bfloat16)
-                else:
-                    own_ref[r - ROWS // 2, span, :] = value.astype(jnp.bfloat16)
-
-            units.append(
-                (
-                    lambda r=r, span=span: query_ref[r, span, :],
-                    lambda r=r: key_ref[r],
-                    lambda i=i: wide_ref[i],
-                    lambda r=r: value_ref[r],
-                    lambda r=r, span=span: gate_ref[r, span, :],
-                    put,
+        for g in range(groups):
+            query_ref, key_ref, value_ref, gate_ref = refs[4 * g : 4 * g + 4]
+            for r in range(ROWS):
+
+                def put(value, i=i, g=g, r=r, s=s):
+                    if columns:
+                        out_ref.reshape(len(steps), QUARTER, ROWS, -1)[i, :, r, :] = value
+                        return
+                    local = pl.ds(pl.multiple_of(place[LOCAL + s] * QUARTER, QUARTER), QUARTER)
+                    half = ROWS // 2
+                    ref = sib_ref if r < half else own_ref
+                    ref[g * half + r % half, local, :] = value.astype(jnp.bfloat16)
+
+                units.append(
+                    (
+                        lambda ref=query_ref, r=r, span=span: ref[r, span, :],
+                        lambda ref=key_ref, r=r: ref[r],
+                        lambda i=i: wide_ref[i],
+                        lambda ref=value_ref, r=r: ref[r],
+                        lambda ref=gate_ref, r=r, span=span: ref[r, span, :],
+                        put,
+                    )
                 )
-            )
-    attend(core, units, QUARTER, query_ref.shape[-1])
+    attend(core, units, QUARTER, sib_ref.shape[-1])
     if columns:
         for i, s in enumerate(steps):
             chips = pl.ds(place[SPOT + s] * YZ, YZ)
@@ -206,13 +238,13 @@
         shape = struct((X * YZ, count, rows, channels))
         scratch.append(pltpu.VMEM((len(steps), YZ, 2, count, rows, channels), jnp.float32))
     else:
-        shape = struct((count, tokens, channels))
+        shape = struct((rows, HALF, channels))
     operands = [place, *projected, *pieces]
     aliases = {}
     if outs is not None:
         aliases = {len(operands) + i: i for i in range(2)}
         operands += list(outs)
-    units = len(steps) * rows * 2
+    units = len(steps) * rows * 2 * len(projected) // 4
     return pl.pallas_call(
         functools.partial(attend_quarters, steps, columns),
         in_specs=[SMEM] + [VMEM] * (len(operands) - 1),
@@ -227,29 +259,41 @@
     )(*operands)
 
 
+def along_x(array, s):
+    return lax.ppermute(array, X_AXES, [(i, i ^ s) for i in range(X)])
+
+
 def attend_all(columns, place, projected, piece):
-    moved = {s: lax.ppermute(piece, "x", [(i, i ^ s) for i in range(X)]) for s in (1, 3, 2)}
-    outs = attend_some((0,), columns, place, projected, [piece], None)
-    outs = attend_some((1, 3), columns, place, projected, [moved[1], moved[3]], outs)
-    return attend_some((2,), columns, place, projected, [moved[2]], outs)
-
-
-def finish_rows(place, own_ref, got_ref, pair_ref, w_ref, wb_ref, one_ref, sent_ref, rows_ref, wide_ref):
-    count, tokens, channels = own_ref.shape
+    steps = [(0,), (1, 3), (2,)] if columns else [(0,), (1,)]
+    moved = {s: along_x(piece, s) for some in steps[1:] for s in some}
+    outs = attend_some(steps[0], columns, place, projected, [piece], None)
+    for some in steps[1:]:
+        outs = attend_some(some, columns, place, projected, [moved[s] for s in some], outs)
+    return outs
+
+
+def finish_rows(place, own_ref, got_ref, pair_ref, far_ref, w_ref, wb_ref, near_ref, other_ref, sent_ref, rows_ref, wide_ref):
+    count, half, channels = near_ref.shape
     chips = sent_ref.shape[0]
-    for r in range(count):
-        gated = own_ref[r] + got_ref[r]
-        branch = jnp.dot(gated, w_ref[0], preferred_element_type=jnp.float32)
-        one = (inner_order(pair_ref[r].astype(jnp.float32)) + branch).astype(jnp.bfloat16)
-        one_ref[r] = one
-        normed = layer_normed(one.astype(jnp.float32))
-        wide_ref[:, r * ROWS : (r + 1) * ROWS] = normed.reshape(chips, ROWS, channels)
-        masked = place[FIRST_ROW] + r >= place[VALID]
-        bias_rows(wb_ref, 1, normed.astype(jnp.bfloat16), r, count, masked, rows_ref)
-    sent_ref[:, : count * ROWS] = wide_ref[...].astype(jnp.bfloat16)
-    for x in range(X):
+    lower = place[UPPER] == 0
+    for far, (raw_ref, one_ref) in enumerate(((pair_ref, near_ref), (far_ref, other_ref))):
+        for r in range(count):
+            at = far * count + r
+            gated = own_ref[at] + got_ref[at]
+            branch = jnp.dot(gated, w_ref[0], preferred_element_type=jnp.float32)
+            q = inner_quarters(raw_ref[r].astype(jnp.float32))
+            raw = jnp.concatenate([jnp.where(lower, q[x], q[2 + x]) for x in range(2)], axis=0)
+            one = (raw + branch).astype(jnp.bfloat16)
+            one_ref[r] = one
+            normed = layer_normed(one.astype(jnp.float32))
+            wide_ref[:, at * ROWS : (at + 1) * ROWS] = normed.reshape(chips, ROWS, channels)
+            masked = place[FIRST_ROW + far] + r >= place[VALID]
+            bias_rows(wb_ref, 1, normed.astype(jnp.bfloat16), at, 2 * count, masked, rows_ref)
+    rows = 2 * count * ROWS
+    sent_ref[:, :rows] = wide_ref[...].astype(jnp.bfloat16)
+    for x in range(X // 2):
         quarter = rows_ref[:, x * QUARTER : (x + 1) * QUARTER].astype(jnp.bfloat16)
-        sent_ref[x * YZ : (x + 1) * YZ, count * ROWS :] = jnp.broadcast_to(
+        sent_ref[x * YZ : (x + 1) * YZ, rows:] = jnp.broadcast_to(
             quarter[None], (YZ,) + quarter.shape
         )
 
@@ -262,12 +306,14 @@
     out_ref[...] = branch.reshape(chips, rows, width, channels).astype(jnp.bfloat16)
 
 
-def add_back(one_ref, back_ref, out_ref):
+def add_back(place, near_ref, got_ref, back_ref, out_ref):
     chips, count, width, channels = back_ref.shape
+    lower = place[UPPER] == 0
     for r in range(count):
         back = back_ref[:, r].astype(jnp.float32).reshape(chips * width, channels)
-        total = one_ref[r].astype(jnp.float32) + back
-        out_ref[r] = outer_order(total).astype(jnp.bfloat16)
+        near, got = near_ref[r].astype(jnp.float32), got_ref[r].astype(jnp.float32)
+        one = jnp.concatenate([jnp.where(lower, near, got), jnp.where(lower, got, near)], axis=0)
+        out_ref[r] = outer_order(one + back).astype(jnp.bfloat16)
 
 
 def swap(array):
@@ -293,10 +339,12 @@
 
 def shards(pair, valid, w_query, w_key, w_value, w_gate, w_bias, w_out):
     count, tokens, channels = pair.shape
-    core, x = lax.axis_index("c"), lax.axis_index("x")
+    core, upper, lower = (lax.axis_index(name) for name in ("c", "xh", "xl"))
+    x = 2 * upper + lower
     chip = lax.axis_index("y") * lax.axis_size("z") + lax.axis_index("z")
-    first_row = (chip * X + x) * ROWS + core * count
-    place = jnp.stack([core, x, valid[0]] + [x ^ s for s in range(X)] + [first_row])
+    first_rows = [(chip * X + (x ^ s)) * ROWS + core * count for s in (0, 2)]
+    spots = [x ^ s for s in range(X)]
+    place = jnp.stack([core, upper, valid[0]] + spots + first_rows + [lower, 1 - lower])
     place = place.astype(jnp.int32)
     wb = jnp.swapaxes(w_bias, 1, 2)
     weights = [w_query, w_key, w_value, w_gate]
@@ -312,10 +360,10 @@
         struct(rows, jnp.float32),
     ]
 
+    far = along_x(pair, 2)
     normed, mine, other = pl.pallas_call(
         prepare_rows,
-        grid=(1,),
-        in_specs=[SMEM, whole(pair.shape), whole(wb.shape)],
+        in_specs=[SMEM, VMEM, VMEM],
         out_specs=[VMEM] * 3,
         out_shape=[struct(held), half, half],
         scratch_shapes=[bias_scratch],
@@ -323,38 +371,65 @@
         cost_estimate=cost(1 << 25, 2 << 20),
     )(place, pair, wb)
     gathered = spread_bias(core, mine, other)
-    *projected, next_weights = pl.pallas_call(
-        project_rows,
+    packed = struct((channels, 4 * channels))
+    first_weights, next_weights = pl.pallas_call(
+        pack_weights,
+        in_specs=[VMEM] * 4,
+        out_specs=[VMEM] * 2,
+        out_shape=[packed, packed],
+        compiler_params=params(),
+    )(*weights)
+    def project_group(array):
+        *projected, done = pl.pallas_call(
+            project_rows,
+            in_specs=[SMEM, VMEM, VMEM, VMEM],
+            out_specs=[VMEM] * 5,
+            out_shape=projections + [struct((8, 128), jnp.float32)],
+            compiler_params=params(),
+            cost_estimate=cost(8 * ROWS * tokens * channels * channels, 6 << 20),
+        )(place, swap(array), array, first_weights)
+        return projected, done
+
+    projected, done = project_group(normed)
+    far, done = lax.optimization_barrier((far, done))
+    normed_far = pl.pallas_call(
+        prepare_far,
+        in_specs=[VMEM],
+        out_specs=VMEM,
+        out_shape=struct(held),
+        compiler_params=params(),
+        cost_estimate=cost(1 << 24, 1 << 20),
+    )(far)
+    projected_far, done = project_group(normed_far)
+    gathered, done = lax.optimization_barrier((gathered, done))
+    projected = projected + projected_far
+    for_sib, own = attend_all(False, place, projected, gathered)
+    peers = X // 2 * YZ
+    message = (peers, 2 * count * ROWS + 8 * count, channels)
+    half_rows = struct((count, HALF, channels))
+    near, other, sent = pl.pallas_call(
+        finish_rows,
         in_specs=[SMEM] + [VMEM] * 6,
-        out_specs=[VMEM] * 5,
-        out_shape=projections + [struct((channels, 4 * channels))],
-        compiler_params=params(),
-        cost_estimate=cost(8 * ROWS * tokens * channels * channels, 6 << 20),
-    )(place, swap(normed), normed, *weights)
-    gathered, *projected = lax.optimization_barrier((gathered, *projected))
-    for_sib, own = attend_all(False, place, projected, gathered)
-    message = (X * YZ, count * ROWS + 4 * count, channels)
-    one, sent = pl.pallas_call(
-        finish_rows,
-        in_specs=[SMEM] + [VMEM] * 5,
-        out_specs=[VMEM] * 2,
-        out_shape=[struct(held), struct(message)],
+        out_specs=[VMEM] * 3,
+        out_shape=[half_rows, half_rows, struct(message)],
         scratch_shapes=[
-            bias_scratch,
-            pltpu.VMEM((X * YZ, count * ROWS, channels), jnp.float32),
+            pltpu.VMEM((8 * count, HALF), jnp.float32),
+            pltpu.VMEM((peers, 2 * count * ROWS, channels), jnp.float32),
         ],
         compiler_params=params(),
         cost_estimate=cost(1 << 27, 3 << 20),
-    )(place, own, swap(for_sib), pair, w_out, wb)
-
-    got = lax.all_to_all(sent, ("x", "y", "z"), 0, 0)
+    )(place, own, swap(for_sib), pair, far, w_out, wb)
+
+    got = lax.all_to_all(sent, ("xl", "y", "z"), 0, 0)
+    got_near = along_x(other, 2)
+    got, got_near = lax.optimization_barrier((got, got_near))
     got_sib = swap(got)
     quarter = pl.pallas_call(
         turn_bias,
         in_specs=[SMEM, VMEM, VMEM],
         out_specs=VMEM,
         out_shape=struct((2, QUARTER, tokens)),
-        scratch_shapes=[pltpu.VMEM((2, X * YZ, ROWS, QUARTER), jnp.float32)],
+        scratch_shapes=[pltpu.VMEM((2, X, YZ, ROWS, QUARTER), jnp.float32)],
         compiler_params=params(),
         cost_estimate=cost(1 << 20, 3 << 20),
     )(place, got, got_sib)
@@ -363,7 +438,7 @@
         in_specs=[SMEM] + [VMEM] * 3,
         out_specs=[VMEM] * 4,
         out_shape=projections,
-        scratch_shapes=[pltpu.VMEM((X * YZ, 2, count, ROWS, channels), jnp.float32)],
+        scratch_shapes=[pltpu.VMEM((X, YZ, 2, count, ROWS, channels), jnp.float32)],
         compiler_params=params(),
         cost_estimate=cost(8 * ROWS * tokens * channels * channels, 6 << 20),
     )(place, got, got_sib, next_weights)
@@ -375,19 +450,19 @@
         out_shape=struct(piece),
         compiler_params=params(),
     )(own, swap(for_sib), w_out)
-    back = lax.all_to_all(branch, ("x", "y", "z"), 0, 0)
+    back = lax.all_to_all(branch, X_AXES + ("y", "z"), 0, 0)
     return pl.pallas_call(
         add_back,
-        in_specs=[VMEM, VMEM],
+        in_specs=[SMEM, VMEM, VMEM, VMEM],
         out_specs=VMEM,
         out_shape=struct(held),
         compiler_params=params(),
-    )(one, back)
+    )(place, near, got_near, back)
 
 
 def solution(mesh):
-    fine = Mesh(mesh.devices.reshape(2, 8, 4, 2, 2), ("y", "z", "x", "c", "dp"))
-    held = P(("dp", "y", "z", "x", "c"), None, None)
+    fine = Mesh(mesh.devices.reshape(2, 8, 2, 2, 2, 2), ("y", "z", "xh", "xl", "c", "dp"))
+    held = P(("dp", "y", "z", "xh", "xl", "c"), None, None)
     return jax.shard_map(
         shards,
         mesh=fine,

time: 132 us -> 124 us (0.939)
  blocking collectives: 58.7 us -> 23.9 us
  waiting for transfers between devices: 11.6 us -> 39.4 us
  local copies, waits for them, and re-layouts: 13.2 us -> 2.62 us
  starting transfers between devices: 19.7 us -> 25.5 us
  Pallas kernels: 26.9 us -> 31.3 us
    all_to_all x2 -> x1, blocking collectives: 58.7 us -> 23.9 us  [shards(): back = lax.all_to_all(branch, X_AXES + ('y', 'z'), 0, 0)]
    unnamed x34 -> x18, local copies, waits for them, and re-layouts: 12.4 us -> 1.76 us
    ppermute x6, waiting for transfers between devices: 4.45 us -> 14 us  [along_x(): return lax.ppermute(array, X_AXES, [(i, i ^ s) for i in range(X)])]
    all_to_all x0 -> x1, waiting for transfers between devices: none -> 9.11 us  [shards(): got = lax.all_to_all(sent, ('xl', 'y', 'z'), 0, 0)]
    all_to_all x1, waiting for transfers between devices: 0.44 us -> 9.14 us  [spread_bias(): lax.all_to_all(jnp.broadcast_to(bias[None], (YZ,) + bias.shape), ('y', 'z...]
    all_to_all x0 -> x1, starting transfers between devices: none -> 5.62 us  [shards(): got = lax.all_to_all(sent, ('xl', 'y', 'z'), 0, 0)]
    pallas_call x4 -> x7, Pallas kernels: 5.59 us -> 10.6 us  [the longest x2 4.69 us: project_group(): pl.pallas_call(project_rows, in_specs=[SMEM, VMEM, VMEM, VMEM], out_specs...]
    pallas_call x6 -> x5, Pallas kernels: 17 us -> 16.4 us  [attend_some(): pl.pallas_call(functools.partial(attend_quarters, steps, columns), in_spe...]
  transfers between devices with their start and end apart: 12 -> 14, of which waited for: 9 -> 8; matrix products, arithmetic and copies ran while one was open for 1% -> 1% of each run, Pallas kernels for 13% -> 16%
where the time goes in v4:
time: 124 us
  waiting for transfers between devices  39.4 us (32%)
  Pallas kernels  31.3 us (25%)
  starting transfers between devices  25.5 us (21%)
  blocking collectives  23.9 us (19%)
  local copies, waits for them, and re-layouts  2.62 us (2%)
    all_to_all x1, blocking collectives, shards(): back = lax.all_to_all(branch, X_AXES + ('y', 'z'), 0, 0)  23.9 us
    pallas_call x5, Pallas kernels, attend_some(): pl.pallas_call(functools.partial(attend_quarters, steps, columns), in_spe...  16.4 us
    ppermute x6, waiting for transfers between devices, along_x(): return lax.ppermute(array, X_AXES, [(i, i ^ s) for i in range(X)])  14 us
    ppermute x6, starting transfers between devices, along_x(): return lax.ppermute(array, X_AXES, [(i, i ^ s) for i in range(X)])  9.63 us
    all_to_all x1, starting transfers between devices, spread_bias(): lax.all_to_all(jnp.broadcast_to(bias[None], (YZ,) + bias.shape), ('y', 'z...  9.29 us
    all_to_all x1, waiting for transfers between devices, spread_bias(): lax.all_to_all(jnp.broadcast_to(bias[None], (YZ,) + bias.shape), ('y', 'z...  9.14 us
    all_to_all x1, waiting for transfers between devices, shards(): got = lax.all_to_all(sent, ('xl', 'y', 'z'), 0, 0)  9.11 us
    ppermute x6, waiting for transfers between devices, swap(): return lax.ppermute(array, 'c', [(0, 1), (1, 0)])  7.24 us
  transfers between devices with their start and end apart: 14, of which 8 were waited for; matrix products, arithmetic and copies ran while one was open for 1% of the time, Pallas kernels for 16%

profile of v4, /device:TPU:16, one launch (start us, length us, event | category | flops | bytes accessed | tf_op | source)
XLA Modules:
  0.0 123.7 jit_solution(16047063902603027041)
XLA Ops:
  0.0 3.0 %collective-permute-start.1 = (bf16[4,512,128]{2,1,0:T(8,128)(2,1)}, bf16[4,512,128]{2,1,0:T(8,128)(2,1)S(1)}, u32[]{:S(2)}, u32[]{:S(2)}) collective-permute-start(bf16[4,512,128]{2,1,0:T(8,128)(2,1)} %pair_ref.3), channel_id=1, source_target_pairs={{0,8},{4,12},{8,0},{12,4},{1,9},{5,13},{9,1},{13,5},{2,10},{6,14},... | collective-permute-start | bytes 1572872 | tf_op jit(solution)/shard_map/ppermute | solution.py:263
  3.8 1.0 copy-done
  4.8 0.7 copy-done.7
  5.5 1.3 %shard_map.82 = (bf16[4,512,128]{2,1,0:T(8,128)(2,1)S(1)}, bf16[8,512]{1,0:T(8,128)(2,1)S(1)}, bf16[8,512]{1,0:T(8,128)(2,1)S(1)}) custom-call(s32[11]{0:T(128)S(1)} %stack.48.place, bf16[4,512,128]{2,1,0:T(8,128)(2,1)S(1)} %copy-done, bf16[2,4,128]{2,1,0:T(4,128)(2,1)S(1)} %bitcast.11), custom_call_target="tpu_custom_call" | custom-call | flops 33554432 | bytes 2097152 | tf_op jit(solution)/shard_map/pallas_call | solution.py:364
  6.9 1.2 collective-permute-done.3
  8.2 0.7 broadcast_in_dim.8
  8.9 9.3 %all-to-all-start = ((bf16[16,16,512]{2,1,0:T(8,128)(2,1)}), bf16[16,16,512]{2,1,0:T(8,128)(2,1)S(1)}, u32[]{:S(2)}, u32[]{:S(2)}) async-start(bf16[16,16,512]{2,1,0:T(8,128)(2,1)} %broadcast_in_dim.8), calls=%async_computation | async-start | bytes 524288 | tf_op jit(solution)/shard_map/all_to_all | solution.py:329
  18.3 0.7 shard_map.85.own_ref
  19.5 9.1 %all-to-all-done.refs_8_ = bf16[16,16,512]{2,1,0:T(8,128)(2,1)S(1)} async-done(((bf16[16,16,512]{2,1,0:T(8,128)(2,1)}), bf16[16,16,512]{2,1,0:T(8,128)(2,1)S(1)}, u32[]{:S(2)}, u32[]{:S(2)}) %all-to-all-start) | async-done | bytes 262176 | tf_op jit(solution)/shard_map/all_to_all | solution.py:329
  28.7 0.6 collective-permute-start.4
  29.3 2.3 %shard_map.84 = (bf16[8,512,128]{2,1,0:T(8,128)(2,1)S(1)}, bf16[8,128,512]{2,1,0:T(8,128)(2,1)S(1)}, bf16[8,512,128]{2,1,0:T(8,128)(2,1)S(1)}, f32[8,512,128]{2,1,0:T(8,128)S(1)}, f32[8,128]{1,0:T(8,128)}) custom-call(s32[11]{0:T(128)S(1)} %stack.48.place, bf16[4,512,128]{2,1,0:T(8,128)(2,1)S(1)} %collective-permute-done.sib_ref, ...), custom_call_target="tpu_custom_call" | custom-call | flops 536870912 | bytes 6291456 | tf_op jit(solution)/shard_map/pallas_call | solution.py:383
  31.7 2.3 %shard_map.86 = (bf16[8,512,128]{2,1,0:T(8,128)(2,1)S(1)}, bf16[8,128,512]{2,1,0:T(8,128)(2,1)S(1)}, bf16[8,512,128]{2,1,0:T(8,128)(2,1)S(1)}, f32[8,512,128]{2,1,0:T(8,128)S(1)}, f32[8,128]{1,0:T(8,128)}) custom-call(s32[11]{0:T(128)S(1)} %stack.48.place, bf16[4,512,128]{2,1,0:T(8,128)(2,1)S(1)} %collective-permute-done.2.sib_ref, ...), custom_call_target="tpu_custom_call" | custom-call | flops 536870912 | bytes 6291456 | tf_op jit(solution)/shard_map/pallas_call | solution.py:383
  34.0 3.7 %shard_map.87 = (bf16[8,256,128]{2,1,0:T(8,128)(2,1)S(1)}, bf16[8,256,128]{2,1,0:T(8,128)(2,1)S(1)}) custom-call(s32[11]{0:T(128)S(1)} %stack.48.place, bf16[8,512,128]{2,1,0:T(8,128)(2,1)S(1)} %get-tuple-element.39.refs_0_, bf16[8,128,512]{2,1,0:T(8,128)(2,1)S(1)} %get-tuple-element.40.refs_1_, bf16[8,512,128]{2,1,0:T(8,128)(2,1)S(1)} %get-tuple-element.41.refs_2_, ...), custom_call_target="tpu_custom_call" | custom-call | flops 1073741824 | bytes 4194304 | tf_op jit(solution)/shard_map/pallas_call | solution.py:248
  37.7 3.7 %shard_map.88 = (bf16[8,256,128]{2,1,0:T(8,128)(2,1)S(1)}, bf16[8,256,128]{2,1,0:T(8,128)(2,1)S(1)}) custom-call(s32[11]{0:T(128)S(1)} %stack.48.place, bf16[8,512,128]{2,1,0:T(8,128)(2,1)S(1)} %get-tuple-element.39.refs_0_, bf16[8,128,512]{2,1,0:T(8,128)(2,1)S(1)} %get-tuple-element.40.refs_1_, ...), custom_call_target="tpu_custom_call", output_to_operand_aliasing={{0}: (10, {}), {1}: (11, {})} | custom-call | flops 1073741824 | bytes 4194304 | tf_op jit(solution)/shard_map/pallas_call | solution.py:248
  41.5 1.9 %collective-permute-done.5.got_ref = bf16[8,256,128]{2,1,0:T(8,128)(2,1)S(1)} collective-permute-done((bf16[8,256,128]{2,1,0:T(8,128)(2,1)S(1)}, bf16[8,256,128]{2,1,0:T(8,128)(2,1)S(1)}, u32[]{:S(2)}, u32[]{:S(2)}) %collective-permute-start.5) | collective-permute-done | bytes 524320 | tf_op jit(solution)/shard_map/ppermute | solution.py:320
  43.4 2.4 %shard_map.89 = (bf16[4,256,128]{2,1,0:T(8,128)(2,1)S(1)}, bf16[4,256,128]{2,1,0:T(8,128)(2,1)S(1)}, bf16[32,96,128]{2,1,0:T(8,128)(2,1)}) custom-call(s32[11]{0:T(128)S(1)} %stack.48.place, bf16[8,256,128]{2,1,0:T(8,128)(2,1)S(1)} %get-tuple-element.51.own_ref, bf16[8,256,128]{2,1,0:T(8,128)(2,1)S(1)} %collective-permute-done.5.got_ref, ...), custom_call_target="tpu_custom_call" | custom-call | flops 134217728 | bytes 3145728 | tf_op jit(solution)/shard_map/pallas_call | solution.py:410
  45.8 5.6 %all-to-all-start.1 = ((bf16[32,96,128]{2,1,0:T(8,128)(2,1)}), bf16[32,96,128]{2,1,0:T(8,128)(2,1)S(1)}, u32[]{:S(2)}, u32[]{:S(2)}) async-start(bf16[32,96,128]{2,1,0:T(8,128)(2,1)} %get-tuple-element.54), calls=%async_computation.1 | async-start | bytes 1572864 | tf_op jit(solution)/shard_map/all_to_all | solution.py:423
  51.5 1.2 collective-permute-start.6
  52.7 12.2 %collective-permute-done.6.got_ref = bf16[4,256,128]{2,1,0:T(8,128)(2,1)S(1)} collective-permute-done((bf16[4,256,128]{2,1,0:T(8,128)(2,1)S(1)}, bf16[4,256,128]{2,1,0:T(8,128)(2,1)S(1)}, u32[]{:S(2)}, u32[]{:S(2)}) %collective-permute-start.6) | collective-permute-done | bytes 262176 | tf_op jit(solution)/shard_map/ppermute | solution.py:263
  64.9 9.1 %all-to-all-done.1.own_in = bf16[32,96,128]{2,1,0:T(8,128)(2,1)S(1)} async-done(((bf16[32,96,128]{2,1,0:T(8,128)(2,1)}), bf16[32,96,128]{2,1,0:T(8,128)(2,1)S(1)}, u32[]{:S(2)}, u32[]{:S(2)}) %all-to-all-start.1) | async-done | bytes 786464 | tf_op jit(solution)/shard_map/all_to_all | solution.py:423
  74.0 2.3 %collective-permute-done.7.sib_in = bf16[32,96,128]{2,1,0:T(8,128)(2,1)S(1)} collective-permute-done((bf16[32,96,128]{2,1,0:T(8,128)(2,1)S(1)}, bf16[32,96,128]{2,1,0:T(8,128)(2,1)S(1)}, u32[]{:S(2)}, u32[]{:S(2)}) %collective-permute-start.7) | collective-permute-done | bytes 786464 | tf_op jit(solution)/shard_map/ppermute | solution.py:320
  76.3 0.8 shard_map.91.refs_4_
  77.3 1.0 collective-permute-start.9
  78.3 3.6 %collective-permute-start.8 = (bf16[2,128,512]{2,1,0:T(8,128)(2,1)S(1)}, bf16[2,128,512]{2,1,0:T(8,128)(2,1)S(1)}, u32[]{:S(2)}, u32[]{:S(2)}) collective-permute-start(bf16[2,128,512]{2,1,0:T(8,128)(2,1)S(1)} %shard_map.91.refs_4_), channel_id=1, source_target_pairs={{0,8},{4,12},{8,0},{12,4},{1,9},{5,13},{9,1},{13,5},{2,10},{6,14},... | collective-permute-start | bytes 786440 | tf_op jit(solution)/shard_map/ppermute | solution.py:263
  81.9 3.3 %shard_map.90 = (bf16[8,512,128]{2,1,0:T(8,128)(2,1)S(1)}, bf16[8,128,512]{2,1,0:T(8,128)(2,1)S(1)}, bf16[8,512,128]{2,1,0:T(8,128)(2,1)S(1)}, f32[8,512,128]{2,1,0:T(8,128)S(1)}) custom-call(s32[11]{0:T(128)S(1)} %stack.48.place, bf16[32,96,128]{2,1,0:T(8,128)(2,1)S(1)} %all-to-all-done.1.own_in, bf16[32,96,128]{2,1,0:T(8,128)(2,1)S(1)} %collective-permute-done.7.sib_in, ...), custom_call_target="tpu_custom_call" | custom-call | flops 536870912 | bytes 6291456 | tf_op jit(solution)/shard_map/pallas_call | solution.py:436
  85.2 2.4 %shard_map.92 = (bf16[64,4,8,128]{3,2,1,0:T(8,128)(2,1)S(1)}, bf16[64,4,8,128]{3,2,1,0:T(8,128)(2,1)S(1)}) custom-call(s32[11]{0:T(128)S(1)} %stack.48.place, bf16[8,512,128]{2,1,0:T(8,128)(2,1)S(1)} %get-tuple-element.59.refs_0_, bf16[8,128,512]{2,1,0:T(8,128)(2,1)S(1)} %get-tuple-element.60.refs_1_, bf16[8,512,128]{2,1,0:T(8,128)(2,1)S(1)} %get-tuple-element.61.refs_2_, ...), custom_call_target="tpu_custom_call" | custom-call | flops 536870912 | bytes 4194304 | tf_op jit(solution)/shard_map/pallas_call | solution.py:248
  87.6 4.2 %shard_map.93 = (bf16[64,4,8,128]{3,2,1,0:T(8,128)(2,1)S(1)}, bf16[64,4,8,128]{3,2,1,0:T(8,128)(2,1)S(1)}) custom-call(s32[11]{0:T(128)S(1)} %stack.48.place, bf16[8,512,128]{2,1,0:T(8,128)(2,1)S(1)} %get-tuple-element.59.refs_0_, bf16[8,128,512]{2,1,0:T(8,128)(2,1)S(1)} %get-tuple-element.60.refs_1_, ...), custom_call_target="tpu_custom_call", output_to_operand_aliasing={{0}: (7, {}), {1}: (8, {})} | custom-call | flops 1073741824 | bytes 4194304 | tf_op jit(solution)/shard_map/pallas_call | solution.py:248
  91.9 1.7 %collective-permute-done.8.refs_4_ = bf16[2,128,512]{2,1,0:T(8,128)(2,1)S(1)} collective-permute-done((bf16[2,128,512]{2,1,0:T(8,128)(2,1)S(1)}, bf16[2,128,512]{2,1,0:T(8,128)(2,1)S(1)}, u32[]{:S(2)}, u32[]{:S(2)}) %collective-permute-start.8) | collective-permute-done | bytes 262176 | tf_op jit(solution)/shard_map/ppermute | solution.py:263
  93.6 2.4 %shard_map.94 = (bf16[64,4,8,128]{3,2,1,0:T(8,128)(2,1)S(1)}, bf16[64,4,8,128]{3,2,1,0:T(8,128)(2,1)S(1)}) custom-call(s32[11]{0:T(128)S(1)} %stack.48.place, bf16[8,512,128]{2,1,0:T(8,128)(2,1)S(1)} %get-tuple-element.59.refs_0_, bf16[8,128,512]{2,1,0:T(8,128)(2,1)S(1)} %get-tuple-element.60.refs_1_, ...), custom_call_target="tpu_custom_call", output_to_operand_aliasing={{0}: (6, {}), {1}: (7, {})} | custom-call | flops 536870912 | bytes 4194304 | tf_op jit(solution)/shard_map/pallas_call | solution.py:248
  96.1 1.9 %collective-permute-done.11.got_ref = bf16[64,4,8,128]{3,2,1,0:T(8,128)(2,1)S(1)} collective-permute-done((bf16[64,4,8,128]{3,2,1,0:T(8,128)(2,1)S(1)}, bf16[64,4,8,128]{3,2,1,0:T(8,128)(2,1)S(1)}, u32[]{:S(2)}, u32[]{:S(2)}) %collective-permute-start.11) | collective-permute-done | bytes 524320 | tf_op jit(solution)/shard_map/ppermute | solution.py:320
  98.3 23.9 %all_to_all.15.back_ref = bf16[64,4,8,128]{3,2,1,0:T(8,128)(2,1)S(1)} all-to-all(bf16[64,4,8,128]{3,2,1,0:T(8,128)(2,1)S(1)} %shard_map.95), channel_id=1, replica_groups=mesh['y'=2,'z'=8,'xh'=2,'xl'=2,'c'=2,'dp'=2] {'xh','xl','y','z'}, dimensions={0} | all-to-all | bytes 1048576 | tf_op jit(solution)/shard_map/all_to_all | solution.py:453
  122.3 1.5 %shard_map.96 = bf16[4,512,128]{2,1,0:T(8,128)(2,1)} custom-call(s32[11]{0:T(128)S(1)} %stack.48.place, bf16[4,256,128]{2,1,0:T(8,128)(2,1)S(1)} %get-tuple-element.53.near_ref, bf16[4,256,128]{2,1,0:T(8,128)(2,1)S(1)} %collective-permute-done.6.got_ref, bf16[64,4,8,128]{3,2,1,0:T(8,128)(2,1)S(1)} %all_to_all.15.back_ref), custom_call_target="tpu_custom_call" | custom-call | tf_op jit(solution)/shard_map/pallas_call | solution.py:454
  (38 shorter events, 1.7 us)
Async XLA Ops:
  0.0 29.3 %copy-start.3 = (bf16[2,128,128]{2,1,0:T(8,128)(2,1)S(1)}, bf16[2,128,128]{2,1,0:T(8,128)(2,1)}, u32[]{:S(2)}) copy-start(bf16[2,128,128]{2,1,0:T(8,128)(2,1)} %wq.1) | copy-start | bytes 196612
  0.0 18.3 %collective-permute-start.1 = (bf16[4,512,128]{2,1,0:T(8,128)(2,1)}, bf16[4,512,128]{2,1,0:T(8,128)(2,1)S(1)}, u32[]{:S(2)}, u32[]{:S(2)}) collective-permute-start(bf16[4,512,128]{2,1,0:T(8,128)(2,1)} %pair_ref.3), channel_id=1, source_target_pairs={{0,8},{4,12},{8,0},{12,4},{1,9},{5,13},{9,1},{13,5},{2,10},{6,14},... | collective-permute-start | bytes 1572872 | tf_op jit(solution)/shard_map/ppermute | solution.py:263
  3.8 1.0 copy-start
  4.8 0.7 copy-start.7
  5.5 23.8 %copy-start.4 = (bf16[2,128,128]{2,1,0:T(8,128)(2,1)S(1)}, bf16[2,128,128]{2,1,0:T(8,128)(2,1)}, u32[]{:S(2)}) copy-start(bf16[2,128,128]{2,1,0:T(8,128)(2,1)} %wk.1) | copy-start | bytes 196612
  5.5 23.8 %copy-start.5 = (bf16[2,128,128]{2,1,0:T(8,128)(2,1)S(1)}, bf16[2,128,128]{2,1,0:T(8,128)(2,1)}, u32[]{:S(2)}) copy-start(bf16[2,128,128]{2,1,0:T(8,128)(2,1)} %wv.1) | copy-start | bytes 196612
  5.5 23.8 %copy-start.6 = (bf16[2,128,128]{2,1,0:T(8,128)(2,1)S(1)}, bf16[2,128,128]{2,1,0:T(8,128)(2,1)}, u32[]{:S(2)}) copy-start(bf16[2,128,128]{2,1,0:T(8,128)(2,1)} %wg.1) | copy-start | bytes 196612
  6.8 1.3 %collective-permute-start.3 = (bf16[8,512]{1,0:T(8,128)(2,1)S(1)}, bf16[8,512]{1,0:T(8,128)(2,1)S(1)}, u32[]{:S(2)}, u32[]{:S(2)}) collective-permute-start(bf16[8,512]{1,0:T(8,128)(2,1)S(1)} %get-tuple-element.48), channel_id=1, source_target_pairs={{0,2},{2,0},{1,3},{3,1},{4,6},{6,4},{5,7},{7,5},{8,10},{10,8},{9,1... | collective-permute-start | bytes 24584 | tf_op jit(solution)/shard_map/ppermute | solution.py:320
  8.9 19.8 %all-to-all-start = ((bf16[16,16,512]{2,1,0:T(8,128)(2,1)}), bf16[16,16,512]{2,1,0:T(8,128)(2,1)S(1)}, u32[]{:S(2)}, u32[]{:S(2)}) async-start(bf16[16,16,512]{2,1,0:T(8,128)(2,1)} %broadcast_in_dim.8), calls=%async_computation | async-start | bytes 524288 | tf_op jit(solution)/shard_map/all_to_all | solution.py:329
  18.2 11.1 %collective-permute-start = (bf16[4,512,128]{2,1,0:T(8,128)(2,1)S(1)}, bf16[4,512,128]{2,1,0:T(8,128)(2,1)S(1)}, u32[]{:S(2)}, u32[]{:S(2)}) collective-permute-start(bf16[4,512,128]{2,1,0:T(8,128)(2,1)S(1)} %get-tuple-element.37.own_ref), channel_id=1, source_target_pairs={{0,2},{2,0},{1,3},{3,1},{4,6},{6,4},{5,7},{7,5},{8,10},{10,8},{9,1... | collective-permute-start | bytes 1572872 | tf_op jit(solution)/shard_map/ppermute | solution.py:320
  19.0 12.7 %collective-permute-start.2 = (bf16[4,512,128]{2,1,0:T(8,128)(2,1)S(1)}, bf16[4,512,128]{2,1,0:T(8,128)(2,1)S(1)}, u32[]{:S(2)}, u32[]{:S(2)}) collective-permute-start(bf16[4,512,128]{2,1,0:T(8,128)(2,1)S(1)} %shard_map.85.own_ref), channel_id=1, source_target_pairs={{0,2},{2,0},{1,3},{3,1},{4,6},{6,4},{5,7},{7,5},{8,10},{10,8},{9,1... | collective-permute-start | bytes 1572872 | tf_op jit(solution)/shard_map/ppermute | solution.py:320
  28.7 9.0 %collective-permute-start.4 = (bf16[16,16,512]{2,1,0:T(8,128)(2,1)S(1)}, bf16[16,16,512]{2,1,0:T(8,128)(2,1)S(1)}, u32[]{:S(2)}, u32[]{:S(2)}) collective-permute-start(bf16[16,16,512]{2,1,0:T(8,128)(2,1)S(1)} %all-to-all-done.refs_8_), channel_id=1, source_target_pairs={{0,4},{4,0},{8,12},{12,8},{1,5},{5,1},{9,13},{13,9},{2,6},{6,2},{1... | collective-permute-start | bytes 786440 | tf_op jit(solution)/shard_map/ppermute | solution.py:263
  37.7 5.7 %copy-start.1 = (bf16[4,512,128]{2,1,0:T(8,128)(2,1)S(1)}, bf16[4,512,128]{2,1,0:T(8,128)(2,1)}, u32[]{:S(2)}) copy-start(bf16[4,512,128]{2,1,0:T(8,128)(2,1)} %pair_ref.3) | copy-start | bytes 1572868
  37.7 5.7 %copy-start.2 = (bf16[2,128,128]{2,1,0:T(8,128)(2,1)S(1)}, bf16[2,128,128]{2,1,0:T(8,128)(2,1)}, u32[]{:S(2)}) copy-start(bf16[2,128,128]{2,1,0:T(8,128)(2,1)} %w_ref.3) | copy-start | bytes 196612
  37.7 5.7 %copy-start.8 = (bf16[2,128,4]{1,2,0:T(4,128)(2,1)S(1)}, bf16[2,128,4]{1,2,0:T(4,128)(2,1)}, u32[]{:S(2)}) copy-start(bf16[2,128,4]{1,2,0:T(4,128)(2,1)} %param.14) | copy-start | bytes 6148
  41.4 2.0 %collective-permute-start.5 = (bf16[8,256,128]{2,1,0:T(8,128)(2,1)S(1)}, bf16[8,256,128]{2,1,0:T(8,128)(2,1)S(1)}, u32[]{:S(2)}, u32[]{:S(2)}) collective-permute-start(bf16[8,256,128]{2,1,0:T(8,128)(2,1)S(1)} %get-tuple-element.52), channel_id=1, source_target_pairs={{0,2},{2,0},{1,3},{3,1},{4,6},{6,4},{5,7},{7,5},{8,10},{10,8},{9,1... | collective-permute-start | bytes 1572872 | tf_op jit(solution)/shard_map/ppermute | solution.py:320
  45.8 28.2 %all-to-all-start.1 = ((bf16[32,96,128]{2,1,0:T(8,128)(2,1)}), bf16[32,96,128]{2,1,0:T(8,128)(2,1)S(1)}, u32[]{:S(2)}, u32[]{:S(2)}) async-start(bf16[32,96,128]{2,1,0:T(8,128)(2,1)} %get-tuple-element.54), calls=%async_computation.1 | async-start | bytes 1572864 | tf_op jit(solution)/shard_map/all_to_all | solution.py:423
  51.5 13.5 %collective-permute-start.6 = (bf16[4,256,128]{2,1,0:T(8,128)(2,1)S(1)}, bf16[4,256,128]{2,1,0:T(8,128)(2,1)S(1)}, u32[]{:S(2)}, u32[]{:S(2)}) collective-permute-start(bf16[4,256,128]{2,1,0:T(8,128)(2,1)S(1)} %get-tuple-element.55), channel_id=1, source_target_pairs={{0,8},{4,12},{8,0},{12,4},{1,9},{5,13},{9,1},{13,5},{2,10},{6,14},... | collective-permute-start | bytes 786440 | tf_op jit(solution)/shard_map/ppermute | solution.py:263
  74.0 2.3 %collective-permute-start.7 = (bf16[32,96,128]{2,1,0:T(8,128)(2,1)S(1)}, bf16[32,96,128]{2,1,0:T(8,128)(2,1)S(1)}, u32[]{:S(2)}, u32[]{:S(2)}) collective-permute-start(bf16[32,96,128]{2,1,0:T(8,128)(2,1)S(1)} %all-to-all-done.1.own_in), channel_id=1, source_target_pairs={{0,2},{2,0},{1,3},{3,1},{4,6},{6,4},{5,7},{7,5},{8,10},{10,8},{9,1... | collective-permute-start | bytes 2359304 | tf_op jit(solution)/shard_map/ppermute | solution.py:320
  77.1 10.5 %collective-permute-start.10 = (bf16[2,128,512]{2,1,0:T(8,128)(2,1)S(1)}, bf16[2,128,512]{2,1,0:T(8,128)(2,1)S(1)}, u32[]{:S(2)}, u32[]{:S(2)}) collective-permute-start(bf16[2,128,512]{2,1,0:T(8,128)(2,1)S(1)} %shard_map.91.refs_4_), channel_id=1, source_target_pairs={{0,12},{4,8},{8,4},{12,0},{1,13},{5,9},{9,5},{13,1},{2,14},{6,10},... | collective-permute-start | bytes 786440 | tf_op jit(solution)/shard_map/ppermute | solution.py:263
  77.3 10.3 %collective-permute-start.9 = (bf16[2,128,512]{2,1,0:T(8,128)(2,1)S(1)}, bf16[2,128,512]{2,1,0:T(8,128)(2,1)S(1)}, u32[]{:S(2)}, u32[]{:S(2)}) collective-permute-start(bf16[2,128,512]{2,1,0:T(8,128)(2,1)S(1)} %shard_map.91.refs_4_), channel_id=1, source_target_pairs={{0,4},{4,0},{8,12},{12,8},{1,5},{5,1},{9,13},{13,9},{2,6},{6,2},{1... | collective-permute-start | bytes 786440 | tf_op jit(solution)/shard_map/ppermute | solution.py:263
  78.3 15.3 %collective-permute-start.8 = (bf16[2,128,512]{2,1,0:T(8,128)(2,1)S(1)}, bf16[2,128,512]{2,1,0:T(8,128)(2,1)S(1)}, u32[]{:S(2)}, u32[]{:S(2)}) collective-permute-start(bf16[2,128,512]{2,1,0:T(8,128)(2,1)S(1)} %shard_map.91.refs_4_), channel_id=1, source_target_pairs={{0,8},{4,12},{8,0},{12,4},{1,9},{5,13},{9,1},{13,5},{2,10},{6,14},... | collective-permute-start | bytes 786440 | tf_op jit(solution)/shard_map/ppermute | solution.py:263
  96.0 2.0 %collective-permute-start.11 = (bf16[64,4,8,128]{3,2,1,0:T(8,128)(2,1)S(1)}, bf16[64,4,8,128]{3,2,1,0:T(8,128)(2,1)S(1)}, u32[]{:S(2)}, u32[]{:S(2)}) collective-permute-start(bf16[64,4,8,128]{3,2,1,0:T(8,128)(2,1)S(1)} %get-tuple-element.68), channel_id=1, source_target_pairs={{0,2},{2,0},{1,3},{3,1},{4,6},{6,4},{5,7},{7,5},{8,10},{10,8},{9,1... | collective-permute-start | bytes 1572872 | tf_op jit(solution)/shard_map/ppermute | solution.py:320

commit v5 on v4

--- a/solution.py
+++ b/solution.py
@@ -85,28 +85,33 @@
         normed_ref[r] = layer_normed(wide).astype(jnp.bfloat16)
 
 
-def project(core, normed, weights):
+def project(core, normed, asking, weights):
     tokens, channels = normed.shape
-    projected = jnp.dot(normed, weights, preferred_element_type=jnp.float32)
-    query = (projected[:, :channels] * (1.0 / math.sqrt(HEAD_DIM))).astype(jnp.bfloat16)
-    key_t = projected[:, channels : 2 * channels].astype(jnp.bfloat16).T
+    kept, asked = weights[:, : 2 * channels], weights[:, 2 * channels :]
+    held = jnp.dot(normed, kept, preferred_element_type=jnp.float32)
+    asked = jnp.dot(asking, asked, preferred_element_type=jnp.float32)
+    query = (asked[:, :channels] * (1.0 / math.sqrt(HEAD_DIM))).astype(jnp.bfloat16)
+    gate = jax.nn.sigmoid(asked[:, channels:])
+    key_t = held[:, :channels].astype(jnp.bfloat16).T
     half = lax.broadcasted_iota(jnp.int32, (tokens, channels), 1) // (2 * HEAD_DIM)
-    value = jnp.where(half == core, projected[:, 2 * channels : 3 * channels], 1.0)
-    gate = jax.nn.sigmoid(projected[:, 3 * channels :])
+    value = jnp.where(half == core, held[:, channels:], 1.0)
     return query, key_t, value.astype(jnp.bfloat16), gate
 
 
 def pack_weights(wq, wk, wv, wg, first_ref, next_ref):
     for step, ref in enumerate((first_ref, next_ref)):
-        ref[...] = jnp.concatenate([w[step] for w in (wq, wk, wv, wg)], axis=1)
-
-
-def project_rows(place, sib_ref, own_ref, w_ref, query_ref, key_ref, value_ref, gate_ref, done_ref):
-    done_ref[...] = jnp.zeros_like(done_ref)
-    for r in range(ROWS):
-        normed = sib_ref[r] if r < ROWS // 2 else own_ref[r - ROWS // 2]
-        query, key_t, value, gate = project(place[CORE], normed, w_ref[...])
-        query_ref[r], key_ref[r], value_ref[r], gate_ref[r] = query, key_t, value, gate
+        ref[...] = jnp.concatenate([w[step] for w in (wk, wv, wq, wg)], axis=1)
+
+
+def project_rows(place, *refs):
+    groups, (w_ref, query_ref, key_ref, value_ref, gate_ref) = refs[:-5], refs[-5:]
+    asking = pl.ds(pl.multiple_of(place[UPPER] * HALF, HALF), HALF)
+    for g, ref in enumerate(groups):
+        count = ref.shape[0]
+        for r in range(count):
+            out = project(place[CORE], ref[r], ref[r, asking, :], w_ref[...])
+            at = g * count + r
+            query_ref[at], key_ref[at], value_ref[at], gate_ref[at] = out
 
 
 def received_quarters(place):
@@ -116,7 +121,7 @@
     ]
 
 
-def project_columns(place, own_in, sib_in, w_ref, query_ref, key_ref, value_ref, gate_ref, cols_ref):
+def project_columns(place, own_in, sib_in, w_ref, near_ref, got_ref, query_ref, key_ref, value_ref, gate_ref, one_ref, cols_ref):
     core = place[CORE]
     _, _, _, count, width, channels = cols_ref.shape
     for ref, at in ((own_in, core), (sib_in, 1 - core)):
@@ -127,8 +132,13 @@
     flat = cols_ref.reshape(X * YZ * 2 * count, width, channels)
     for j in range(width):
         normed = flat[:, j, :].astype(jnp.bfloat16)
-        query, key_t, value, gate = project(core, normed, w_ref[...])
-        query_ref[j], key_ref[j], value_ref[j], gate_ref[j] = query, key_t, value, gate
+        out = project(core, normed, normed, w_ref[...])
+        query_ref[j], key_ref[j], value_ref[j], gate_ref[j] = out
+    lower = place[UPPER] == 0
+    for r in range(count):
+        near, got = near_ref[r].astype(jnp.float32), got_ref[r].astype(jnp.float32)
+        one = jnp.concatenate([jnp.where(lower, near, got), jnp.where(lower, got, near)], axis=0)
+        one_ref[r] = outer_order(one).astype(jnp.bfloat16)
 
 
 def turn_bias(place, own_in, sib_in, out_ref, keyed_ref):
@@ -186,71 +196,76 @@
     finish(*pending)
 
 
-def attend_quarters(steps, columns, place, *refs):
+def attend_quarters(steps, columns, parts, place, *refs):
     core = place[CORE]
-    groups = 1 if columns else 2
-    pieces = refs[4 * groups : 4 * groups + len(steps)]
-    sib_ref, own_ref, wide_ref = refs[-4:-1] if columns else refs[-3:]
-    out_ref = refs[-1]
+    query_ref, key_ref, value_ref, gate_ref = refs[:4]
+    pieces = refs[4 : 4 + len(steps)]
+    wide_ref, columns_ref = (refs[-2], refs[-1]) if columns else (refs[-1], None)
+    outs = refs[-2 - len(parts) : -2] if columns else refs[-1 - len(parts) : -1]
+    half = ROWS // 2
     units = []
     for i, (s, piece_ref) in enumerate(zip(steps, pieces)):
         wide = piece_ref[...].astype(jnp.float32)
         for h in range(2):
             rows = wide[h] if columns else wide[:, h * ROWS : (h + 1) * ROWS]
             wide_ref[i, h] = rows.reshape(wide_ref.shape[2:])
-        span = pl.ds(pl.multiple_of(place[SPOT + s] * QUARTER, QUARTER), QUARTER)
-        for g in range(groups):
-            query_ref, key_ref, value_ref, gate_ref = refs[4 * g : 4 * g + 4]
-            for r in range(ROWS):
-
-                def put(value, i=i, g=g, r=r, s=s):
-                    if columns:
-                        out_ref.reshape(len(steps), QUARTER, ROWS, -1)[i, :, r, :] = value
-                        return
-                    local = pl.ds(pl.multiple_of(place[LOCAL + s] * QUARTER, QUARTER), QUARTER)
-                    half = ROWS // 2
-                    ref = sib_ref if r < half else own_ref
-                    ref[g * half + r % half, local, :] = value.astype(jnp.bfloat16)
-
-                units.append(
-                    (
-                        lambda ref=query_ref, r=r, span=span: ref[r, span, :],
-                        lambda ref=key_ref, r=r: ref[r],
-                        lambda i=i: wide_ref[i],
-                        lambda ref=value_ref, r=r: ref[r],
-                        lambda ref=gate_ref, r=r, span=span: ref[r, span, :],
-                        put,
-                    )
-                )
-    attend(core, units, QUARTER, sib_ref.shape[-1])
+        spot = place[(SPOT if columns else LOCAL) + s]
+        span = pl.ds(pl.multiple_of(spot * QUARTER, QUARTER), QUARTER)
+
+        def unit(row, put, i=i, span=span):
+            return (
+                lambda: query_ref[row, span, :],
+                lambda: key_ref[row],
+                lambda: wide_ref[i],
+                lambda: value_ref[row],
+                lambda: gate_ref[row, span, :],
+                put,
+            )
+
+        if columns:
+            for j in range(ROWS):
+
+                def put(value, i=i, j=j):
+                    columns_ref.reshape(len(steps), QUARTER, ROWS, -1)[i, :, j, :] = value
+
+                units.append(unit(j, put))
+        else:
+            for part, ref in zip(parts, outs):
+                for g in range(2):
+                    for r in range(half):
+
+                        def put(value, ref=ref, at=g * half + r, span=span):
+                            ref[at, span, :] = value.astype(jnp.bfloat16)
+
+                        units.append(unit(g * ROWS + part * half + r, put))
+    attend(core, units, QUARTER, outs[0].shape[-1])
     if columns:
         for i, s in enumerate(steps):
             chips = pl.ds(place[SPOT + s] * YZ, YZ)
-            for ref, at in ((own_ref, core), (sib_ref, 1 - core)):
-                ref[chips] = out_ref[i, :, pl.ds(at, 1)][:, 0].astype(jnp.bfloat16)
-
-
-def attend_some(steps, columns, place, projected, pieces, outs):
-    rows, tokens, channels = projected[0].shape
-    count = rows // 2
+            for ref, at in zip(outs, (1 - core, core)):
+                ref[chips] = columns_ref[i, :, pl.ds(at, 1)][:, 0].astype(jnp.bfloat16)
+
+
+def attend_some(steps, columns, parts, place, projected, pieces, outs):
+    rows, channels, tokens = projected[1].shape
     scratch = [pltpu.VMEM((len(steps), 2, QUARTER, tokens), jnp.float32)]
     if columns:
-        shape = struct((X * YZ, count, rows, channels))
-        scratch.append(pltpu.VMEM((len(steps), YZ, 2, count, rows, channels), jnp.float32))
+        shape = struct((X * YZ, rows // 2, rows, channels))
+        scratch.append(pltpu.VMEM((len(steps), YZ, 2, rows // 2, rows, channels), jnp.float32))
     else:
-        shape = struct((rows, HALF, channels))
+        shape = struct((rows // 2, HALF, channels))
     operands = [place, *projected, *pieces]
     aliases = {}
     if outs is not None:
-        aliases = {len(operands) + i: i for i in range(2)}
+        aliases = {len(operands) + i: i for i in range(len(parts))}
         operands += list(outs)
-    units = len(steps) * rows * 2 * len(projected) // 4
+    units = len(steps) * rows * len(parts)
     return pl.pallas_call(
-        functools.partial(attend_quarters, steps, columns),
+        functools.partial(attend_quarters, steps, columns, parts),
         in_specs=[SMEM] + [VMEM] * (len(operands) - 1),
-        out_specs=[VMEM, VMEM],
+        out_specs=[VMEM] * len(parts),
         scratch_shapes=scratch,
-        out_shape=[shape, shape],
+        out_shape=[shape] * len(parts),
         input_output_aliases=aliases,
         compiler_params=params(16),
         cost_estimate=cost(
@@ -263,13 +278,23 @@
     return lax.ppermute(array, X_AXES, [(i, i ^ s) for i in range(X)])
 
 
-def attend_all(columns, place, projected, piece):
-    steps = [(0,), (1, 3), (2,)] if columns else [(0,), (1,)]
-    moved = {s: along_x(piece, s) for some in steps[1:] for s in some}
-    outs = attend_some(steps[0], columns, place, projected, [piece], None)
-    for some in steps[1:]:
-        outs = attend_some(some, columns, place, projected, [moved[s] for s in some], outs)
-    return outs
+def attend_rows(place, projected, piece):
+    moved = along_x(piece, 1)
+    for_sib, own = attend_some((0,), False, (0, 1), place, projected, [piece], None)
+    (for_sib,) = attend_some((1,), False, (0,), place, projected, [moved], [for_sib])
+    got = swap(for_sib)
+    (own,) = attend_some((1,), False, (1,), place, projected, [moved], [own])
+    return got, own
+
+
+def attend_columns(place, projected, piece):
+    moved = {s: along_x(piece, s) for s in (1, 3, 2)}
+    outs = None
+    for steps in ((0,), (1, 3), (2,)):
+        pieces = [moved[s] if s else piece for s in steps]
+        outs = attend_some(steps, True, (0, 1), place, projected, pieces, outs)
+    for_sib, own = outs
+    return swap(for_sib), own
 
 
 def finish_rows(place, own_ref, got_ref, pair_ref, far_ref, w_ref, wb_ref, near_ref, other_ref, sent_ref, rows_ref, wide_ref):
@@ -306,14 +331,12 @@
     out_ref[...] = branch.reshape(chips, rows, width, channels).astype(jnp.bfloat16)
 
 
-def add_back(place, near_ref, got_ref, back_ref, out_ref):
+def add_back(one_ref, back_ref, out_ref):
     chips, count, width, channels = back_ref.shape
-    lower = place[UPPER] == 0
     for r in range(count):
         back = back_ref[:, r].astype(jnp.float32).reshape(chips * width, channels)
-        near, got = near_ref[r].astype(jnp.float32), got_ref[r].astype(jnp.float32)
-        one = jnp.concatenate([jnp.where(lower, near, got), jnp.where(lower, got, near)], axis=0)
-        out_ref[r] = outer_order(one + back).astype(jnp.bfloat16)
+        total = one_ref[r].astype(jnp.float32) + outer_order(back)
+        out_ref[r] = total.astype(jnp.bfloat16)
 
 
 def swap(array):
@@ -353,12 +376,14 @@
     held = (count, tokens, channels)
     half = struct((ROWS, tokens))
     bias_scratch = pltpu.VMEM((4 * count, tokens), jnp.float32)
-    projections = [
-        struct(rows),
-        struct((ROWS, channels, tokens)),
-        struct(rows),
-        struct(rows, jnp.float32),
-    ]
+
+    def projections(number, asking):
+        return [
+            struct((number, asking, channels)),
+            struct((number, channels, tokens)),
+            struct((number, tokens, channels)),
+            struct((number, asking, channels), jnp.float32),
+        ]
 
     far = along_x(pair, 2)
     normed, mine, other = pl.pallas_call(
@@ -379,19 +404,6 @@
         out_shape=[packed, packed],
         compiler_params=params(),
     )(*weights)
-    def project_group(array):
-        *projected, done = pl.pallas_call(
-            project_rows,
-            in_specs=[SMEM, VMEM, VMEM, VMEM],
-            out_specs=[VMEM] * 5,
-            out_shape=projections + [struct((8, 128), jnp.float32)],
-            compiler_params=params(),
-            cost_estimate=cost(8 * ROWS * tokens * channels * channels, 6 << 20),
-        )(place, swap(array), array, first_weights)
-        return projected, done
-
-    projected, done = project_group(normed)
-    far, done = lax.optimization_barrier((far, done))
     normed_far = pl.pallas_call(
         prepare_far,
         in_specs=[VMEM],
@@ -400,10 +412,15 @@
         compiler_params=params(),
         cost_estimate=cost(1 << 24, 1 << 20),
     )(far)
-    projected_far, done = project_group(normed_far)
-    gathered, done = lax.optimization_barrier((gathered, done))
-    projected = projected + projected_far
-    for_sib, own = attend_all(False, place, projected, gathered)
+    projected = pl.pallas_call(
+        project_rows,
+        in_specs=[SMEM] + [VMEM] * 5,
+        out_specs=[VMEM] * 4,
+        out_shape=projections(2 * ROWS, HALF),
+        compiler_params=params(),
+        cost_estimate=cost(12 * ROWS * tokens * channels * channels, 12 << 20),
+    )(place, swap(normed), normed, swap(normed_far), normed_far, first_weights)
+    got, own = attend_rows(place, projected, gathered)
     peers = X // 2 * YZ
     message = (peers, 2 * count * ROWS + 8 * count, channels)
     half_rows = struct((count, HALF, channels))
@@ -418,7 +435,7 @@
         ],
         compiler_params=params(),
         cost_estimate=cost(1 << 27, 3 << 20),
-    )(place, own, swap(for_sib), pair, far, w_out, wb)
+    )(place, own, got, pair, far, w_out, wb)
 
     got = lax.all_to_all(sent, ("xl", "y", "z"), 0, 0)
     got_near = along_x(other, 2)
@@ -433,31 +450,31 @@
         compiler_params=params(),
         cost_estimate=cost(1 << 20, 3 << 20),
     )(place, got, got_sib)
-    projected = pl.pallas_call(
+    *projected, one = pl.pallas_call(
         project_columns,
-        in_specs=[SMEM] + [VMEM] * 3,
-        out_specs=[VMEM] * 4,
-        out_shape=projections,
+        in_specs=[SMEM] + [VMEM] * 5,
+        out_specs=[VMEM] * 5,
+        out_shape=projections(ROWS, tokens) + [struct(held)],
         scratch_shapes=[pltpu.VMEM((X, YZ, 2, count, ROWS, channels), jnp.float32)],
         compiler_params=params(),
         cost_estimate=cost(8 * ROWS * tokens * channels * channels, 6 << 20),
-    )(place, got, got_sib, next_weights)
-    for_sib, own = attend_all(True, place, projected, quarter)
+    )(place, got, got_sib, next_weights, near, got_near)
+    got, own = attend_columns(place, projected, quarter)
     branch = pl.pallas_call(
         finish_columns,
         in_specs=[VMEM] * 3,
         out_specs=VMEM,
         out_shape=struct(piece),
         compiler_params=params(),
-    )(own, swap(for_sib), w_out)
+    )(own, got, w_out)
     back = lax.all_to_all(branch, X_AXES + ("y", "z"), 0, 0)
     return pl.pallas_call(
         add_back,
-        in_specs=[SMEM, VMEM, VMEM, VMEM],
+        in_specs=[VMEM, VMEM],
         out_specs=VMEM,
         out_shape=struct(held),
         compiler_params=params(),
-    )(place, near, got_near, back)
+    )(one, back)
 
 
 def solution(mesh):

time: 124 us -> 121 us (0.976)
  waiting for transfers between devices: 39.4 us -> 36.7 us
  Pallas kernels: 31.3 us -> 29.3 us
  starting transfers between devices: 25.5 us -> 26.8 us
    pallas_call x9, Pallas kernels: 25.8 us -> 23.7 us  [the longest x6 17.1 us: attend_some(): pl.pallas_call(functools.partial(attend_quarters, steps, columns, parts),...]
    ppermute x6, waiting for transfers between devices: 7.24 us -> 5.34 us  [swap(): return lax.ppermute(array, 'c', [(0, 1), (1, 0)])]
  transfers between devices with their start and end apart: 14 -> 14, of which waited for: 8 -> 7; matrix products, arithmetic and copies ran while one was open for 1% -> 1% of each run, Pallas kernels for 16% -> 17%
where the time goes in v5:
time: 121 us
  waiting for transfers between devices  36.7 us (30%)
  Pallas kernels  29.3 us (24%)
  starting transfers between devices  26.8 us (22%)
  blocking collectives  24.7 us (20%)
  local copies, waits for them, and re-layouts  2.62 us (2%)
    all_to_all x1, blocking collectives, shards(): back = lax.all_to_all(branch, X_AXES + ('y', 'z'), 0, 0)  24.7 us
    pallas_call x6, Pallas kernels, attend_some(): pl.pallas_call(functools.partial(attend_quarters, steps, columns, parts),...  17.1 us
    ppermute x6, waiting for transfers between devices, along_x(): return lax.ppermute(array, X_AXES, [(i, i ^ s) for i in range(X)])  13 us
    ppermute x6, starting transfers between devices, along_x(): return lax.ppermute(array, X_AXES, [(i, i ^ s) for i in range(X)])  10.5 us
    all_to_all x1, starting transfers between devices, spread_bias(): lax.all_to_all(jnp.broadcast_to(bias[None], (YZ,) + bias.shape), ('y', 'z...  9.29 us
    all_to_all x1, waiting for transfers between devices, shards(): got = lax.all_to_all(sent, ('xl', 'y', 'z'), 0, 0)  9.25 us
    all_to_all x1, waiting for transfers between devices, spread_bias(): lax.all_to_all(jnp.broadcast_to(bias[None], (YZ,) + bias.shape), ('y', 'z...  9.14 us
    all_to_all x1, starting transfers between devices, shards(): got = lax.all_to_all(sent, ('xl', 'y', 'z'), 0, 0)  5.86 us
  transfers between devices with their start and end apart: 14, of which 7 were waited for; matrix products, arithmetic and copies ran while one was open for 1% of the time, Pallas kernels for 17%

profile of v5, /device:TPU:16, one launch (start us, length us, event | category | flops | bytes accessed | tf_op | source)
XLA Modules:
  0.0 121.0 jit_solution(70465926572294795)
XLA Ops:
  0.0 3.0 %collective-permute-start.1 = (bf16[4,512,128]{2,1,0:T(8,128)(2,1)}, bf16[4,512,128]{2,1,0:T(8,128)(2,1)S(1)}, u32[]{:S(2)}, u32[]{:S(2)}) collective-permute-start(bf16[4,512,128]{2,1,0:T(8,128)(2,1)} %pair_ref.3), channel_id=1, source_target_pairs={{0,8},{4,12},{8,0},{12,4},{1,9},{5,13},{9,1},{13,5},{2,10},{6,14},... | collective-permute-start | bytes 1572872 | tf_op jit(solution)/shard_map/ppermute | solution.py:278
  3.8 1.0 copy-done
  4.8 0.7 copy-done.7
  5.5 1.3 %shard_map.82 = (bf16[4,512,128]{2,1,0:T(8,128)(2,1)S(1)}, bf16[8,512]{1,0:T(8,128)(2,1)S(1)}, bf16[8,512]{1,0:T(8,128)(2,1)S(1)}) custom-call(s32[11]{0:T(128)S(1)} %stack.48.place, bf16[4,512,128]{2,1,0:T(8,128)(2,1)S(1)} %copy-done, bf16[2,4,128]{2,1,0:T(4,128)(2,1)S(1)} %bitcast.11), custom_call_target="tpu_custom_call" | custom-call | flops 33554432 | bytes 2097152 | tf_op jit(solution)/shard_map/pallas_call | solution.py:389
  6.9 1.2 collective-permute-done.3
  8.2 0.7 broadcast_in_dim.8
  8.9 9.3 %all-to-all-start = ((bf16[16,16,512]{2,1,0:T(8,128)(2,1)}), bf16[16,16,512]{2,1,0:T(8,128)(2,1)S(1)}, u32[]{:S(2)}, u32[]{:S(2)}) async-start(bf16[16,16,512]{2,1,0:T(8,128)(2,1)} %broadcast_in_dim.8), calls=%async_computation | async-start | bytes 524288 | tf_op jit(solution)/shard_map/all_to_all | solution.py:352
  18.3 0.7 shard_map.83.refs_3_
  19.5 9.1 %all-to-all-done.refs_4_ = bf16[16,16,512]{2,1,0:T(8,128)(2,1)S(1)} async-done(((bf16[16,16,512]{2,1,0:T(8,128)(2,1)}), bf16[16,16,512]{2,1,0:T(8,128)(2,1)S(1)}, u32[]{:S(2)}, u32[]{:S(2)}) %all-to-all-start) | async-done | bytes 262176 | tf_op jit(solution)/shard_map/all_to_all | solution.py:352
  28.7 0.6 collective-permute-start.4
  29.4 2.4 %shard_map.85 = (bf16[16,256,128]{2,1,0:T(8,128)(2,1)S(1)}, bf16[16,128,512]{2,1,0:T(8,128)(2,1)S(1)}, bf16[16,512,128]{2,1,0:T(8,128)(2,1)S(1)}, f32[16,256,128]{2,1,0:T(8,128)S(1)}) custom-call(s32[11]{0:T(128)S(1)} %stack.48.place, bf16[4,512,128]{2,1,0:T(8,128)(2,1)S(1)} %collective-permute-done.refs_0_, ...), custom_call_target="tpu_custom_call" | custom-call | flops 805306368 | bytes 12582912 | tf_op jit(solution)/shard_map/pallas_call | solution.py:415
  31.7 3.7 %shard_map.86 = (bf16[8,256,128]{2,1,0:T(8,128)(2,1)S(1)}, bf16[8,256,128]{2,1,0:T(8,128)(2,1)S(1)}) custom-call(s32[11]{0:T(128)S(1)} %stack.48.place, bf16[16,256,128]{2,1,0:T(8,128)(2,1)S(1)} %get-tuple-element.34.refs_0_, bf16[16,128,512]{2,1,0:T(8,128)(2,1)S(1)} %get-tuple-element.35.refs_1_, bf16[16,512,128]{2,1,0:T(8,128)(2,1)S(1)} %get-tuple-element.36.refs_2_, ...), custom_call_target="tpu_custom_call" | custom-call | flops 1073741824 | bytes 4194304 | tf_op jit(solution)/shard_map/pallas_call | solution.py:263
  35.4 2.2 %shard_map.88 = bf16[8,256,128]{2,1,0:T(8,128)(2,1)S(1)} custom-call(s32[11]{0:T(128)S(1)} %stack.48.place, bf16[16,256,128]{2,1,0:T(8,128)(2,1)S(1)} %get-tuple-element.34.refs_0_, bf16[16,128,512]{2,1,0:T(8,128)(2,1)S(1)} %get-tuple-element.35.refs_1_, bf16[16,512,128]{2,1,0:T(8,128)(2,1)S(1)} %get-tuple-element.36.refs_2_, ...), custom_call_target="tpu_custom_call", output_to_operand_aliasing={{}: (6, {})} | custom-call | flops 536870912 | bytes 4194304 | tf_op jit(solution)/shard_map/pallas_call | solution.py:263
  37.9 2.2 %shard_map.87.own_ref = bf16[8,256,128]{2,1,0:T(8,128)(2,1)S(1)} custom-call(s32[11]{0:T(128)S(1)} %stack.48.place, bf16[16,256,128]{2,1,0:T(8,128)(2,1)S(1)} %get-tuple-element.34.refs_0_, bf16[16,128,512]{2,1,0:T(8,128)(2,1)S(1)} %get-tuple-element.35.refs_1_, bf16[16,512,128]{2,1,0:T(8,128)(2,1)S(1)} %get-tuple-element.36.refs_2_, ...), custom_call_target="tpu_custom_call", output_to_operand_aliasing={{}: (6, {})} | custom-call | flops 536870912 | bytes 4194304 | tf_op jit(solution)/shard_map/pallas_call | solution.py:263
  40.1 2.4 %shard_map.89 = (bf16[4,256,128]{2,1,0:T(8,128)(2,1)S(1)}, bf16[4,256,128]{2,1,0:T(8,128)(2,1)S(1)}, bf16[32,96,128]{2,1,0:T(8,128)(2,1)}) custom-call(s32[11]{0:T(128)S(1)} %stack.48.place, bf16[8,256,128]{2,1,0:T(8,128)(2,1)S(1)} %shard_map.87.own_ref, bf16[8,256,128]{2,1,0:T(8,128)(2,1)S(1)} %collective-permute-done.5.got_ref, ...), custom_call_target="tpu_custom_call" | custom-call | flops 134217728 | bytes 3145728 | tf_op jit(solution)/shard_map/pallas_call | solution.py:427
  42.6 5.9 %all-to-all-start.1 = ((bf16[32,96,128]{2,1,0:T(8,128)(2,1)}), bf16[32,96,128]{2,1,0:T(8,128)(2,1)S(1)}, u32[]{:S(2)}, u32[]{:S(2)}) async-start(bf16[32,96,128]{2,1,0:T(8,128)(2,1)} %get-tuple-element.42), calls=%async_computation.1 | async-start | bytes 1572864 | tf_op jit(solution)/shard_map/all_to_all | solution.py:440
  48.4 2.1 %collective-permute-start.6 = (bf16[4,256,128]{2,1,0:T(8,128)(2,1)S(1)}, bf16[4,256,128]{2,1,0:T(8,128)(2,1)S(1)}, u32[]{:S(2)}, u32[]{:S(2)}) collective-permute-start(bf16[4,256,128]{2,1,0:T(8,128)(2,1)S(1)} %get-tuple-element.43), channel_id=1, source_target_pairs={{0,8},{4,12},{8,0},{12,4},{1,9},{5,13},{9,1},{13,5},{2,10},{6,14},... | collective-permute-start | bytes 786440 | tf_op jit(solution)/shard_map/ppermute | solution.py:278
  50.5 11.3 %collective-permute-done.6.got_ref = bf16[4,256,128]{2,1,0:T(8,128)(2,1)S(1)} collective-permute-done((bf16[4,256,128]{2,1,0:T(8,128)(2,1)S(1)}, bf16[4,256,128]{2,1,0:T(8,128)(2,1)S(1)}, u32[]{:S(2)}, u32[]{:S(2)}) %collective-permute-start.6) | collective-permute-done | bytes 262176 | tf_op jit(solution)/shard_map/ppermute | solution.py:278
  61.8 9.2 %all-to-all-done.1.own_in = bf16[32,96,128]{2,1,0:T(8,128)(2,1)S(1)} async-done(((bf16[32,96,128]{2,1,0:T(8,128)(2,1)}), bf16[32,96,128]{2,1,0:T(8,128)(2,1)S(1)}, u32[]{:S(2)}, u32[]{:S(2)}) %all-to-all-start.1) | async-done | bytes 786464 | tf_op jit(solution)/shard_map/all_to_all | solution.py:440
  71.1 2.3 %collective-permute-done.7.sib_in = bf16[32,96,128]{2,1,0:T(8,128)(2,1)S(1)} collective-permute-done((bf16[32,96,128]{2,1,0:T(8,128)(2,1)S(1)}, bf16[32,96,128]{2,1,0:T(8,128)(2,1)S(1)}, u32[]{:S(2)}, u32[]{:S(2)}) %collective-permute-start.7) | collective-permute-done | bytes 786464 | tf_op jit(solution)/shard_map/ppermute | solution.py:343
  73.4 0.8 shard_map.91.refs_4_
  74.2 1.1 collective-permute-start.10
  75.3 0.9 collective-permute-start.9
  76.2 2.7 %collective-permute-start.8 = (bf16[2,128,512]{2,1,0:T(8,128)(2,1)S(1)}, bf16[2,128,512]{2,1,0:T(8,128)(2,1)S(1)}, u32[]{:S(2)}, u32[]{:S(2)}) collective-permute-start(bf16[2,128,512]{2,1,0:T(8,128)(2,1)S(1)} %shard_map.91.refs_4_), channel_id=1, source_target_pairs={{0,8},{4,12},{8,0},{12,4},{1,9},{5,13},{9,1},{13,5},{2,10},{6,14},... | collective-permute-start | bytes 786440 | tf_op jit(solution)/shard_map/ppermute | solution.py:278
  79.0 3.3 %shard_map.90 = (bf16[8,512,128]{2,1,0:T(8,128)(2,1)S(1)}, bf16[8,128,512]{2,1,0:T(8,128)(2,1)S(1)}, bf16[8,512,128]{2,1,0:T(8,128)(2,1)S(1)}, f32[8,512,128]{2,1,0:T(8,128)S(1)}, bf16[4,512,128]{2,1,0:T(8,128)(2,1)S(1)}) custom-call(s32[11]{0:T(128)S(1)} %stack.48.place, bf16[32,96,128]{2,1,0:T(8,128)(2,1)S(1)} %all-to-all-done.1.own_in, ...), custom_call_target="tpu_custom_call" | custom-call | flops 536870912 | bytes 6291456 | tf_op jit(solution)/shard_map/pallas_call | solution.py:453
  82.3 2.4 %shard_map.92 = (bf16[64,4,8,128]{3,2,1,0:T(8,128)(2,1)S(1)}, bf16[64,4,8,128]{3,2,1,0:T(8,128)(2,1)S(1)}) custom-call(s32[11]{0:T(128)S(1)} %stack.48.place, bf16[8,512,128]{2,1,0:T(8,128)(2,1)S(1)} %get-tuple-element.49.refs_0_, bf16[8,128,512]{2,1,0:T(8,128)(2,1)S(1)} %get-tuple-element.50.refs_1_, bf16[8,512,128]{2,1,0:T(8,128)(2,1)S(1)} %get-tuple-element.51.refs_2_, ...), custom_call_target="tpu_custom_call" | custom-call | flops 536870912 | bytes 4194304 | tf_op jit(solution)/shard_map/pallas_call | solution.py:263
  84.8 4.2 %shard_map.93 = (bf16[64,4,8,128]{3,2,1,0:T(8,128)(2,1)S(1)}, bf16[64,4,8,128]{3,2,1,0:T(8,128)(2,1)S(1)}) custom-call(s32[11]{0:T(128)S(1)} %stack.48.place, bf16[8,512,128]{2,1,0:T(8,128)(2,1)S(1)} %get-tuple-element.49.refs_0_, bf16[8,128,512]{2,1,0:T(8,128)(2,1)S(1)} %get-tuple-element.50.refs_1_, ...), custom_call_target="tpu_custom_call", output_to_operand_aliasing={{0}: (7, {}), {1}: (8, {})} | custom-call | flops 1073741824 | bytes 4194304 | tf_op jit(solution)/shard_map/pallas_call | solution.py:263
  89.0 1.6 %collective-permute-done.8.refs_4_ = bf16[2,128,512]{2,1,0:T(8,128)(2,1)S(1)} collective-permute-done((bf16[2,128,512]{2,1,0:T(8,128)(2,1)S(1)}, bf16[2,128,512]{2,1,0:T(8,128)(2,1)S(1)}, u32[]{:S(2)}, u32[]{:S(2)}) %collective-permute-start.8) | collective-permute-done | bytes 262176 | tf_op jit(solution)/shard_map/ppermute | solution.py:278
  90.6 2.4 %shard_map.94 = (bf16[64,4,8,128]{3,2,1,0:T(8,128)(2,1)S(1)}, bf16[64,4,8,128]{3,2,1,0:T(8,128)(2,1)S(1)}) custom-call(s32[11]{0:T(128)S(1)} %stack.48.place, bf16[8,512,128]{2,1,0:T(8,128)(2,1)S(1)} %get-tuple-element.49.refs_0_, bf16[8,128,512]{2,1,0:T(8,128)(2,1)S(1)} %get-tuple-element.50.refs_1_, ...), custom_call_target="tpu_custom_call", output_to_operand_aliasing={{0}: (6, {}), {1}: (7, {})} | custom-call | flops 536870912 | bytes 4194304 | tf_op jit(solution)/shard_map/pallas_call | solution.py:263
  93.2 1.9 %collective-permute-done.11.got_ref = bf16[64,4,8,128]{3,2,1,0:T(8,128)(2,1)S(1)} collective-permute-done((bf16[64,4,8,128]{3,2,1,0:T(8,128)(2,1)S(1)}, bf16[64,4,8,128]{3,2,1,0:T(8,128)(2,1)S(1)}, u32[]{:S(2)}, u32[]{:S(2)}) %collective-permute-start.11) | collective-permute-done | bytes 524320 | tf_op jit(solution)/shard_map/ppermute | solution.py:343
  95.4 24.7 %all_to_all.15.back_ref = bf16[64,4,8,128]{3,2,1,0:T(8,128)(2,1)S(1)} all-to-all(bf16[64,4,8,128]{3,2,1,0:T(8,128)(2,1)S(1)} %shard_map.95), channel_id=1, replica_groups=mesh['y'=2,'z'=8,'xh'=2,'xl'=2,'c'=2,'dp'=2] {'xh','xl','y','z'}, dimensions={0} | all-to-all | bytes 1048576 | tf_op jit(solution)/shard_map/all_to_all | solution.py:470
  120.1 0.9 shard_map.96
  (38 shorter events, 1.7 us)
Async XLA Ops:
  0.0 29.3 %copy-start.3 = (bf16[2,128,128]{2,1,0:T(8,128)(2,1)S(1)}, bf16[2,128,128]{2,1,0:T(8,128)(2,1)}, u32[]{:S(2)}) copy-start(bf16[2,128,128]{2,1,0:T(8,128)(2,1)} %wq.1) | copy-start | bytes 196612
  0.0 18.3 %collective-permute-start.1 = (bf16[4,512,128]{2,1,0:T(8,128)(2,1)}, bf16[4,512,128]{2,1,0:T(8,128)(2,1)S(1)}, u32[]{:S(2)}, u32[]{:S(2)}) collective-permute-start(bf16[4,512,128]{2,1,0:T(8,128)(2,1)} %pair_ref.3), channel_id=1, source_target_pairs={{0,8},{4,12},{8,0},{12,4},{1,9},{5,13},{9,1},{13,5},{2,10},{6,14},... | collective-permute-start | bytes 1572872 | tf_op jit(solution)/shard_map/ppermute | solution.py:278
  3.8 1.0 copy-start
  4.8 0.7 copy-start.7
  5.5 23.8 %copy-start.4 = (bf16[2,128,128]{2,1,0:T(8,128)(2,1)S(1)}, bf16[2,128,128]{2,1,0:T(8,128)(2,1)}, u32[]{:S(2)}) copy-start(bf16[2,128,128]{2,1,0:T(8,128)(2,1)} %wk.1) | copy-start | bytes 196612
  5.5 23.8 %copy-start.5 = (bf16[2,128,128]{2,1,0:T(8,128)(2,1)S(1)}, bf16[2,128,128]{2,1,0:T(8,128)(2,1)}, u32[]{:S(2)}) copy-start(bf16[2,128,128]{2,1,0:T(8,128)(2,1)} %wv.1) | copy-start | bytes 196612
  5.5 23.8 %copy-start.6 = (bf16[2,128,128]{2,1,0:T(8,128)(2,1)S(1)}, bf16[2,128,128]{2,1,0:T(8,128)(2,1)}, u32[]{:S(2)}) copy-start(bf16[2,128,128]{2,1,0:T(8,128)(2,1)} %wg.1) | copy-start | bytes 196612
  6.8 1.3 %collective-permute-start.3 = (bf16[8,512]{1,0:T(8,128)(2,1)S(1)}, bf16[8,512]{1,0:T(8,128)(2,1)S(1)}, u32[]{:S(2)}, u32[]{:S(2)}) collective-permute-start(bf16[8,512]{1,0:T(8,128)(2,1)S(1)} %get-tuple-element.39), channel_id=1, source_target_pairs={{0,2},{2,0},{1,3},{3,1},{4,6},{6,4},{5,7},{7,5},{8,10},{10,8},{9,1... | collective-permute-start | bytes 24584 | tf_op jit(solution)/shard_map/ppermute | solution.py:343
  8.9 19.8 %all-to-all-start = ((bf16[16,16,512]{2,1,0:T(8,128)(2,1)}), bf16[16,16,512]{2,1,0:T(8,128)(2,1)S(1)}, u32[]{:S(2)}, u32[]{:S(2)}) async-start(bf16[16,16,512]{2,1,0:T(8,128)(2,1)} %broadcast_in_dim.8), calls=%async_computation | async-start | bytes 524288 | tf_op jit(solution)/shard_map/all_to_all | solution.py:352
  18.2 11.1 %collective-permute-start = (bf16[4,512,128]{2,1,0:T(8,128)(2,1)S(1)}, bf16[4,512,128]{2,1,0:T(8,128)(2,1)S(1)}, u32[]{:S(2)}, u32[]{:S(2)}) collective-permute-start(bf16[4,512,128]{2,1,0:T(8,128)(2,1)S(1)} %get-tuple-element.32.refs_1_), channel_id=1, source_target_pairs={{0,2},{2,0},{1,3},{3,1},{4,6},{6,4},{5,7},{7,5},{8,10},{10,8},{9,1... | collective-permute-start | bytes 1572872 | tf_op jit(solution)/shard_map/ppermute | solution.py:343
  19.0 10.4 %collective-permute-start.2 = (bf16[4,512,128]{2,1,0:T(8,128)(2,1)S(1)}, bf16[4,512,128]{2,1,0:T(8,128)(2,1)S(1)}, u32[]{:S(2)}, u32[]{:S(2)}) collective-permute-start(bf16[4,512,128]{2,1,0:T(8,128)(2,1)S(1)} %shard_map.83.refs_3_), channel_id=1, source_target_pairs={{0,2},{2,0},{1,3},{3,1},{4,6},{6,4},{5,7},{7,5},{8,10},{10,8},{9,1... | collective-permute-start | bytes 1572872 | tf_op jit(solution)/shard_map/ppermute | solution.py:343
  28.7 6.7 %collective-permute-start.4 = (bf16[16,16,512]{2,1,0:T(8,128)(2,1)S(1)}, bf16[16,16,512]{2,1,0:T(8,128)(2,1)S(1)}, u32[]{:S(2)}, u32[]{:S(2)}) collective-permute-start(bf16[16,16,512]{2,1,0:T(8,128)(2,1)S(1)} %all-to-all-done.refs_4_), channel_id=1, source_target_pairs={{0,4},{4,0},{8,12},{12,8},{1,5},{5,1},{9,13},{13,9},{2,6},{6,2},{1... | collective-permute-start | bytes 786440 | tf_op jit(solution)/shard_map/ppermute | solution.py:278
  37.6 2.5 %collective-permute-start.5 = (bf16[8,256,128]{2,1,0:T(8,128)(2,1)S(1)}, bf16[8,256,128]{2,1,0:T(8,128)(2,1)S(1)}, u32[]{:S(2)}, u32[]{:S(2)}) collective-permute-start(bf16[8,256,128]{2,1,0:T(8,128)(2,1)S(1)} %shard_map.88), channel_id=1, source_target_pairs={{0,2},{2,0},{1,3},{3,1},{4,6},{6,4},{5,7},{7,5},{8,10},{10,8},{9,1... | collective-permute-start | bytes 1572872 | tf_op jit(solution)/shard_map/ppermute | solution.py:343
  37.9 2.2 %copy-start.1 = (bf16[4,512,128]{2,1,0:T(8,128)(2,1)S(1)}, bf16[4,512,128]{2,1,0:T(8,128)(2,1)}, u32[]{:S(2)}) copy-start(bf16[4,512,128]{2,1,0:T(8,128)(2,1)} %pair_ref.3) | copy-start | bytes 1572868
  37.9 2.2 %copy-start.2 = (bf16[2,128,128]{2,1,0:T(8,128)(2,1)S(1)}, bf16[2,128,128]{2,1,0:T(8,128)(2,1)}, u32[]{:S(2)}) copy-start(bf16[2,128,128]{2,1,0:T(8,128)(2,1)} %w_ref.3) | copy-start | bytes 196612
  37.9 2.2 %copy-start.8 = (bf16[2,128,4]{1,2,0:T(4,128)(2,1)S(1)}, bf16[2,128,4]{1,2,0:T(4,128)(2,1)}, u32[]{:S(2)}) copy-start(bf16[2,128,4]{1,2,0:T(4,128)(2,1)} %param.14) | copy-start | bytes 6148
  42.6 28.5 %all-to-all-start.1 = ((bf16[32,96,128]{2,1,0:T(8,128)(2,1)}), bf16[32,96,128]{2,1,0:T(8,128)(2,1)S(1)}, u32[]{:S(2)}, u32[]{:S(2)}) async-start(bf16[32,96,128]{2,1,0:T(8,128)(2,1)} %get-tuple-element.42), calls=%async_computation.1 | async-start | bytes 1572864 | tf_op jit(solution)/shard_map/all_to_all | solution.py:440
  48.4 13.4 %collective-permute-start.6 = (bf16[4,256,128]{2,1,0:T(8,128)(2,1)S(1)}, bf16[4,256,128]{2,1,0:T(8,128)(2,1)S(1)}, u32[]{:S(2)}, u32[]{:S(2)}) collective-permute-start(bf16[4,256,128]{2,1,0:T(8,128)(2,1)S(1)} %get-tuple-element.43), channel_id=1, source_target_pairs={{0,8},{4,12},{8,0},{12,4},{1,9},{5,13},{9,1},{13,5},{2,10},{6,14},... | collective-permute-start | bytes 786440 | tf_op jit(solution)/shard_map/ppermute | solution.py:278
  71.1 2.3 %collective-permute-start.7 = (bf16[32,96,128]{2,1,0:T(8,128)(2,1)S(1)}, bf16[32,96,128]{2,1,0:T(8,128)(2,1)S(1)}, u32[]{:S(2)}, u32[]{:S(2)}) collective-permute-start(bf16[32,96,128]{2,1,0:T(8,128)(2,1)S(1)} %all-to-all-done.1.own_in), channel_id=1, source_target_pairs={{0,2},{2,0},{1,3},{3,1},{4,6},{6,4},{5,7},{7,5},{8,10},{10,8},{9,1... | collective-permute-start | bytes 2359304 | tf_op jit(solution)/shard_map/ppermute | solution.py:343
  74.2 10.6 %collective-permute-start.10 = (bf16[2,128,512]{2,1,0:T(8,128)(2,1)S(1)}, bf16[2,128,512]{2,1,0:T(8,128)(2,1)S(1)}, u32[]{:S(2)}, u32[]{:S(2)}) collective-permute-start(bf16[2,128,512]{2,1,0:T(8,128)(2,1)S(1)} %shard_map.91.refs_4_), channel_id=1, source_target_pairs={{0,12},{4,8},{8,4},{12,0},{1,13},{5,9},{9,5},{13,1},{2,14},{6,10},... | collective-permute-start | bytes 786440 | tf_op jit(solution)/shard_map/ppermute | solution.py:278
  75.3 9.5 %collective-permute-start.9 = (bf16[2,128,512]{2,1,0:T(8,128)(2,1)S(1)}, bf16[2,128,512]{2,1,0:T(8,128)(2,1)S(1)}, u32[]{:S(2)}, u32[]{:S(2)}) collective-permute-start(bf16[2,128,512]{2,1,0:T(8,128)(2,1)S(1)} %shard_map.91.refs_4_), channel_id=1, source_target_pairs={{0,4},{4,0},{8,12},{12,8},{1,5},{5,1},{9,13},{13,9},{2,6},{6,2},{1... | collective-permute-start | bytes 786440 | tf_op jit(solution)/shard_map/ppermute | solution.py:278
  76.2 14.4 %collective-permute-start.8 = (bf16[2,128,512]{2,1,0:T(8,128)(2,1)S(1)}, bf16[2,128,512]{2,1,0:T(8,128)(2,1)S(1)}, u32[]{:S(2)}, u32[]{:S(2)}) collective-permute-start(bf16[2,128,512]{2,1,0:T(8,128)(2,1)S(1)} %shard_map.91.refs_4_), channel_id=1, source_target_pairs={{0,8},{4,12},{8,0},{12,4},{1,9},{5,13},{9,1},{13,5},{2,10},{6,14},... | collective-permute-start | bytes 786440 | tf_op jit(solution)/shard_map/ppermute | solution.py:278
  93.1 2.0 %collective-permute-start.11 = (bf16[64,4,8,128]{3,2,1,0:T(8,128)(2,1)S(1)}, bf16[64,4,8,128]{3,2,1,0:T(8,128)(2,1)S(1)}, u32[]{:S(2)}, u32[]{:S(2)}) collective-permute-start(bf16[64,4,8,128]{3,2,1,0:T(8,128)(2,1)S(1)} %get-tuple-element.58), channel_id=1, source_target_pairs={{0,2},{2,0},{1,3},{3,1},{4,6},{6,4},{5,7},{7,5},{8,10},{10,8},{9,1... | collective-permute-start | bytes 1572872 | tf_op jit(solution)/shard_map/ppermute | solution.py:343

commit v6 on v5

--- a/solution.py
+++ b/solution.py
@@ -53,30 +53,30 @@
     return moved * lax.rsqrt(spread + EPSILON)
 
 
-def bias_rows(wb_ref, step, normed, r, count, masked, rows_ref):
+def head_bias(wb_ref, step, normed, masked):
     four = lax.dot_general(
         wb_ref[step], normed, (((1,), (1,)), ((), ())), preferred_element_type=jnp.float32
     )
-    four = jnp.where(masked, MASKED, four)
-    for h in range(four.shape[0]):
-        rows_ref[h * count + r : h * count + r + 1, :] = four[h : h + 1]
-
-
-def prepare_rows(place, pair_ref, wb_ref, normed_ref, mine_ref, other_ref, rows_ref):
-    count, tokens, _ = pair_ref.shape
+    return jnp.where(masked, MASKED, four)
+
+
+def prepare_rows(place, sib_ref, own_ref, wb_ref, normed_ref, bias_ref, rows_ref):
+    count, tokens, _ = own_ref.shape
+    core = place[CORE]
     lane = lax.broadcasted_iota(jnp.int32, (1, tokens), 1)
     x, rest = lane // QUARTER, lane % QUARTER
     token = ((rest // ROWS) * X + x) * ROWS + rest % ROWS
     masked = token >= place[VALID]
-    for r in range(count):
-        wide = inner_order(pair_ref[r].astype(jnp.float32))
-        normed = layer_normed(wide).astype(jnp.bfloat16)
-        normed_ref[r] = normed
-        bias_rows(wb_ref, 0, normed, r, count, masked, rows_ref)
-    low, high = rows_ref[: 2 * count], rows_ref[2 * count :]
-    first = place[CORE] == 0
-    mine_ref[...] = jnp.where(first, low, high).astype(jnp.bfloat16)
-    other_ref[...] = jnp.where(first, high, low).astype(jnp.bfloat16)
+    for half, (ref, at) in enumerate(((sib_ref, 1 - core), (own_ref, core))):
+        for r in range(count):
+            wide = inner_order(ref[r].astype(jnp.float32))
+            normed = layer_normed(wide).astype(jnp.bfloat16)
+            normed_ref[half * count + r] = normed
+            four = head_bias(wb_ref, 0, normed, masked)
+            for h in range(2):
+                row = jnp.where(core == 0, four[h : h + 1], four[2 + h : 3 + h])
+                rows_ref[pl.ds(h * ROWS + at * count + r, 1), :] = row
+    bias_ref[...] = rows_ref[...].astype(jnp.bfloat16)
 
 
 def prepare_far(far_ref, normed_ref):
@@ -106,12 +106,9 @@
 def project_rows(place, *refs):
     groups, (w_ref, query_ref, key_ref, value_ref, gate_ref) = refs[:-5], refs[-5:]
     asking = pl.ds(pl.multiple_of(place[UPPER] * HALF, HALF), HALF)
-    for g, ref in enumerate(groups):
-        count = ref.shape[0]
-        for r in range(count):
-            out = project(place[CORE], ref[r], ref[r, asking, :], w_ref[...])
-            at = g * count + r
-            query_ref[at], key_ref[at], value_ref[at], gate_ref[at] = out
+    for at, (ref, r) in enumerate((ref, r) for ref in groups for r in range(ref.shape[0])):
+        out = project(place[CORE], ref[r], ref[r, asking, :], w_ref[...])
+        query_ref[at], key_ref[at], value_ref[at], gate_ref[at] = out
 
 
 def received_quarters(place):
@@ -290,7 +287,7 @@
 def attend_columns(place, projected, piece):
     moved = {s: along_x(piece, s) for s in (1, 3, 2)}
     outs = None
-    for steps in ((0,), (1, 3), (2,)):
+    for steps in ((0,), (3, 1), (2,)):
         pieces = [moved[s] if s else piece for s in steps]
         outs = attend_some(steps, True, (0, 1), place, projected, pieces, outs)
     for_sib, own = outs
@@ -313,7 +310,10 @@
             normed = layer_normed(one.astype(jnp.float32))
             wide_ref[:, at * ROWS : (at + 1) * ROWS] = normed.reshape(chips, ROWS, channels)
             masked = place[FIRST_ROW + far] + r >= place[VALID]
-            bias_rows(wb_ref, 1, normed.astype(jnp.bfloat16), at, 2 * count, masked, rows_ref)
+            four = head_bias(wb_ref, 1, normed.astype(jnp.bfloat16), masked)
+            for h in range(4):
+                spot = 2 * count * h + at
+                rows_ref[spot : spot + 1, :] = four[h : h + 1]
     rows = 2 * count * ROWS
     sent_ref[:, :rows] = wide_ref[...].astype(jnp.bfloat16)
     for x in range(X // 2):
@@ -341,19 +341,6 @@
 
 def swap(array):
     return lax.ppermute(array, "c", [(0, 1), (1, 0)])
-
-
-def spread_bias(core, mine, other):
-    got = swap(other)
-    rows, tokens = mine.shape
-    mine, got = (a.reshape(2, rows // 2, tokens) for a in (mine, got))
-    low, high = jnp.where(core == 0, mine, got), jnp.where(core == 0, got, mine)
-    bias = jnp.stack([low, high], axis=1).reshape(2 * rows, tokens)
-    return lax.all_to_all(jnp.broadcast_to(bias[None], (YZ,) + bias.shape), ("y", "z"), 0, 0)
-
-
-def whole(shape):
-    return pl.BlockSpec(shape, lambda s: (0,) * len(shape))
 
 
 def struct(shape, kind=jnp.bfloat16):
@@ -374,7 +361,6 @@
     piece = (X * YZ, count, ROWS, channels)
     rows = (ROWS, tokens, channels)
     held = (count, tokens, channels)
-    half = struct((ROWS, tokens))
     bias_scratch = pltpu.VMEM((4 * count, tokens), jnp.float32)
 
     def projections(number, asking):
@@ -385,17 +371,19 @@
             struct((number, asking, channels), jnp.float32),
         ]
 
+    sib = swap(pair)
     far = along_x(pair, 2)
-    normed, mine, other = pl.pallas_call(
+    normed, bias = pl.pallas_call(
         prepare_rows,
-        in_specs=[SMEM, VMEM, VMEM],
-        out_specs=[VMEM] * 3,
-        out_shape=[struct(held), half, half],
+        in_specs=[SMEM, VMEM, VMEM, VMEM],
+        out_specs=[VMEM] * 2,
+        out_shape=[struct(rows), struct((2 * ROWS, tokens))],
         scratch_shapes=[bias_scratch],
         compiler_params=params(),
         cost_estimate=cost(1 << 25, 2 << 20),
-    )(place, pair, wb)
-    gathered = spread_bias(core, mine, other)
+    )(place, sib, pair, wb)
+    copies = jnp.broadcast_to(bias[None], (YZ,) + bias.shape)
+    gathered = lax.all_to_all(copies, ("y", "z"), 0, 0)
     packed = struct((channels, 4 * channels))
     first_weights, next_weights = pl.pallas_call(
         pack_weights,
@@ -414,12 +402,12 @@
     )(far)
     projected = pl.pallas_call(
         project_rows,
-        in_specs=[SMEM] + [VMEM] * 5,
+        in_specs=[SMEM] + [VMEM] * 4,
         out_specs=[VMEM] * 4,
         out_shape=projections(2 * ROWS, HALF),
         compiler_params=params(),
         cost_estimate=cost(12 * ROWS * tokens * channels * channels, 12 << 20),
-    )(place, swap(normed), normed, swap(normed_far), normed_far, first_weights)
+    )(place, normed, swap(normed_far), normed_far, first_weights)
     got, own = attend_rows(place, projected, gathered)
     peers = X // 2 * YZ
     message = (peers, 2 * count * ROWS + 8 * count, channels)

time: 121 us -> 121 us (level)
    ppermute x6 -> x5, waiting for transfers between devices: 5.34 us -> 4.19 us  [swap(): return lax.ppermute(array, 'c', [(0, 1), (1, 0)])]
  transfers between devices with their start and end apart: 14 -> 13, of which waited for: 7 -> 6; matrix products, arithmetic and copies ran while one was open for 1% -> 1% of each run, Pallas kernels for 17% -> 17%
where the time goes in v6:
time: 121 us; the launch traced here: 120 us
  waiting for transfers between devices  36.1 us (30%)
  Pallas kernels  29.8 us (25%)
  starting transfers between devices  26.2 us (22%)
  blocking collectives  24.7 us (20%)
  local copies, waits for them, and re-layouts  2.57 us (2%)
    all_to_all x1, blocking collectives, shards(): back = lax.all_to_all(branch, X_AXES + ('y', 'z'), 0, 0)  24.7 us
    pallas_call x6, Pallas kernels, attend_some(): pl.pallas_call(functools.partial(attend_quarters, steps, columns, parts),...  17.1 us
    ppermute x6, waiting for transfers between devices, along_x(): return lax.ppermute(array, X_AXES, [(i, i ^ s) for i in range(X)])  13 us
    ppermute x6, starting transfers between devices, along_x(): return lax.ppermute(array, X_AXES, [(i, i ^ s) for i in range(X)])  10.6 us
    all_to_all x1, waiting for transfers between devices, shards(): gathered = lax.all_to_all(copies, ('y', 'z'), 0, 0)  9.7 us
    all_to_all x1, starting transfers between devices, shards(): gathered = lax.all_to_all(copies, ('y', 'z'), 0, 0)  9.29 us
    all_to_all x1, waiting for transfers between devices, shards(): got = lax.all_to_all(sent, ('xl', 'y', 'z'), 0, 0)  9.26 us
    all_to_all x1, starting transfers between devices, shards(): got = lax.all_to_all(sent, ('xl', 'y', 'z'), 0, 0)  5.87 us
  transfers between devices with their start and end apart: 13, of which 6 were waited for; matrix products, arithmetic and copies ran while one was open for 1% of the time, Pallas kernels for 17%

profile of v6, /device:TPU:16, one launch (start us, length us, event | category | flops | bytes accessed | tf_op | source)
XLA Modules:
  0.0 120.3 jit_solution(10322433258752587614)
XLA Ops:
  0.0 3.1 %collective-permute-start.1 = (bf16[4,512,128]{2,1,0:T(8,128)(2,1)}, bf16[4,512,128]{2,1,0:T(8,128)(2,1)S(1)}, u32[]{:S(2)}, u32[]{:S(2)}) collective-permute-start(bf16[4,512,128]{2,1,0:T(8,128)(2,1)} %pair_ref.1), channel_id=1, source_target_pairs={{0,8},{4,12},{8,0},{12,4},{1,9},{5,13},{9,1},{13,5},{2,10},{6,14},... | collective-permute-start | bytes 1572872 | tf_op jit(solution)/shard_map/ppermute | solution.py:275
  3.9 1.0 copy-done
  4.9 0.7 copy-done.7
  5.6 1.9 %shard_map.82 = (bf16[8,512,128]{2,1,0:T(8,128)(2,1)S(1)}, bf16[16,512]{1,0:T(8,128)(2,1)S(1)}) custom-call(s32[11]{0:T(128)S(1)} %stack.43.place, bf16[4,512,128]{2,1,0:T(8,128)(2,1)S(1)} %collective-permute-done.sib_ref, bf16[4,512,128]{2,1,0:T(8,128)(2,1)S(1)} %copy-done, bf16[2,4,128]{2,1,0:T(4,128)(2,1)S(1)} %bitcast.11), custom_call_target="tpu_custom_call" | custom-call | flops 33554432 | bytes 2097152 | tf_op jit(solution)/shard_map/pallas_call | solution.py:376
  7.5 0.7 broadcast_in_dim.2
  8.2 9.3 %all-to-all-start = ((bf16[16,16,512]{2,1,0:T(8,128)(2,1)}), bf16[16,16,512]{2,1,0:T(8,128)(2,1)S(1)}, u32[]{:S(2)}, u32[]{:S(2)}) async-start(bf16[16,16,512]{2,1,0:T(8,128)(2,1)} %broadcast_in_dim.2), calls=%async_computation | async-start | bytes 524288 | tf_op jit(solution)/shard_map/all_to_all | solution.py:386
  17.5 0.7 shard_map.83.refs_2_
  18.3 9.7 %all-to-all-done.refs_4_ = bf16[16,16,512]{2,1,0:T(8,128)(2,1)S(1)} async-done(((bf16[16,16,512]{2,1,0:T(8,128)(2,1)}), bf16[16,16,512]{2,1,0:T(8,128)(2,1)S(1)}, u32[]{:S(2)}, u32[]{:S(2)}) %all-to-all-start) | async-done | bytes 262176 | tf_op jit(solution)/shard_map/all_to_all | solution.py:386
  28.0 0.6 collective-permute-start.3
  28.7 2.4 %shard_map.85 = (bf16[16,256,128]{2,1,0:T(8,128)(2,1)S(1)}, bf16[16,128,512]{2,1,0:T(8,128)(2,1)S(1)}, bf16[16,512,128]{2,1,0:T(8,128)(2,1)S(1)}, f32[16,256,128]{2,1,0:T(8,128)S(1)}) custom-call(s32[11]{0:T(128)S(1)} %stack.43.place, bf16[8,512,128]{2,1,0:T(8,128)(2,1)S(1)} %get-tuple-element.31.refs_0_, ...), custom_call_target="tpu_custom_call" | custom-call | flops 805306368 | bytes 12582912 | tf_op jit(solution)/shard_map/pallas_call | solution.py:403
  31.0 3.7 %shard_map.86 = (bf16[8,256,128]{2,1,0:T(8,128)(2,1)S(1)}, bf16[8,256,128]{2,1,0:T(8,128)(2,1)S(1)}) custom-call(s32[11]{0:T(128)S(1)} %stack.43.place, bf16[16,256,128]{2,1,0:T(8,128)(2,1)S(1)} %get-tuple-element.33.refs_0_, bf16[16,128,512]{2,1,0:T(8,128)(2,1)S(1)} %get-tuple-element.34.refs_1_, bf16[16,512,128]{2,1,0:T(8,128)(2,1)S(1)} %get-tuple-element.35.refs_2_, ...), custom_call_target="tpu_custom_call" | custom-call | flops 1073741824 | bytes 4194304 | tf_op jit(solution)/shard_map/pallas_call | solution.py:260
  34.7 2.2 %shard_map.88 = bf16[8,256,128]{2,1,0:T(8,128)(2,1)S(1)} custom-call(s32[11]{0:T(128)S(1)} %stack.43.place, bf16[16,256,128]{2,1,0:T(8,128)(2,1)S(1)} %get-tuple-element.33.refs_0_, bf16[16,128,512]{2,1,0:T(8,128)(2,1)S(1)} %get-tuple-element.34.refs_1_, bf16[16,512,128]{2,1,0:T(8,128)(2,1)S(1)} %get-tuple-element.35.refs_2_, ...), custom_call_target="tpu_custom_call", output_to_operand_aliasing={{}: (6, {})} | custom-call | flops 536870912 | bytes 4194304 | tf_op jit(solution)/shard_map/pallas_call | solution.py:260
  37.2 2.2 %shard_map.87.own_ref = bf16[8,256,128]{2,1,0:T(8,128)(2,1)S(1)} custom-call(s32[11]{0:T(128)S(1)} %stack.43.place, bf16[16,256,128]{2,1,0:T(8,128)(2,1)S(1)} %get-tuple-element.33.refs_0_, bf16[16,128,512]{2,1,0:T(8,128)(2,1)S(1)} %get-tuple-element.34.refs_1_, bf16[16,512,128]{2,1,0:T(8,128)(2,1)S(1)} %get-tuple-element.35.refs_2_, ...), custom_call_target="tpu_custom_call", output_to_operand_aliasing={{}: (6, {})} | custom-call | flops 536870912 | bytes 4194304 | tf_op jit(solution)/shard_map/pallas_call | solution.py:260
  39.5 2.4 %shard_map.89 = (bf16[4,256,128]{2,1,0:T(8,128)(2,1)S(1)}, bf16[4,256,128]{2,1,0:T(8,128)(2,1)S(1)}, bf16[32,96,128]{2,1,0:T(8,128)(2,1)}) custom-call(s32[11]{0:T(128)S(1)} %stack.43.place, bf16[8,256,128]{2,1,0:T(8,128)(2,1)S(1)} %shard_map.87.own_ref, bf16[8,256,128]{2,1,0:T(8,128)(2,1)S(1)} %collective-permute-done.4.got_ref, ...), custom_call_target="tpu_custom_call" | custom-call | flops 134217728 | bytes 3145728 | tf_op jit(solution)/shard_map/pallas_call | solution.py:415
  41.9 5.9 %all-to-all-start.1 = ((bf16[32,96,128]{2,1,0:T(8,128)(2,1)}), bf16[32,96,128]{2,1,0:T(8,128)(2,1)S(1)}, u32[]{:S(2)}, u32[]{:S(2)}) async-start(bf16[32,96,128]{2,1,0:T(8,128)(2,1)} %get-tuple-element.40), calls=%async_computation.1 | async-start | bytes 1572864 | tf_op jit(solution)/shard_map/all_to_all | solution.py:428
  47.8 2.1 %collective-permute-start.5 = (bf16[4,256,128]{2,1,0:T(8,128)(2,1)S(1)}, bf16[4,256,128]{2,1,0:T(8,128)(2,1)S(1)}, u32[]{:S(2)}, u32[]{:S(2)}) collective-permute-start(bf16[4,256,128]{2,1,0:T(8,128)(2,1)S(1)} %get-tuple-element.41), channel_id=1, source_target_pairs={{0,8},{4,12},{8,0},{12,4},{1,9},{5,13},{9,1},{13,5},{2,10},{6,14},... | collective-permute-start | bytes 786440 | tf_op jit(solution)/shard_map/ppermute | solution.py:275
  49.9 11.3 %collective-permute-done.5.got_ref = bf16[4,256,128]{2,1,0:T(8,128)(2,1)S(1)} collective-permute-done((bf16[4,256,128]{2,1,0:T(8,128)(2,1)S(1)}, bf16[4,256,128]{2,1,0:T(8,128)(2,1)S(1)}, u32[]{:S(2)}, u32[]{:S(2)}) %collective-permute-start.5) | collective-permute-done | bytes 262176 | tf_op jit(solution)/shard_map/ppermute | solution.py:275
  61.2 9.3 %all-to-all-done.1.own_in = bf16[32,96,128]{2,1,0:T(8,128)(2,1)S(1)} async-done(((bf16[32,96,128]{2,1,0:T(8,128)(2,1)}), bf16[32,96,128]{2,1,0:T(8,128)(2,1)S(1)}, u32[]{:S(2)}, u32[]{:S(2)}) %all-to-all-start.1) | async-done | bytes 786464 | tf_op jit(solution)/shard_map/all_to_all | solution.py:428
  70.4 2.3 %collective-permute-done.6.sib_in = bf16[32,96,128]{2,1,0:T(8,128)(2,1)S(1)} collective-permute-done((bf16[32,96,128]{2,1,0:T(8,128)(2,1)S(1)}, bf16[32,96,128]{2,1,0:T(8,128)(2,1)S(1)}, u32[]{:S(2)}, u32[]{:S(2)}) %collective-permute-start.6) | collective-permute-done | bytes 786464 | tf_op jit(solution)/shard_map/ppermute | solution.py:343
  72.7 0.8 shard_map.91.refs_4_
  73.5 1.1 collective-permute-start.8
  74.6 0.9 collective-permute-start.9
  75.6 2.8 %collective-permute-start.7 = (bf16[2,128,512]{2,1,0:T(8,128)(2,1)S(1)}, bf16[2,128,512]{2,1,0:T(8,128)(2,1)S(1)}, u32[]{:S(2)}, u32[]{:S(2)}) collective-permute-start(bf16[2,128,512]{2,1,0:T(8,128)(2,1)S(1)} %shard_map.91.refs_4_), channel_id=1, source_target_pairs={{0,8},{4,12},{8,0},{12,4},{1,9},{5,13},{9,1},{13,5},{2,10},{6,14},... | collective-permute-start | bytes 786440 | tf_op jit(solution)/shard_map/ppermute | solution.py:275
  78.3 3.3 %shard_map.90 = (bf16[8,512,128]{2,1,0:T(8,128)(2,1)S(1)}, bf16[8,128,512]{2,1,0:T(8,128)(2,1)S(1)}, bf16[8,512,128]{2,1,0:T(8,128)(2,1)S(1)}, f32[8,512,128]{2,1,0:T(8,128)S(1)}, bf16[4,512,128]{2,1,0:T(8,128)(2,1)S(1)}) custom-call(s32[11]{0:T(128)S(1)} %stack.43.place, bf16[32,96,128]{2,1,0:T(8,128)(2,1)S(1)} %all-to-all-done.1.own_in, ...), custom_call_target="tpu_custom_call" | custom-call | flops 536870912 | bytes 6291456 | tf_op jit(solution)/shard_map/pallas_call | solution.py:441
  81.7 2.4 %shard_map.92 = (bf16[64,4,8,128]{3,2,1,0:T(8,128)(2,1)S(1)}, bf16[64,4,8,128]{3,2,1,0:T(8,128)(2,1)S(1)}) custom-call(s32[11]{0:T(128)S(1)} %stack.43.place, bf16[8,512,128]{2,1,0:T(8,128)(2,1)S(1)} %get-tuple-element.47.refs_0_, bf16[8,128,512]{2,1,0:T(8,128)(2,1)S(1)} %get-tuple-element.48.refs_1_, bf16[8,512,128]{2,1,0:T(8,128)(2,1)S(1)} %get-tuple-element.49.refs_2_, ...), custom_call_target="tpu_custom_call" | custom-call | flops 536870912 | bytes 4194304 | tf_op jit(solution)/shard_map/pallas_call | solution.py:260
  84.1 4.2 %shard_map.93 = (bf16[64,4,8,128]{3,2,1,0:T(8,128)(2,1)S(1)}, bf16[64,4,8,128]{3,2,1,0:T(8,128)(2,1)S(1)}) custom-call(s32[11]{0:T(128)S(1)} %stack.43.place, bf16[8,512,128]{2,1,0:T(8,128)(2,1)S(1)} %get-tuple-element.47.refs_0_, bf16[8,128,512]{2,1,0:T(8,128)(2,1)S(1)} %get-tuple-element.48.refs_1_, ...), custom_call_target="tpu_custom_call", output_to_operand_aliasing={{0}: (7, {}), {1}: (8, {})} | custom-call | flops 1073741824 | bytes 4194304 | tf_op jit(solution)/shard_map/pallas_call | solution.py:260
  88.3 1.6 %collective-permute-done.7.refs_4_ = bf16[2,128,512]{2,1,0:T(8,128)(2,1)S(1)} collective-permute-done((bf16[2,128,512]{2,1,0:T(8,128)(2,1)S(1)}, bf16[2,128,512]{2,1,0:T(8,128)(2,1)S(1)}, u32[]{:S(2)}, u32[]{:S(2)}) %collective-permute-start.7) | collective-permute-done | bytes 262176 | tf_op jit(solution)/shard_map/ppermute | solution.py:275
  90.0 2.4 %shard_map.94 = (bf16[64,4,8,128]{3,2,1,0:T(8,128)(2,1)S(1)}, bf16[64,4,8,128]{3,2,1,0:T(8,128)(2,1)S(1)}) custom-call(s32[11]{0:T(128)S(1)} %stack.43.place, bf16[8,512,128]{2,1,0:T(8,128)(2,1)S(1)} %get-tuple-element.47.refs_0_, bf16[8,128,512]{2,1,0:T(8,128)(2,1)S(1)} %get-tuple-element.48.refs_1_, ...), custom_call_target="tpu_custom_call", output_to_operand_aliasing={{0}: (6, {}), {1}: (7, {})} | custom-call | flops 536870912 | bytes 4194304 | tf_op jit(solution)/shard_map/pallas_call | solution.py:260
  92.5 1.9 %collective-permute-done.10.got_ref = bf16[64,4,8,128]{3,2,1,0:T(8,128)(2,1)S(1)} collective-permute-done((bf16[64,4,8,128]{3,2,1,0:T(8,128)(2,1)S(1)}, bf16[64,4,8,128]{3,2,1,0:T(8,128)(2,1)S(1)}, u32[]{:S(2)}, u32[]{:S(2)}) %collective-permute-start.10) | collective-permute-done | bytes 524320 | tf_op jit(solution)/shard_map/ppermute | solution.py:343
  94.4 0.3 shard_map.95
  94.7 24.7 %all_to_all.15.back_ref = bf16[64,4,8,128]{3,2,1,0:T(8,128)(2,1)S(1)} all-to-all(bf16[64,4,8,128]{3,2,1,0:T(8,128)(2,1)S(1)} %shard_map.95), channel_id=1, replica_groups=mesh['y'=2,'z'=8,'xh'=2,'xl'=2,'c'=2,'dp'=2] {'xh','xl','y','z'}, dimensions={0} | all-to-all | bytes 1048576 | tf_op jit(solution)/shard_map/all_to_all | solution.py:458
  119.4 0.9 shard_map.96
  (30 shorter events, 0.6 us)
Async XLA Ops:
  0.0 28.6 %copy-start.3 = (bf16[2,128,128]{2,1,0:T(8,128)(2,1)S(1)}, bf16[2,128,128]{2,1,0:T(8,128)(2,1)}, u32[]{:S(2)}) copy-start(bf16[2,128,128]{2,1,0:T(8,128)(2,1)} %wq.1) | copy-start | bytes 196612
  0.0 3.9 %collective-permute-start = (bf16[4,512,128]{2,1,0:T(8,128)(2,1)}, bf16[4,512,128]{2,1,0:T(8,128)(2,1)S(1)}, u32[]{:S(2)}, u32[]{:S(2)}) collective-permute-start(bf16[4,512,128]{2,1,0:T(8,128)(2,1)} %pair_ref.1), channel_id=1, source_target_pairs={{0,2},{2,0},{1,3},{3,1},{4,6},{6,4},{5,7},{7,5},{8,10},{10,8},{9,1... | collective-permute-start | bytes 1572872 | tf_op jit(solution)/shard_map/ppermute | solution.py:343
  0.0 17.5 %collective-permute-start.1 = (bf16[4,512,128]{2,1,0:T(8,128)(2,1)}, bf16[4,512,128]{2,1,0:T(8,128)(2,1)S(1)}, u32[]{:S(2)}, u32[]{:S(2)}) collective-permute-start(bf16[4,512,128]{2,1,0:T(8,128)(2,1)} %pair_ref.1), channel_id=1, source_target_pairs={{0,8},{4,12},{8,0},{12,4},{1,9},{5,13},{9,1},{13,5},{2,10},{6,14},... | collective-permute-start | bytes 1572872 | tf_op jit(solution)/shard_map/ppermute | solution.py:275
  3.9 1.0 copy-start
  4.9 0.7 copy-start.7
  5.6 23.0 %copy-start.4 = (bf16[2,128,128]{2,1,0:T(8,128)(2,1)S(1)}, bf16[2,128,128]{2,1,0:T(8,128)(2,1)}, u32[]{:S(2)}) copy-start(bf16[2,128,128]{2,1,0:T(8,128)(2,1)} %wk.1) | copy-start | bytes 196612
  5.6 23.0 %copy-start.5 = (bf16[2,128,128]{2,1,0:T(8,128)(2,1)S(1)}, bf16[2,128,128]{2,1,0:T(8,128)(2,1)}, u32[]{:S(2)}) copy-start(bf16[2,128,128]{2,1,0:T(8,128)(2,1)} %wv.1) | copy-start | bytes 196612
  5.6 23.0 %copy-start.6 = (bf16[2,128,128]{2,1,0:T(8,128)(2,1)S(1)}, bf16[2,128,128]{2,1,0:T(8,128)(2,1)}, u32[]{:S(2)}) copy-start(bf16[2,128,128]{2,1,0:T(8,128)(2,1)} %wg.1) | copy-start | bytes 196612
  8.2 19.8 %all-to-all-start = ((bf16[16,16,512]{2,1,0:T(8,128)(2,1)}), bf16[16,16,512]{2,1,0:T(8,128)(2,1)S(1)}, u32[]{:S(2)}, u32[]{:S(2)}) async-start(bf16[16,16,512]{2,1,0:T(8,128)(2,1)} %broadcast_in_dim.2), calls=%async_computation | async-start | bytes 524288 | tf_op jit(solution)/shard_map/all_to_all | solution.py:386
  18.2 10.5 %collective-permute-start.2 = (bf16[4,512,128]{2,1,0:T(8,128)(2,1)S(1)}, bf16[4,512,128]{2,1,0:T(8,128)(2,1)S(1)}, u32[]{:S(2)}, u32[]{:S(2)}) collective-permute-start(bf16[4,512,128]{2,1,0:T(8,128)(2,1)S(1)} %shard_map.83.refs_2_), channel_id=1, source_target_pairs={{0,2},{2,0},{1,3},{3,1},{4,6},{6,4},{5,7},{7,5},{8,10},{10,8},{9,1... | collective-permute-start | bytes 1572872 | tf_op jit(solution)/shard_map/ppermute | solution.py:343
  28.0 6.7 %collective-permute-start.3 = (bf16[16,16,512]{2,1,0:T(8,128)(2,1)S(1)}, bf16[16,16,512]{2,1,0:T(8,128)(2,1)S(1)}, u32[]{:S(2)}, u32[]{:S(2)}) collective-permute-start(bf16[16,16,512]{2,1,0:T(8,128)(2,1)S(1)} %all-to-all-done.refs_4_), channel_id=1, source_target_pairs={{0,4},{4,0},{8,12},{12,8},{1,5},{5,1},{9,13},{13,9},{2,6},{6,2},{1... | collective-permute-start | bytes 786440 | tf_op jit(solution)/shard_map/ppermute | solution.py:275
  36.9 2.5 %collective-permute-start.4 = (bf16[8,256,128]{2,1,0:T(8,128)(2,1)S(1)}, bf16[8,256,128]{2,1,0:T(8,128)(2,1)S(1)}, u32[]{:S(2)}, u32[]{:S(2)}) collective-permute-start(bf16[8,256,128]{2,1,0:T(8,128)(2,1)S(1)} %shard_map.88), channel_id=1, source_target_pairs={{0,2},{2,0},{1,3},{3,1},{4,6},{6,4},{5,7},{7,5},{8,10},{10,8},{9,1... | collective-permute-start | bytes 1572872 | tf_op jit(solution)/shard_map/ppermute | solution.py:343
  37.2 2.2 %copy-start.1 = (bf16[4,512,128]{2,1,0:T(8,128)(2,1)S(1)}, bf16[4,512,128]{2,1,0:T(8,128)(2,1)}, u32[]{:S(2)}) copy-start(bf16[4,512,128]{2,1,0:T(8,128)(2,1)} %pair_ref.1) | copy-start | bytes 1572868
  37.2 2.2 %copy-start.2 = (bf16[2,128,128]{2,1,0:T(8,128)(2,1)S(1)}, bf16[2,128,128]{2,1,0:T(8,128)(2,1)}, u32[]{:S(2)}) copy-start(bf16[2,128,128]{2,1,0:T(8,128)(2,1)} %w_ref.3) | copy-start | bytes 196612
  37.2 2.2 %copy-start.8 = (bf16[2,128,4]{1,2,0:T(4,128)(2,1)S(1)}, bf16[2,128,4]{1,2,0:T(4,128)(2,1)}, u32[]{:S(2)}) copy-start(bf16[2,128,4]{1,2,0:T(4,128)(2,1)} %param.14) | copy-start | bytes 6148
  41.9 28.6 %all-to-all-start.1 = ((bf16[32,96,128]{2,1,0:T(8,128)(2,1)}), bf16[32,96,128]{2,1,0:T(8,128)(2,1)S(1)}, u32[]{:S(2)}, u32[]{:S(2)}) async-start(bf16[32,96,128]{2,1,0:T(8,128)(2,1)} %get-tuple-element.40), calls=%async_computation.1 | async-start | bytes 1572864 | tf_op jit(solution)/shard_map/all_to_all | solution.py:428
  47.8 13.4 %collective-permute-start.5 = (bf16[4,256,128]{2,1,0:T(8,128)(2,1)S(1)}, bf16[4,256,128]{2,1,0:T(8,128)(2,1)S(1)}, u32[]{:S(2)}, u32[]{:S(2)}) collective-permute-start(bf16[4,256,128]{2,1,0:T(8,128)(2,1)S(1)} %get-tuple-element.41), channel_id=1, source_target_pairs={{0,8},{4,12},{8,0},{12,4},{1,9},{5,13},{9,1},{13,5},{2,10},{6,14},... | collective-permute-start | bytes 786440 | tf_op jit(solution)/shard_map/ppermute | solution.py:275
  70.4 2.3 %collective-permute-start.6 = (bf16[32,96,128]{2,1,0:T(8,128)(2,1)S(1)}, bf16[32,96,128]{2,1,0:T(8,128)(2,1)S(1)}, u32[]{:S(2)}, u32[]{:S(2)}) collective-permute-start(bf16[32,96,128]{2,1,0:T(8,128)(2,1)S(1)} %all-to-all-done.1.own_in), channel_id=1, source_target_pairs={{0,2},{2,0},{1,3},{3,1},{4,6},{6,4},{5,7},{7,5},{8,10},{10,8},{9,1... | collective-permute-start | bytes 2359304 | tf_op jit(solution)/shard_map/ppermute | solution.py:343
  73.5 10.6 %collective-permute-start.8 = (bf16[2,128,512]{2,1,0:T(8,128)(2,1)S(1)}, bf16[2,128,512]{2,1,0:T(8,128)(2,1)S(1)}, u32[]{:S(2)}, u32[]{:S(2)}) collective-permute-start(bf16[2,128,512]{2,1,0:T(8,128)(2,1)S(1)} %shard_map.91.refs_4_), channel_id=1, source_target_pairs={{0,12},{4,8},{8,4},{12,0},{1,13},{5,9},{9,5},{13,1},{2,14},{6,10},... | collective-permute-start | bytes 786440 | tf_op jit(solution)/shard_map/ppermute | solution.py:275
  74.6 9.5 %collective-permute-start.9 = (bf16[2,128,512]{2,1,0:T(8,128)(2,1)S(1)}, bf16[2,128,512]{2,1,0:T(8,128)(2,1)S(1)}, u32[]{:S(2)}, u32[]{:S(2)}) collective-permute-start(bf16[2,128,512]{2,1,0:T(8,128)(2,1)S(1)} %shard_map.91.refs_4_), channel_id=1, source_target_pairs={{0,4},{4,0},{8,12},{12,8},{1,5},{5,1},{9,13},{13,9},{2,6},{6,2},{1... | collective-permute-start | bytes 786440 | tf_op jit(solution)/shard_map/ppermute | solution.py:275
  75.6 14.4 %collective-permute-start.7 = (bf16[2,128,512]{2,1,0:T(8,128)(2,1)S(1)}, bf16[2,128,512]{2,1,0:T(8,128)(2,1)S(1)}, u32[]{:S(2)}, u32[]{:S(2)}) collective-permute-start(bf16[2,128,512]{2,1,0:T(8,128)(2,1)S(1)} %shard_map.91.refs_4_), channel_id=1, source_target_pairs={{0,8},{4,12},{8,0},{12,4},{1,9},{5,13},{9,1},{13,5},{2,10},{6,14},... | collective-permute-start | bytes 786440 | tf_op jit(solution)/shard_map/ppermute | solution.py:275
  92.4 2.0 %collective-permute-start.10 = (bf16[64,4,8,128]{3,2,1,0:T(8,128)(2,1)S(1)}, bf16[64,4,8,128]{3,2,1,0:T(8,128)(2,1)S(1)}, u32[]{:S(2)}, u32[]{:S(2)}) collective-permute-start(bf16[64,4,8,128]{3,2,1,0:T(8,128)(2,1)S(1)} %get-tuple-element.56), channel_id=1, source_target_pairs={{0,2},{2,0},{1,3},{3,1},{4,6},{6,4},{5,7},{7,5},{8,10},{10,8},{9,1... | collective-permute-start | bytes 1572872 | tf_op jit(solution)/shard_map/ppermute | solution.py:343

commit v7 on v6

--- a/solution.py
+++ b/solution.py
@@ -24,7 +24,7 @@
 X_AXES = ("xh", "xl")
 
 
-def params(mebibytes=12):
+def params(mebibytes=6):
     return pltpu.CompilerParams(vmem_limit_bytes=mebibytes * 1024 * 1024)
 
 
@@ -264,7 +264,7 @@
         scratch_shapes=scratch,
         out_shape=[shape] * len(parts),
         input_output_aliases=aliases,
-        compiler_params=params(16),
+        compiler_params=params(8),
         cost_estimate=cost(
             units * 4 * QUARTER * tokens * channels, 4 << 20, units * QUARTER * tokens
         ),

time: 121 us -> 121 us (level)
  no operation moved by 1% of the time
where the time goes in v7:
time: 121 us; the launch traced here: 120 us
  waiting for transfers between devices  36.1 us (30%)
  Pallas kernels  29.8 us (25%)
  starting transfers between devices  26.2 us (22%)
  blocking collectives  24.7 us (20%)
  local copies, waits for them, and re-layouts  2.57 us (2%)
    all_to_all x1, blocking collectives, shards(): back = lax.all_to_all(branch, X_AXES + ('y', 'z'), 0, 0)  24.7 us
    pallas_call x6, Pallas kernels, attend_some(): pl.pallas_call(functools.partial(attend_quarters, steps, columns, parts),...  17.1 us
    ppermute x6, waiting for transfers between devices, along_x(): return lax.ppermute(array, X_AXES, [(i, i ^ s) for i in range(X)])  13 us
    ppermute x6, starting transfers between devices, along_x(): return lax.ppermute(array, X_AXES, [(i, i ^ s) for i in range(X)])  10.6 us
    all_to_all x1, waiting for transfers between devices, shards(): gathered = lax.all_to_all(copies, ('y', 'z'), 0, 0)  9.7 us
    all_to_all x1, starting transfers between devices, shards(): gathered = lax.all_to_all(copies, ('y', 'z'), 0, 0)  9.29 us
    all_to_all x1, waiting for transfers between devices, shards(): got = lax.all_to_all(sent, ('xl', 'y', 'z'), 0, 0)  9.26 us
    all_to_all x1, starting transfers between devices, shards(): got = lax.all_to_all(sent, ('xl', 'y', 'z'), 0, 0)  5.87 us
  transfers between devices with their start and end apart: 13, of which 6 were waited for; matrix products, arithmetic and copies ran while one was open for 1% of the time, Pallas kernels for 17%

profile of v7, /device:TPU:16, one launch (start us, length us, event | category | flops | bytes accessed | tf_op | source)
XLA Modules:
  0.0 120.3 jit_solution(7444800091586319157)
XLA Ops:
  0.0 3.1 %collective-permute-start.1 = (bf16[4,512,128]{2,1,0:T(8,128)(2,1)}, bf16[4,512,128]{2,1,0:T(8,128)(2,1)S(1)}, u32[]{:S(2)}, u32[]{:S(2)}) collective-permute-start(bf16[4,512,128]{2,1,0:T(8,128)(2,1)} %pair_ref.1), channel_id=1, source_target_pairs={{0,8},{4,12},{8,0},{12,4},{1,9},{5,13},{9,1},{13,5},{2,10},{6,14},... | collective-permute-start | bytes 1572872 | tf_op jit(solution)/shard_map/ppermute | solution.py:275
  3.9 1.0 copy-done
  4.9 0.7 copy-done.7
  5.6 1.9 %shard_map.82 = (bf16[8,512,128]{2,1,0:T(8,128)(2,1)S(1)}, bf16[16,512]{1,0:T(8,128)(2,1)S(1)}) custom-call(s32[11]{0:T(128)S(1)} %stack.43.place, bf16[4,512,128]{2,1,0:T(8,128)(2,1)S(1)} %collective-permute-done.sib_ref, bf16[4,512,128]{2,1,0:T(8,128)(2,1)S(1)} %copy-done, bf16[2,4,128]{2,1,0:T(4,128)(2,1)S(1)} %bitcast.11), custom_call_target="tpu_custom_call" | custom-call | flops 33554432 | bytes 2097152 | tf_op jit(solution)/shard_map/pallas_call | solution.py:376
  7.5 0.7 broadcast_in_dim.2
  8.2 9.3 %all-to-all-start = ((bf16[16,16,512]{2,1,0:T(8,128)(2,1)}), bf16[16,16,512]{2,1,0:T(8,128)(2,1)S(1)}, u32[]{:S(2)}, u32[]{:S(2)}) async-start(bf16[16,16,512]{2,1,0:T(8,128)(2,1)} %broadcast_in_dim.2), calls=%async_computation | async-start | bytes 524288 | tf_op jit(solution)/shard_map/all_to_all | solution.py:386
  17.5 0.7 shard_map.83.refs_2_
  18.3 9.7 %all-to-all-done.refs_4_ = bf16[16,16,512]{2,1,0:T(8,128)(2,1)S(1)} async-done(((bf16[16,16,512]{2,1,0:T(8,128)(2,1)}), bf16[16,16,512]{2,1,0:T(8,128)(2,1)S(1)}, u32[]{:S(2)}, u32[]{:S(2)}) %all-to-all-start) | async-done | bytes 262176 | tf_op jit(solution)/shard_map/all_to_all | solution.py:386
  28.0 0.6 collective-permute-start.3
  28.7 2.4 %shard_map.85 = (bf16[16,256,128]{2,1,0:T(8,128)(2,1)S(1)}, bf16[16,128,512]{2,1,0:T(8,128)(2,1)S(1)}, bf16[16,512,128]{2,1,0:T(8,128)(2,1)S(1)}, f32[16,256,128]{2,1,0:T(8,128)S(1)}) custom-call(s32[11]{0:T(128)S(1)} %stack.43.place, bf16[8,512,128]{2,1,0:T(8,128)(2,1)S(1)} %get-tuple-element.31.refs_0_, ...), custom_call_target="tpu_custom_call" | custom-call | flops 805306368 | bytes 12582912 | tf_op jit(solution)/shard_map/pallas_call | solution.py:403
  31.0 3.7 %shard_map.86 = (bf16[8,256,128]{2,1,0:T(8,128)(2,1)S(1)}, bf16[8,256,128]{2,1,0:T(8,128)(2,1)S(1)}) custom-call(s32[11]{0:T(128)S(1)} %stack.43.place, bf16[16,256,128]{2,1,0:T(8,128)(2,1)S(1)} %get-tuple-element.33.refs_0_, bf16[16,128,512]{2,1,0:T(8,128)(2,1)S(1)} %get-tuple-element.34.refs_1_, bf16[16,512,128]{2,1,0:T(8,128)(2,1)S(1)} %get-tuple-element.35.refs_2_, ...), custom_call_target="tpu_custom_call" | custom-call | flops 1073741824 | bytes 4194304 | tf_op jit(solution)/shard_map/pallas_call | solution.py:260
  34.7 2.2 %shard_map.88 = bf16[8,256,128]{2,1,0:T(8,128)(2,1)S(1)} custom-call(s32[11]{0:T(128)S(1)} %stack.43.place, bf16[16,256,128]{2,1,0:T(8,128)(2,1)S(1)} %get-tuple-element.33.refs_0_, bf16[16,128,512]{2,1,0:T(8,128)(2,1)S(1)} %get-tuple-element.34.refs_1_, bf16[16,512,128]{2,1,0:T(8,128)(2,1)S(1)} %get-tuple-element.35.refs_2_, ...), custom_call_target="tpu_custom_call", output_to_operand_aliasing={{}: (6, {})} | custom-call | flops 536870912 | bytes 4194304 | tf_op jit(solution)/shard_map/pallas_call | solution.py:260
  37.2 2.2 %shard_map.87.own_ref = bf16[8,256,128]{2,1,0:T(8,128)(2,1)S(1)} custom-call(s32[11]{0:T(128)S(1)} %stack.43.place, bf16[16,256,128]{2,1,0:T(8,128)(2,1)S(1)} %get-tuple-element.33.refs_0_, bf16[16,128,512]{2,1,0:T(8,128)(2,1)S(1)} %get-tuple-element.34.refs_1_, bf16[16,512,128]{2,1,0:T(8,128)(2,1)S(1)} %get-tuple-element.35.refs_2_, ...), custom_call_target="tpu_custom_call", output_to_operand_aliasing={{}: (6, {})} | custom-call | flops 536870912 | bytes 4194304 | tf_op jit(solution)/shard_map/pallas_call | solution.py:260
  39.5 2.4 %shard_map.89 = (bf16[4,256,128]{2,1,0:T(8,128)(2,1)S(1)}, bf16[4,256,128]{2,1,0:T(8,128)(2,1)S(1)}, bf16[32,96,128]{2,1,0:T(8,128)(2,1)}) custom-call(s32[11]{0:T(128)S(1)} %stack.43.place, bf16[8,256,128]{2,1,0:T(8,128)(2,1)S(1)} %shard_map.87.own_ref, bf16[8,256,128]{2,1,0:T(8,128)(2,1)S(1)} %collective-permute-done.4.got_ref, ...), custom_call_target="tpu_custom_call" | custom-call | flops 134217728 | bytes 3145728 | tf_op jit(solution)/shard_map/pallas_call | solution.py:415
  41.9 5.9 %all-to-all-start.1 = ((bf16[32,96,128]{2,1,0:T(8,128)(2,1)}), bf16[32,96,128]{2,1,0:T(8,128)(2,1)S(1)}, u32[]{:S(2)}, u32[]{:S(2)}) async-start(bf16[32,96,128]{2,1,0:T(8,128)(2,1)} %get-tuple-element.40), calls=%async_computation.1 | async-start | bytes 1572864 | tf_op jit(solution)/shard_map/all_to_all | solution.py:428
  47.8 2.1 %collective-permute-start.5 = (bf16[4,256,128]{2,1,0:T(8,128)(2,1)S(1)}, bf16[4,256,128]{2,1,0:T(8,128)(2,1)S(1)}, u32[]{:S(2)}, u32[]{:S(2)}) collective-permute-start(bf16[4,256,128]{2,1,0:T(8,128)(2,1)S(1)} %get-tuple-element.41), channel_id=1, source_target_pairs={{0,8},{4,12},{8,0},{12,4},{1,9},{5,13},{9,1},{13,5},{2,10},{6,14},... | collective-permute-start | bytes 786440 | tf_op jit(solution)/shard_map/ppermute | solution.py:275
  49.9 11.3 %collective-permute-done.5.got_ref = bf16[4,256,128]{2,1,0:T(8,128)(2,1)S(1)} collective-permute-done((bf16[4,256,128]{2,1,0:T(8,128)(2,1)S(1)}, bf16[4,256,128]{2,1,0:T(8,128)(2,1)S(1)}, u32[]{:S(2)}, u32[]{:S(2)}) %collective-permute-start.5) | collective-permute-done | bytes 262176 | tf_op jit(solution)/shard_map/ppermute | solution.py:275
  61.2 9.3 %all-to-all-done.1.own_in = bf16[32,96,128]{2,1,0:T(8,128)(2,1)S(1)} async-done(((bf16[32,96,128]{2,1,0:T(8,128)(2,1)}), bf16[32,96,128]{2,1,0:T(8,128)(2,1)S(1)}, u32[]{:S(2)}, u32[]{:S(2)}) %all-to-all-start.1) | async-done | bytes 786464 | tf_op jit(solution)/shard_map/all_to_all | solution.py:428
  70.4 2.3 %collective-permute-done.6.sib_in = bf16[32,96,128]{2,1,0:T(8,128)(2,1)S(1)} collective-permute-done((bf16[32,96,128]{2,1,0:T(8,128)(2,1)S(1)}, bf16[32,96,128]{2,1,0:T(8,128)(2,1)S(1)}, u32[]{:S(2)}, u32[]{:S(2)}) %collective-permute-start.6) | collective-permute-done | bytes 786464 | tf_op jit(solution)/shard_map/ppermute | solution.py:343
  72.7 0.8 shard_map.91.refs_4_
  73.5 1.1 collective-permute-start.8
  74.6 0.9 collective-permute-start.9
  75.6 2.8 %collective-permute-start.7 = (bf16[2,128,512]{2,1,0:T(8,128)(2,1)S(1)}, bf16[2,128,512]{2,1,0:T(8,128)(2,1)S(1)}, u32[]{:S(2)}, u32[]{:S(2)}) collective-permute-start(bf16[2,128,512]{2,1,0:T(8,128)(2,1)S(1)} %shard_map.91.refs_4_), channel_id=1, source_target_pairs={{0,8},{4,12},{8,0},{12,4},{1,9},{5,13},{9,1},{13,5},{2,10},{6,14},... | collective-permute-start | bytes 786440 | tf_op jit(solution)/shard_map/ppermute | solution.py:275
  78.3 3.3 %shard_map.90 = (bf16[8,512,128]{2,1,0:T(8,128)(2,1)S(1)}, bf16[8,128,512]{2,1,0:T(8,128)(2,1)S(1)}, bf16[8,512,128]{2,1,0:T(8,128)(2,1)S(1)}, f32[8,512,128]{2,1,0:T(8,128)S(1)}, bf16[4,512,128]{2,1,0:T(8,128)(2,1)S(1)}) custom-call(s32[11]{0:T(128)S(1)} %stack.43.place, bf16[32,96,128]{2,1,0:T(8,128)(2,1)S(1)} %all-to-all-done.1.own_in, ...), custom_call_target="tpu_custom_call" | custom-call | flops 536870912 | bytes 6291456 | tf_op jit(solution)/shard_map/pallas_call | solution.py:441
  81.7 2.4 %shard_map.92 = (bf16[64,4,8,128]{3,2,1,0:T(8,128)(2,1)S(1)}, bf16[64,4,8,128]{3,2,1,0:T(8,128)(2,1)S(1)}) custom-call(s32[11]{0:T(128)S(1)} %stack.43.place, bf16[8,512,128]{2,1,0:T(8,128)(2,1)S(1)} %get-tuple-element.47.refs_0_, bf16[8,128,512]{2,1,0:T(8,128)(2,1)S(1)} %get-tuple-element.48.refs_1_, bf16[8,512,128]{2,1,0:T(8,128)(2,1)S(1)} %get-tuple-element.49.refs_2_, ...), custom_call_target="tpu_custom_call" | custom-call | flops 536870912 | bytes 4194304 | tf_op jit(solution)/shard_map/pallas_call | solution.py:260
  84.1 4.2 %shard_map.93 = (bf16[64,4,8,128]{3,2,1,0:T(8,128)(2,1)S(1)}, bf16[64,4,8,128]{3,2,1,0:T(8,128)(2,1)S(1)}) custom-call(s32[11]{0:T(128)S(1)} %stack.43.place, bf16[8,512,128]{2,1,0:T(8,128)(2,1)S(1)} %get-tuple-element.47.refs_0_, bf16[8,128,512]{2,1,0:T(8,128)(2,1)S(1)} %get-tuple-element.48.refs_1_, ...), custom_call_target="tpu_custom_call", output_to_operand_aliasing={{0}: (7, {}), {1}: (8, {})} | custom-call | flops 1073741824 | bytes 4194304 | tf_op jit(solution)/shard_map/pallas_call | solution.py:260
  88.3 1.6 %collective-permute-done.7.refs_4_ = bf16[2,128,512]{2,1,0:T(8,128)(2,1)S(1)} collective-permute-done((bf16[2,128,512]{2,1,0:T(8,128)(2,1)S(1)}, bf16[2,128,512]{2,1,0:T(8,128)(2,1)S(1)}, u32[]{:S(2)}, u32[]{:S(2)}) %collective-permute-start.7) | collective-permute-done | bytes 262176 | tf_op jit(solution)/shard_map/ppermute | solution.py:275
  90.0 2.4 %shard_map.94 = (bf16[64,4,8,128]{3,2,1,0:T(8,128)(2,1)S(1)}, bf16[64,4,8,128]{3,2,1,0:T(8,128)(2,1)S(1)}) custom-call(s32[11]{0:T(128)S(1)} %stack.43.place, bf16[8,512,128]{2,1,0:T(8,128)(2,1)S(1)} %get-tuple-element.47.refs_0_, bf16[8,128,512]{2,1,0:T(8,128)(2,1)S(1)} %get-tuple-element.48.refs_1_, ...), custom_call_target="tpu_custom_call", output_to_operand_aliasing={{0}: (6, {}), {1}: (7, {})} | custom-call | flops 536870912 | bytes 4194304 | tf_op jit(solution)/shard_map/pallas_call | solution.py:260
  92.5 1.9 %collective-permute-done.10.got_ref = bf16[64,4,8,128]{3,2,1,0:T(8,128)(2,1)S(1)} collective-permute-done((bf16[64,4,8,128]{3,2,1,0:T(8,128)(2,1)S(1)}, bf16[64,4,8,128]{3,2,1,0:T(8,128)(2,1)S(1)}, u32[]{:S(2)}, u32[]{:S(2)}) %collective-permute-start.10) | collective-permute-done | bytes 524320 | tf_op jit(solution)/shard_map/ppermute | solution.py:343
  94.4 0.3 shard_map.95
  94.7 24.7 %all_to_all.15.back_ref = bf16[64,4,8,128]{3,2,1,0:T(8,128)(2,1)S(1)} all-to-all(bf16[64,4,8,128]{3,2,1,0:T(8,128)(2,1)S(1)} %shard_map.95), channel_id=1, replica_groups=mesh['y'=2,'z'=8,'xh'=2,'xl'=2,'c'=2,'dp'=2] {'xh','xl','y','z'}, dimensions={0} | all-to-all | bytes 1048576 | tf_op jit(solution)/shard_map/all_to_all | solution.py:458
  119.4 0.9 shard_map.96
  (30 shorter events, 0.6 us)
Async XLA Ops:
  0.0 28.6 %copy-start.3 = (bf16[2,128,128]{2,1,0:T(8,128)(2,1)S(1)}, bf16[2,128,128]{2,1,0:T(8,128)(2,1)}, u32[]{:S(2)}) copy-start(bf16[2,128,128]{2,1,0:T(8,128)(2,1)} %wq.1) | copy-start | bytes 196612
  0.0 3.9 %collective-permute-start = (bf16[4,512,128]{2,1,0:T(8,128)(2,1)}, bf16[4,512,128]{2,1,0:T(8,128)(2,1)S(1)}, u32[]{:S(2)}, u32[]{:S(2)}) collective-permute-start(bf16[4,512,128]{2,1,0:T(8,128)(2,1)} %pair_ref.1), channel_id=1, source_target_pairs={{0,2},{2,0},{1,3},{3,1},{4,6},{6,4},{5,7},{7,5},{8,10},{10,8},{9,1... | collective-permute-start | bytes 1572872 | tf_op jit(solution)/shard_map/ppermute | solution.py:343
  0.0 17.5 %collective-permute-start.1 = (bf16[4,512,128]{2,1,0:T(8,128)(2,1)}, bf16[4,512,128]{2,1,0:T(8,128)(2,1)S(1)}, u32[]{:S(2)}, u32[]{:S(2)}) collective-permute-start(bf16[4,512,128]{2,1,0:T(8,128)(2,1)} %pair_ref.1), channel_id=1, source_target_pairs={{0,8},{4,12},{8,0},{12,4},{1,9},{5,13},{9,1},{13,5},{2,10},{6,14},... | collective-permute-start | bytes 1572872 | tf_op jit(solution)/shard_map/ppermute | solution.py:275
  3.9 1.0 copy-start
  4.9 0.7 copy-start.7
  5.6 23.0 %copy-start.4 = (bf16[2,128,128]{2,1,0:T(8,128)(2,1)S(1)}, bf16[2,128,128]{2,1,0:T(8,128)(2,1)}, u32[]{:S(2)}) copy-start(bf16[2,128,128]{2,1,0:T(8,128)(2,1)} %wk.1) | copy-start | bytes 196612
  5.6 23.0 %copy-start.5 = (bf16[2,128,128]{2,1,0:T(8,128)(2,1)S(1)}, bf16[2,128,128]{2,1,0:T(8,128)(2,1)}, u32[]{:S(2)}) copy-start(bf16[2,128,128]{2,1,0:T(8,128)(2,1)} %wv.1) | copy-start | bytes 196612
  5.6 23.0 %copy-start.6 = (bf16[2,128,128]{2,1,0:T(8,128)(2,1)S(1)}, bf16[2,128,128]{2,1,0:T(8,128)(2,1)}, u32[]{:S(2)}) copy-start(bf16[2,128,128]{2,1,0:T(8,128)(2,1)} %wg.1) | copy-start | bytes 196612
  8.2 19.8 %all-to-all-start = ((bf16[16,16,512]{2,1,0:T(8,128)(2,1)}), bf16[16,16,512]{2,1,0:T(8,128)(2,1)S(1)}, u32[]{:S(2)}, u32[]{:S(2)}) async-start(bf16[16,16,512]{2,1,0:T(8,128)(2,1)} %broadcast_in_dim.2), calls=%async_computation | async-start | bytes 524288 | tf_op jit(solution)/shard_map/all_to_all | solution.py:386
  18.2 10.5 %collective-permute-start.2 = (bf16[4,512,128]{2,1,0:T(8,128)(2,1)S(1)}, bf16[4,512,128]{2,1,0:T(8,128)(2,1)S(1)}, u32[]{:S(2)}, u32[]{:S(2)}) collective-permute-start(bf16[4,512,128]{2,1,0:T(8,128)(2,1)S(1)} %shard_map.83.refs_2_), channel_id=1, source_target_pairs={{0,2},{2,0},{1,3},{3,1},{4,6},{6,4},{5,7},{7,5},{8,10},{10,8},{9,1... | collective-permute-start | bytes 1572872 | tf_op jit(solution)/shard_map/ppermute | solution.py:343
  28.0 6.7 %collective-permute-start.3 = (bf16[16,16,512]{2,1,0:T(8,128)(2,1)S(1)}, bf16[16,16,512]{2,1,0:T(8,128)(2,1)S(1)}, u32[]{:S(2)}, u32[]{:S(2)}) collective-permute-start(bf16[16,16,512]{2,1,0:T(8,128)(2,1)S(1)} %all-to-all-done.refs_4_), channel_id=1, source_target_pairs={{0,4},{4,0},{8,12},{12,8},{1,5},{5,1},{9,13},{13,9},{2,6},{6,2},{1... | collective-permute-start | bytes 786440 | tf_op jit(solution)/shard_map/ppermute | solution.py:275
  36.9 2.5 %collective-permute-start.4 = (bf16[8,256,128]{2,1,0:T(8,128)(2,1)S(1)}, bf16[8,256,128]{2,1,0:T(8,128)(2,1)S(1)}, u32[]{:S(2)}, u32[]{:S(2)}) collective-permute-start(bf16[8,256,128]{2,1,0:T(8,128)(2,1)S(1)} %shard_map.88), channel_id=1, source_target_pairs={{0,2},{2,0},{1,3},{3,1},{4,6},{6,4},{5,7},{7,5},{8,10},{10,8},{9,1... | collective-permute-start | bytes 1572872 | tf_op jit(solution)/shard_map/ppermute | solution.py:343
  37.2 2.2 %copy-start.1 = (bf16[4,512,128]{2,1,0:T(8,128)(2,1)S(1)}, bf16[4,512,128]{2,1,0:T(8,128)(2,1)}, u32[]{:S(2)}) copy-start(bf16[4,512,128]{2,1,0:T(8,128)(2,1)} %pair_ref.1) | copy-start | bytes 1572868
  37.2 2.2 %copy-start.2 = (bf16[2,128,128]{2,1,0:T(8,128)(2,1)S(1)}, bf16[2,128,128]{2,1,0:T(8,128)(2,1)}, u32[]{:S(2)}) copy-start(bf16[2,128,128]{2,1,0:T(8,128)(2,1)} %w_ref.3) | copy-start | bytes 196612
  37.2 2.2 %copy-start.8 = (bf16[2,128,4]{1,2,0:T(4,128)(2,1)S(1)}, bf16[2,128,4]{1,2,0:T(4,128)(2,1)}, u32[]{:S(2)}) copy-start(bf16[2,128,4]{1,2,0:T(4,128)(2,1)} %param.14) | copy-start | bytes 6148
  41.9 28.6 %all-to-all-start.1 = ((bf16[32,96,128]{2,1,0:T(8,128)(2,1)}), bf16[32,96,128]{2,1,0:T(8,128)(2,1)S(1)}, u32[]{:S(2)}, u32[]{:S(2)}) async-start(bf16[32,96,128]{2,1,0:T(8,128)(2,1)} %get-tuple-element.40), calls=%async_computation.1 | async-start | bytes 1572864 | tf_op jit(solution)/shard_map/all_to_all | solution.py:428
  47.8 13.4 %collective-permute-start.5 = (bf16[4,256,128]{2,1,0:T(8,128)(2,1)S(1)}, bf16[4,256,128]{2,1,0:T(8,128)(2,1)S(1)}, u32[]{:S(2)}, u32[]{:S(2)}) collective-permute-start(bf16[4,256,128]{2,1,0:T(8,128)(2,1)S(1)} %get-tuple-element.41), channel_id=1, source_target_pairs={{0,8},{4,12},{8,0},{12,4},{1,9},{5,13},{9,1},{13,5},{2,10},{6,14},... | collective-permute-start | bytes 786440 | tf_op jit(solution)/shard_map/ppermute | solution.py:275
  70.4 2.3 %collective-permute-start.6 = (bf16[32,96,128]{2,1,0:T(8,128)(2,1)S(1)}, bf16[32,96,128]{2,1,0:T(8,128)(2,1)S(1)}, u32[]{:S(2)}, u32[]{:S(2)}) collective-permute-start(bf16[32,96,128]{2,1,0:T(8,128)(2,1)S(1)} %all-to-all-done.1.own_in), channel_id=1, source_target_pairs={{0,2},{2,0},{1,3},{3,1},{4,6},{6,4},{5,7},{7,5},{8,10},{10,8},{9,1... | collective-permute-start | bytes 2359304 | tf_op jit(solution)/shard_map/ppermute | solution.py:343
  73.5 10.6 %collective-permute-start.8 = (bf16[2,128,512]{2,1,0:T(8,128)(2,1)S(1)}, bf16[2,128,512]{2,1,0:T(8,128)(2,1)S(1)}, u32[]{:S(2)}, u32[]{:S(2)}) collective-permute-start(bf16[2,128,512]{2,1,0:T(8,128)(2,1)S(1)} %shard_map.91.refs_4_), channel_id=1, source_target_pairs={{0,12},{4,8},{8,4},{12,0},{1,13},{5,9},{9,5},{13,1},{2,14},{6,10},... | collective-permute-start | bytes 786440 | tf_op jit(solution)/shard_map/ppermute | solution.py:275
  74.6 9.5 %collective-permute-start.9 = (bf16[2,128,512]{2,1,0:T(8,128)(2,1)S(1)}, bf16[2,128,512]{2,1,0:T(8,128)(2,1)S(1)}, u32[]{:S(2)}, u32[]{:S(2)}) collective-permute-start(bf16[2,128,512]{2,1,0:T(8,128)(2,1)S(1)} %shard_map.91.refs_4_), channel_id=1, source_target_pairs={{0,4},{4,0},{8,12},{12,8},{1,5},{5,1},{9,13},{13,9},{2,6},{6,2},{1... | collective-permute-start | bytes 786440 | tf_op jit(solution)/shard_map/ppermute | solution.py:275
  75.6 14.4 %collective-permute-start.7 = (bf16[2,128,512]{2,1,0:T(8,128)(2,1)S(1)}, bf16[2,128,512]{2,1,0:T(8,128)(2,1)S(1)}, u32[]{:S(2)}, u32[]{:S(2)}) collective-permute-start(bf16[2,128,512]{2,1,0:T(8,128)(2,1)S(1)} %shard_map.91.refs_4_), channel_id=1, source_target_pairs={{0,8},{4,12},{8,0},{12,4},{1,9},{5,13},{9,1},{13,5},{2,10},{6,14},... | collective-permute-start | bytes 786440 | tf_op jit(solution)/shard_map/ppermute | solution.py:275
  92.4 2.0 %collective-permute-start.10 = (bf16[64,4,8,128]{3,2,1,0:T(8,128)(2,1)S(1)}, bf16[64,4,8,128]{3,2,1,0:T(8,128)(2,1)S(1)}, u32[]{:S(2)}, u32[]{:S(2)}) collective-permute-start(bf16[64,4,8,128]{3,2,1,0:T(8,128)(2,1)S(1)} %get-tuple-element.56), channel_id=1, source_target_pairs={{0,2},{2,0},{1,3},{3,1},{4,6},{6,4},{5,7},{7,5},{8,10},{10,8},{9,1... | collective-permute-start | bytes 1572872 | tf_op jit(solution)/shard_map/ppermute | solution.py:343
